TPU v7x, 512 devices: a whole 4x4x16 slice. The times are simulated.
512 devices in a mesh: role: 2 (over core), inst: 16 (over z_lo, y), tp: 16 (over z_hi, x).
Axes of the slice: x: 4, y: 4, z: 16 (z_hi: 4, z_lo: 4; z = z_hi * 4 + z_lo), core: 2. Of those that a mesh axis runs over, the one named last changes fastest.
Arguments:
- hidden: bfloat16 [2, 16, 256, 8192], P('role', 'inst', None, 'tp'), may hold values from -6 to 6
- queries: bfloat16 [2, 16, 256, 16384], P('role', 'inst', None, 'tp'), may hold values from -120 to 120
- prefix_cache: bfloat16 [2, 16, 16, 2, 2048, 128], P('role', 'inst', 'tp'), may hold values from -4 to 4
- lengths: int32 [2, 16], P('role', 'inst'), may hold values from 1 to 32, as said below
- pairing: int32 [16], replicated, may hold values from 0 to 15, as said below
- w_kv: bfloat16 [8192, 2048], P('tp'), may hold values from -0.0625 to 0.0625
Outputs:
- attended: bfloat16 [2, 16, 256, 16384], P('role', 'inst', None, 'tp')
- layer_kv: bfloat16 [2, 16, 256, 2048], P('role', 'inst', None, 'tp')
Inputs may be any that keep to these rules, and one draw needn't show every extreme that they name: `lengths`: every request has at least one cached block; some request holds all 32 blocks. `pairing`: each decode instance takes over exactly one prefill instance; for some decode instance j, it is prefill instance (j + 8) mod 16.
All inputs are finite; a program needn't handle non-finite values.
Results may differ from a plain program's by a relative error of at most 0.0052.
Values may be sent and summed in bfloat16 or wider, within the bound.
No kernel may reach another device: no remote copies, remote signals or barrier semaphores. Data moves between devices by JAX's collectives and lax.ppermute only.
A program may use at most 64 MiB of HBM per device.

v0:
```python
import math

import jax
import jax.numpy as jnp
from jax import lax
from jax.sharding import PartitionSpec as P

BLOCK = 128


def from_partner(array, axis, bit):
    return lax.ppermute(array, axis, [(i, i ^ 1 << bit) for i in range(lax.axis_size(axis))])


def shifted(array, axis, by):
    length = lax.axis_size(axis)
    pairs = [(i, i + by) for i in range(length) if 0 <= i + by < length]
    return lax.ppermute(array, axis, pairs)


def rotate(key_rows, positions):
    half_dim = key_rows.shape[-1] // 2
    steps_range = jnp.arange(half_dim).astype(jnp.float32)
    frequency = jnp.exp(steps_range * (-2.0 * math.log(500000.0) / key_rows.shape[-1]))
    angles = positions[:, None] * frequency[None, :]
    cosine = jnp.cos(angles)
    sine_term = jnp.sin(angles)
    front_half = key_rows[..., :half_dim]
    back_half = key_rows[..., half_dim:]
    return jnp.concatenate(
        [front_half * cosine - back_half * sine_term, back_half * cosine + front_half * sine_term],
        axis=-1,
    )


def attend(queried, keys_all, values_all, limit_rows, new_len):
    prefix_len = keys_all.shape[0] - new_len
    scores = lax.dot_general(
        queried, keys_all, (((1,), (1,)), ((), ())), preferred_element_type=jnp.float32
    )
    scores = scores * queried.shape[-1] ** (-0.5)
    key_pos = jnp.arange(keys_all.shape[0])[None, :]
    row_pos = (jnp.arange(queried.shape[0]) % new_len)[:, None]
    allowed = (key_pos < limit_rows) | (key_pos >= prefix_len) & (key_pos - prefix_len <= row_pos)
    masked = jnp.where(allowed, scores, -jnp.inf)
    row_max = jnp.max(masked, axis=1, keepdims=True)
    weights = jnp.exp(masked - row_max)
    weight_sum = jnp.sum(weights, axis=1, keepdims=True)
    product = jnp.dot(weights.astype(jnp.bfloat16), values_all, preferred_element_type=jnp.float32)
    return (product / weight_sum).astype(jnp.bfloat16)


def per_device(hidden, queries, prefix_cache, lengths, pairing, w_kv):
    new_len = hidden.shape[2]
    head_dim = prefix_cache.shape[-1]
    member = lax.axis_index("tp")
    is_lower = member % 2 == 0
    length = lengths[0, 0]
    positions = (length * BLOCK + jnp.arange(new_len)).astype(jnp.float32)
    partial_kv = jnp.dot(hidden[0, 0], w_kv, preferred_element_type=jnp.float32)
    summed = lax.psum(partial_kv, "tp")
    pair_cols = lax.dynamic_slice_in_dim(summed, member // 2 * 2 * head_dim, 2 * head_dim, 1)
    keys_new = rotate(pair_cols[:, :head_dim], positions).astype(jnp.bfloat16)
    values_new = pair_cols[:, head_dim:].astype(jnp.bfloat16)
    own_kv = jnp.where(is_lower, keys_new, values_new)
    resident = prefix_cache[0, 0, 0]
    across = from_partner(resident, "tp", 0)
    front_rows = jnp.where(is_lower, resident, across)
    back_rows = jnp.where(is_lower, across, resident)
    keys_all = jnp.concatenate([front_rows[0], back_rows[0], keys_new], axis=0)
    values_all = jnp.concatenate([front_rows[1], back_rows[1], values_new], axis=0)
    heads_dev = queries.shape[-1] // head_dim
    per_group = math.gcd(heads_dev, max(1, 512 // new_len))
    grouped = queries[0, 0].reshape(new_len, heads_dev, head_dim).transpose(1, 0, 2)
    grouped = grouped.reshape(heads_dev // per_group, per_group * new_len, head_dim)
    limit_rows = length * BLOCK
    results = lax.map(
        lambda queried: attend(queried, keys_all, values_all, limit_rows, new_len), grouped
    )
    attended = (
        results.reshape(heads_dev, new_len, head_dim)
        .transpose(1, 0, 2)
        .reshape(1, 1, new_len, heads_dev * head_dim)
    )
    role_index = lax.axis_index("role")
    inst_index = lax.axis_index("inst")
    count_inst = pairing.shape[0]
    source = jnp.sum(jnp.where(pairing == inst_index, jnp.arange(count_inst, dtype=jnp.int32), 0))
    collected = lax.all_gather(own_kv[None], "inst", axis=0, tiled=True)
    picked = lax.dynamic_index_in_dim(collected, source, 0, keepdims=False)
    handed = shifted(picked, "role", 1)
    layer_kv = jnp.where(role_index == 1, handed, own_kv)[None, None]
    return (attended, layer_kv)


def solution(mesh):
    in_specs = (
        P("role", "inst", None, "tp"),
        P("role", "inst", None, "tp"),
        P("role", "inst", "tp", None, None, None),
        P("role", "inst"),
        P(),
        P("tp", None),
    )
    out_specs = (P("role", "inst", None, "tp"), P("role", "inst", None, "tp"))
    return jax.shard_map(
        per_device, mesh=mesh, in_specs=in_specs, out_specs=out_specs, check_vma=False
    )
```

profile of v0, /device:TPU:20, one launch (start us, length us, event | category | flops | bytes accessed | tf_op | source)
XLA Modules:
  0.0 393.3 jit_solution(11930086683064135384)
XLA Ops:
  7.2 1.5 copy-done
  8.8 3.2 fusion.23
  12.0 3.1 collective-permute-start
  15.9 1.1 copy.19
  17.0 0.9 copy.10
  17.9 0.6 fusion.33
  20.5 250.1 %all-reduce.2.cloned.1.call-done = f32[256,2048]{0,1:T(8,128)} async-done(((f32[256,2048]{0,1:T(8,128)}), f32[256,2048]{0,1:T(8,128)}) %all-reduce.2.cloned.1.call-update) | async-done | bytes 2097168 | tf_op jit(solution)/shard_map/psum | solution.py:61
  270.6 1.2 fusion.30
  271.8 1.6 broadcast_select_fusion.2
  273.4 1.4 broadcast_select_fusion.1
  274.8 1.4 slice_bitcast_fusion
  276.4 1.4 pad_maximum_fusion.1
  277.9 1.1 pad_maximum_fusion
  279.0 71.2 %all-gather.3.cloned.1.call-done = bf16[4096,128]{0,1:T(8,128)(2,1)} async-done(((bf16[256,128]{0,1:T(8,128)(2,1)}), bf16[4096,128]{0,1:T(8,128)(2,1)}) %all-gather.3.cloned.1.call-update) | async-done | bytes 1048592 | tf_op jit(solution)/shard_map/all_gather | solution.py:89
  350.2 1.5 copy.20
  351.8 1.3 collective-permute-start.1
  353.1 30.1 %while.12 = (s32[]{:T(128)}, bf16[4,512,128]{2,1,0:T(8,128)(2,1)}, s32[]{:T(128)}, bf16[4,512,128]{2,1,0:T(8,128)(2,1)}, bf16[4352,128]{1,0:T(8,128)(2,1)}, /*index=5*/bf16[4352,128]{1,0:T(8,128)(2,1)S(1)}, s32[]{:T(128)}) while((s32[]{:T(128)}, bf16[4,512,128]{2,1,0:T(8,128)(2,1)}, s32[]{:T(128)}, bf16[4,512,128]{2,1,0:T(8,128)(2,1)}, ...), condition=%wide.region_4.5_spmd, body=%wide.region_1.4_spmd.sunk | while | flops 1163279104 | bytes 29296720 | solution.py:77
  353.2 4.0 %fusion.47 = (f32[512]{0:T(512)S(1)}, f32[512,4352]{1,0:T(8,128)S(1)}) fusion(bf16[4352,128]{1,0:T(8,128)(2,1)} %get-tuple-element.176, bf16[4,512,128]{2,1,0:T(8,128)(2,1)} %get-tuple-element.175, s32[]{:T(128)} %get-tuple-element.165, s32[512]{0:T(512)S(1)} %add_select_fusion.2, s32[4352]{0:T(1024)S(1)} %iota_add_fusion.2, ...), kind=kOutput, calls=%fused_computation.52.clone.1 | convolution fusion | flops 583794176 | bytes 10188800 | tf_op jit(solution)/shard_map/while/body/eval_jaxpr/dot_general | solution.py:38
  357.2 1.4 fusion.48
  358.6 2.1 fusion.49
  360.7 4.0 %fusion.47 = (f32[512]{0:T(512)S(1)}, f32[512,4352]{1,0:T(8,128)S(1)}) fusion(bf16[4352,128]{1,0:T(8,128)(2,1)} %get-tuple-element.176, bf16[4,512,128]{2,1,0:T(8,128)(2,1)} %get-tuple-element.175, s32[]{:T(128)} %get-tuple-element.165, s32[512]{0:T(512)S(1)} %add_select_fusion.2, s32[4352]{0:T(1024)S(1)} %iota_add_fusion.2, ...), kind=kOutput, calls=%fused_computation.52.clone.1 | convolution fusion | flops 583794176 | bytes 10188800 | tf_op jit(solution)/shard_map/while/body/eval_jaxpr/dot_general | solution.py:38
  364.8 1.4 fusion.48
  366.1 2.1 fusion.49
  368.2 4.0 %fusion.47 = (f32[512]{0:T(512)S(1)}, f32[512,4352]{1,0:T(8,128)S(1)}) fusion(bf16[4352,128]{1,0:T(8,128)(2,1)} %get-tuple-element.176, bf16[4,512,128]{2,1,0:T(8,128)(2,1)} %get-tuple-element.175, s32[]{:T(128)} %get-tuple-element.165, s32[512]{0:T(512)S(1)} %add_select_fusion.2, s32[4352]{0:T(1024)S(1)} %iota_add_fusion.2, ...), kind=kOutput, calls=%fused_computation.52.clone.1 | convolution fusion | flops 583794176 | bytes 10188800 | tf_op jit(solution)/shard_map/while/body/eval_jaxpr/dot_general | solution.py:38
  372.3 1.4 fusion.48
  373.6 2.1 fusion.49
  375.8 4.0 %fusion.47 = (f32[512]{0:T(512)S(1)}, f32[512,4352]{1,0:T(8,128)S(1)}) fusion(bf16[4352,128]{1,0:T(8,128)(2,1)} %get-tuple-element.176, bf16[4,512,128]{2,1,0:T(8,128)(2,1)} %get-tuple-element.175, s32[]{:T(128)} %get-tuple-element.165, s32[512]{0:T(512)S(1)} %add_select_fusion.2, s32[4352]{0:T(1024)S(1)} %iota_add_fusion.2, ...), kind=kOutput, calls=%fused_computation.52.clone.1 | convolution fusion | flops 583794176 | bytes 10188800 | tf_op jit(solution)/shard_map/while/body/eval_jaxpr/dot_general | solution.py:38
  379.8 1.4 fusion.48
  381.2 2.1 fusion.49
  383.3 1.4 copy.23
  384.7 1.0 reshape.54
  385.7 0.7 copy.16
  (37 shorter events, 0.7 us)
Async XLA Ops:
  7.2 1.6 copy-start
  7.2 4.9 %copy-start.3 = (bf16[1,1,1,2,2048,128]{5,4,3,2,1,0:T(8,128)(2,1)S(1)}, bf16[1,1,1,2,2048,128]{5,4,3,2,1,0:T(8,128)(2,1)}, u32[]{:S(2)}) copy-start(bf16[1,1,1,2,2048,128]{5,4,3,2,1,0:T(8,128)(2,1)} %param.10) | copy-start | bytes 3145732
  7.2 263.4 %all-reduce.2.cloned.1.call-start = ((), (), s32[]{:S(2)}) async-start(), calls=%async_computation | async-start | bytes 4194304 | tf_op jit(solution)/shard_map/psum | solution.py:61
  12.0 6.0 %copy-start.5 = (s32[16]{0:T(128)S(1)}, s32[16]{0:T(128)}, u32[]{:S(2)}) copy-start(s32[16]{0:T(128)} %param.12) | copy-start | bytes 196
  12.0 338.2 %all-gather.3.cloned.1.call-start = ((), (), s32[]{:S(2)}) async-start(), calls=%async_computation.1 | async-start | bytes 1114112 | tf_op jit(solution)/shard_map/all_gather | solution.py:89
  12.0 261.4 %collective-permute-start = (bf16[2,2048,128]{2,1,0:T(8,128)(2,1)S(1)}, bf16[2,2048,128]{2,1,0:T(8,128)(2,1)}, u32[]{:S(2)}, u32[]{:S(2)}) collective-permute-start(bf16[2,2048,128]{2,1,0:T(8,128)(2,1)S(1)} %bitcast.58), channel_id=1, source_target_pairs={{0,1},{1,0},{2,3},{3,2},{4,5},{5,4},{6,7},{7,6},{8,9},{9,8},{10,11... | collective-permute-start | bytes 3145736 | tf_op jit(solution)/shard_map/ppermute | solution.py:12
  276.4 1.4 copy-start.1
  276.4 1.5 copy-start.2
  351.8 33.9 %collective-permute-start.1 = (bf16[256,128]{0,1:T(8,128)(2,1)S(1)}, bf16[256,128]{0,1:T(8,128)(2,1)S(1)}, u32[]{:S(2)}, u32[]{:S(2)}) collective-permute-start(bf16[256,128]{0,1:T(8,128)(2,1)S(1)} %bitcast.62), channel_id=1, source_target_pairs={{0,256},{1,257},{2,258},{3,259},{4,260},{5,261},{6,262},{7,263},{8... | collective-permute-start | bytes 196616 | tf_op jit(solution)/shard_map/ppermute | solution.py:18
  353.1 32.6 %copy-start.4 = (bf16[256,128]{0,1:T(8,128)(2,1)S(1)}, bf16[256,128]{0,1:T(8,128)(2,1)}, u32[]{:S(2)}) copy-start(bf16[256,128]{0,1:T(8,128)(2,1)} %get-tuple-element.96) | copy-start | bytes 196612
Sparse Core Ops, SparseCore 0:
  12.1 258.4 all-reduce.1
  273.5 76.5 all-gather.2
where the time goes:
time: 394 us; the launch traced here: 393 us
  waiting for transfers between devices  321 us (81%)
  matrix products  27.8 us (7%)
  between operations  16.8 us (4%)
  other arithmetic  12.7 us (3%)
  local copies, waits for them, and re-layouts  10.1 us (3%)
  starting transfers between devices  4.48 us (1%)
    psum x1, waiting for transfers between devices, per_device(): summed = lax.psum(partial_kv, 'tp')  250 us
    all_gather x1, waiting for transfers between devices, per_device(): collected = lax.all_gather(own_kv[None], 'inst', axis=0, tiled=True)  71.2 us
    dot_general x4, matrix products, attend(): lax.dot_general(queried, keys_all, (((1,), (1,)), ((), ())), preferred_el...  16.2 us
    dot_general x4, matrix products, attend(): jnp.dot(weights.astype(jnp.bfloat16), values_all, preferred_element_type=...  8.4 us
  transfers between devices with their start and end apart: 4, of which 2 were waited for; matrix products, arithmetic and copies ran while one was open for 11% of the time, Pallas kernels for 0%

commit v1 on v0

v1 whole, which is shorter than its diff:
```python
import functools
import math

import jax
import jax.numpy as jnp
from jax import lax
from jax.experimental import pallas as pl
from jax.experimental.pallas import tpu as pltpu
from jax.sharding import PartitionSpec as P

BLOCK = 128
HD = 128
TOK = 256
HALF = 2048
HEADS = 8
STEP_HEADS = 2
CHUNKS = 2
CHUNK = HALF // CHUNKS
LOW = -1e30
SCALE = HD**-0.5 * math.log2(math.e)
VMEM_LIMIT = 40 * 1024 * 1024


def swap_tp(array, mask):
    return lax.ppermute(array, "tp", [(i, i ^ mask) for i in range(16)])


def role_inst(array, pairs):
    return lax.ppermute(array, ("role", "inst"), pairs)


def project_kernel(at_ref, hidden_ref, w_ref, own_ref, *send_refs):
    x, zh = at_ref[0], at_ref[1]
    for j in (1, 2, 3, 0):
        for k in range(4):
            column = pl.multiple_of(((zh ^ k) * 4 + (x ^ j)) * HD, HD)
            part = jnp.dot(
                hidden_ref[...], w_ref[:, pl.ds(column, HD)], preferred_element_type=jnp.float32
            )
            if j == 0:
                own_ref[k] = part
            else:
                send_refs[j - 1][k] = part.astype(jnp.bfloat16)


def project(hidden, w_kv, x, zh):
    vmem = pl.BlockSpec(memory_space=pltpu.VMEM)
    return pl.pallas_call(
        project_kernel,
        out_shape=[jax.ShapeDtypeStruct((4, TOK, HD), jnp.float32)]
        + [jax.ShapeDtypeStruct((4, TOK, HD), jnp.bfloat16)] * 3,
        in_specs=[pl.BlockSpec(memory_space=pltpu.SMEM), vmem, vmem],
        out_specs=[vmem] * 4,
        compiler_params=pltpu.CompilerParams(vmem_limit_bytes=VMEM_LIMIT),
        cost_estimate=pl.CostEstimate(
            flops=2 * TOK * 512 * 2048, bytes_accessed=4 << 20, transcendentals=0
        ),
        name="project",
    )(jnp.stack([x, zh]), hidden, w_kv)


def dot_rows(a, b):
    return lax.dot_general(a, b, (((1,), (1,)), ((), ())), preferred_element_type=jnp.float32)


def attend_kernel(first, last, *refs):
    refs = list(refs)
    valid_ref, q_ref, kv_ref = refs[:3]
    refs = refs[3:]
    if not first:
        acc_in, stat_in = refs[:2]
        refs = refs[2:]
    if last:
        fresh_k, fresh_v = refs[:2]
        refs = refs[2:]
        out_ref = refs[0]
        refs = refs[1:]
    else:
        acc_out, stat_out = refs[:2]
        refs = refs[2:]
    keys, values = refs[:2]
    if last:
        fresh_ext = refs[2]
    step = pl.program_id(0)
    valid = valid_ref[0]
    count = keys.shape[0]

    @pl.when(step == 0)
    def prepare():
        inside = lax.broadcasted_iota(jnp.int32, (count, HD), 0) < valid
        rows = kv_ref[0]
        keys[...] = jnp.where(inside, rows, jnp.broadcast_to(rows[:1], rows.shape))
        values[:, :HD] = jnp.where(inside, kv_ref[1], 0)
        values[:, HD:] = jnp.where(inside, 1.0, 0.0).astype(jnp.bfloat16)
        if last:
            fresh_ext[:, :HD] = fresh_v[...]
            fresh_ext[:, HD:] = jnp.ones((TOK, HD), jnp.bfloat16)

    lane = lax.broadcasted_iota(jnp.int32, (TOK, HD), 1)

    def state(at):
        if first:
            return (
                jnp.full((TOK, 1), LOW, jnp.float32),
                jnp.zeros((TOK, HD), jnp.float32),
                jnp.zeros((TOK, HD), jnp.float32),
            )
        head = step * STEP_HEADS + at
        stats = stat_in[...]
        top = jnp.sum(jnp.where(lane == head, stats, 0.0), axis=1, keepdims=True)
        total = jnp.sum(jnp.where(lane == head + HEADS, stats, 0.0), axis=1, keepdims=True)
        acc = acc_in[:, at * HD : (at + 1) * HD]
        return top, jnp.broadcast_to(total, (TOK, HD)), acc

    def store(at, top, total, acc):
        if last:
            out_ref[:, at * HD : (at + 1) * HD] = (acc / total).astype(jnp.bfloat16)
        else:
            head = step * STEP_HEADS + at
            acc_out[:, at * HD : (at + 1) * HD] = acc
            stat_out[...] = jnp.where(
                lane == head,
                jnp.broadcast_to(top, (TOK, HD)),
                jnp.where(lane == head + HEADS, total, stat_out[...]),
            )

    def compute(with_cache):
        for at in range(STEP_HEADS):
            queried = q_ref[:, at * HD : (at + 1) * HD]
            top, total, acc = state(at)
            scores = []
            if with_cache:
                scores.append(dot_rows(queried, keys[...]))
            if last:
                new = dot_rows(queried, fresh_k[...])
                row = lax.broadcasted_iota(jnp.int32, (TOK, TOK), 0)
                column = lax.broadcasted_iota(jnp.int32, (TOK, TOK), 1)
                scores.append(jnp.where(column <= row, new, LOW))
            peak = top
            for block in scores:
                peak = jnp.maximum(peak, jnp.max(block, axis=1, keepdims=True))
            shift = peak * SCALE
            ext = None
            for index, block in enumerate(scores):
                weights = jnp.exp2(block * SCALE - shift).astype(jnp.bfloat16)
                holder = values if with_cache and index == 0 else fresh_ext
                term = jnp.dot(weights, holder[...], preferred_element_type=jnp.float32)
                ext = term if ext is None else ext + term
            if ext is None:
                store(at, top, total, acc)
            elif first:
                store(at, peak, ext[:, HD:], ext[:, :HD])
            else:
                decay = jnp.exp2((top - peak) * SCALE)
                store(at, peak, total * decay + ext[:, HD:], acc * decay + ext[:, :HD])

    if not last:

        @pl.when(step == 0)
        def clear():
            stat_out[...] = jnp.zeros_like(stat_out)

    pl.when(valid > 0)(lambda: compute(True))
    pl.when(valid <= 0)(lambda: compute(False))


def attend(valid, queries, cache, chunk, count, state=None, fresh=None):
    first, last = state is None, fresh is not None
    wide = STEP_HEADS * HD
    heads_spec = pl.BlockSpec((TOK, wide), lambda h: (0, h))
    whole = pl.BlockSpec((TOK, HD), lambda h: (0, 0))
    in_specs = [
        pl.BlockSpec(memory_space=pltpu.SMEM),
        heads_spec,
        pl.BlockSpec((2, count, HD), lambda h: (0, chunk, 0)),
    ]
    args = [valid.reshape(1), queries, cache]
    if not first:
        in_specs += [heads_spec, whole]
        args += list(state)
    scratch = [pltpu.VMEM((count, HD), jnp.bfloat16), pltpu.VMEM((count, 2 * HD), jnp.bfloat16)]
    if last:
        in_specs += [whole, whole]
        args += list(fresh)
        scratch.append(pltpu.VMEM((TOK, 2 * HD), jnp.bfloat16))
        out_shape = jax.ShapeDtypeStruct((TOK, HEADS * HD), jnp.bfloat16)
        out_specs = heads_spec
    else:
        out_shape = [
            jax.ShapeDtypeStruct((TOK, HEADS * HD), jnp.float32),
            jax.ShapeDtypeStruct((TOK, HD), jnp.float32),
        ]
        out_specs = [heads_spec, whole]
    slots = count + (TOK if last else 0)
    return pl.pallas_call(
        functools.partial(attend_kernel, first, last),
        grid=(HEADS // STEP_HEADS,),
        out_shape=out_shape,
        in_specs=in_specs,
        out_specs=out_specs,
        scratch_shapes=scratch,
        compiler_params=pltpu.CompilerParams(vmem_limit_bytes=VMEM_LIMIT),
        cost_estimate=pl.CostEstimate(
            flops=8 * TOK * HEADS * slots * HD,
            bytes_accessed=4 << 20,
            transcendentals=TOK * HEADS * slots,
        ),
        name="attend_last" if last else ("attend_first" if first else "attend_more"),
    )(*args)


def rotation(positions, is_key):
    half = HD // 2
    frequency = jnp.exp(jnp.arange(half).astype(jnp.float32) * (-2.0 * math.log(500000.0) / HD))
    angles = positions[:, None] * frequency[None, :]
    cosine = jnp.where(is_key, jnp.cos(angles), 1.0)
    sine = jnp.where(is_key, jnp.sin(angles), 0.0)
    return cosine, sine


def per_device(hidden, queries, prefix_cache, lengths, pairing, w_kv):
    member = lax.axis_index("tp")
    inst = lax.axis_index("inst")
    role = lax.axis_index("role")
    x, zh = member % 4, member // 4
    y, zl = inst % 4, inst // 4
    is_key = member % 2 == 0
    length = lengths[0, 0]
    limit = length * BLOCK
    low_valid = jnp.minimum(limit, HALF)
    high_valid = limit - low_valid
    own_valid = jnp.where(is_key, low_valid, high_valid)
    other_valid = jnp.where(is_key, high_valid, low_valid)
    resident = prefix_cache[0, 0, 0]
    queried = queries[0, 0]

    own, *sends = project(hidden[0, 0], w_kv, x, zh)
    with jax.named_scope("sum_x"):
        arrived = [swap_tp(sends[j - 1], j) for j in (1, 2, 3)]
    with jax.named_scope("prefix"):
        across = [
            swap_tp(resident[:, c * CHUNK : (c + 1) * CHUNK], 1) for c in range(CHUNKS)
        ]
    summed = own
    for block in arrived:
        summed = summed + block.astype(jnp.float32)
    with jax.named_scope("sum_z"):
        arrived = [swap_tp(summed[k].astype(jnp.bfloat16), 4 * k) for k in (1, 2, 3)]
    total = summed[0]
    for block in arrived:
        total = total + block.astype(jnp.float32)
    cosine, sine = rotation((limit + jnp.arange(TOK)).astype(jnp.float32), is_key)
    front, back = total[:, : HD // 2], total[:, HD // 2 :]
    own_kv = jnp.concatenate(
        [front * cosine - back * sine, back * cosine + front * sine], axis=1
    ).astype(jnp.bfloat16)

    with jax.named_scope("pair"):
        other_kv = swap_tp(own_kv, 1)
    keys_new = jnp.where(is_key, own_kv, other_kv)
    values_new = jnp.where(is_key, other_kv, own_kv)

    with jax.named_scope("attention"):
        state = attend(own_valid, queried, resident, 0, HALF)
        for c in range(CHUNKS - 1):
            valid = jnp.clip(other_valid - c * CHUNK, 0, CHUNK)
            state = attend(valid, queried, across[c], 0, CHUNK, state)
        valid = jnp.clip(other_valid - (CHUNKS - 1) * CHUNK, 0, CHUNK)
        attended = attend(
            valid, queried, across[-1], 0, CHUNK, state, (keys_new, values_new)
        )

    slots = jnp.arange(16, dtype=jnp.int32)
    sources = jnp.sum(jnp.where(pairing[None, :] == slots[:, None], slots[None, :], 0), axis=1)
    with jax.named_scope("handoff_y"):
        column = [own_kv] + [
            role_inst(own_kv, [(i, i ^ j) for i in range(16)]) for j in (1, 2, 3)
        ]
    column = jnp.stack(column)
    with jax.named_scope("handoff_z"):
        offers = []
        for j in range(4):
            source = sources[(zl ^ j) * 4 + y]
            offer = lax.dynamic_index_in_dim(column, (source % 4) ^ y, 0, keepdims=False)
            offers.append(role_inst(offer, [(i, 16 + (i ^ (4 * j))) for i in range(16)]))
    handed = lax.dynamic_index_in_dim(
        jnp.stack(offers), (sources[inst] // 4) ^ zl, 0, keepdims=False
    )
    layer_kv = jnp.where(role == 1, handed, own_kv)
    return attended[None, None], layer_kv[None, None]


def solution(mesh):
    in_specs = (
        P("role", "inst", None, "tp"),
        P("role", "inst", None, "tp"),
        P("role", "inst", "tp", None, None, None),
        P("role", "inst"),
        P(),
        P("tp", None),
    )
    out_specs = (P("role", "inst", None, "tp"), P("role", "inst", None, "tp"))
    return jax.shard_map(
        per_device, mesh=mesh, in_specs=in_specs, out_specs=out_specs, check_vma=False
    )
```

time: 394 us -> 121 us (0.31)
  the two profiles are of different devices: /device:TPU:20 before, /device:TPU:27 now
where the time goes in v1:
time: 121 us
  starting transfers between devices  47.2 us (39%)
  waiting for transfers between devices  29.7 us (25%)
  Pallas kernels  22.5 us (19%)
  between operations  11.6 us (10%)
  local copies, waits for them, and re-layouts  6.56 us (5%)
  other arithmetic  3.04 us (3%)
    ppermute x9, starting transfers between devices, swap_tp(): return lax.ppermute(array, 'tp', [(i, i ^ mask) for i in range(16)])  40.1 us
    pallas_call x3, Pallas kernels, attend(): pl.pallas_call(functools.partial(attend_kernel, first, last), grid=(HEADS...  20.6 us
    ppermute x9, waiting for transfers between devices, swap_tp(): return lax.ppermute(array, 'tp', [(i, i ^ mask) for i in range(16)])  15.2 us
    ppermute x7, waiting for transfers between devices, role_inst(): return lax.ppermute(array, ('role', 'inst'), pairs)  14.5 us
    ppermute x7, starting transfers between devices, role_inst(): return lax.ppermute(array, ('role', 'inst'), pairs)  7.16 us
    unnamed x14, local copies, waits for them, and re-layouts  4.76 us
  transfers between devices with their start and end apart: 16, of which 7 were waited for; matrix products, arithmetic and copies ran while one was open for 4% of the time, Pallas kernels for 12%

profile of v1, /device:TPU:27, one launch (start us, length us, event | category | flops | bytes accessed | tf_op | source)
XLA Modules:
  0.0 120.6 jit_solution(3780067545073993521)
XLA Ops:
  0.7 1.6 %copy-done = bf16[512,2048]{1,0:T(8,128)(2,1)S(1)} copy-done((bf16[512,2048]{1,0:T(8,128)(2,1)S(1)}, bf16[512,2048]{1,0:T(8,128)(2,1)}, u32[]{:S(2)}) %copy-start) | copy-done | bytes 2097176
  2.3 0.9 copy-done.2
  3.3 1.9 %project.1 = (f32[4,256,128]{2,1,0:T(8,128)S(1)}, bf16[4,256,128]{2,1,0:T(8,128)(2,1)S(1)}, bf16[4,256,128]{2,1,0:T(8,128)(2,1)S(1)}, bf16[4,256,128]{2,1,0:T(8,128)(2,1)S(1)}) custom-call(s32[2]{0:T(128)S(1)} %pad_add_fusion.at_ref, bf16[256,512]{1,0:T(8,128)(2,1)S(1)} %bitcast.54, bf16[512,2048]{1,0:T(8,128)(2,1)S(1)} %copy-done), custom_call_target="tpu_custom_call" | custom-call | flops 536870912 | bytes 4194304 | tf_op jit(solution)/shard_map/project/pallas_call | solution.py:48
  5.1 2.2 %collective-permute-start.2 = (bf16[4,256,128]{2,1,0:T(8,128)(2,1)S(1)}, bf16[4,256,128]{2,1,0:T(8,128)(2,1)}, u32[]{:S(2)}, u32[]{:S(2)}) collective-permute-start(bf16[4,256,128]{2,1,0:T(8,128)(2,1)S(1)} %get-tuple-element.15), channel_id=1, source_target_pairs={{0,1},{1,0},{2,3},{3,2},{4,5},{5,4},{6,7},{7,6},{8,9},{9,8},{10,11... | collective-permute-start | bytes 786440 | tf_op jit(solution)/shard_map/sum_x/ppermute | solution.py:25
  7.3 4.1 %collective-permute-start.3 = (bf16[4,256,128]{2,1,0:T(8,128)(2,1)S(1)}, bf16[4,256,128]{2,1,0:T(8,128)(2,1)}, u32[]{:S(2)}, u32[]{:S(2)}) collective-permute-start(bf16[4,256,128]{2,1,0:T(8,128)(2,1)S(1)} %get-tuple-element.16), channel_id=1, source_target_pairs={{0,2},{1,3},{2,0},{3,1},{4,6},{5,7},{6,4},{7,5},{8,10},{9,11},{10,... | collective-permute-start | bytes 786440 | tf_op jit(solution)/shard_map/sum_x/ppermute | solution.py:25
  11.4 2.2 %collective-permute-start.4 = (bf16[4,256,128]{2,1,0:T(8,128)(2,1)S(1)}, bf16[4,256,128]{2,1,0:T(8,128)(2,1)}, u32[]{:S(2)}, u32[]{:S(2)}) collective-permute-start(bf16[4,256,128]{2,1,0:T(8,128)(2,1)S(1)} %get-tuple-element.17), channel_id=1, source_target_pairs={{0,3},{1,2},{2,1},{3,0},{4,7},{5,6},{6,5},{7,4},{8,11},{9,10},{10,... | collective-permute-start | bytes 786440 | tf_op jit(solution)/shard_map/sum_x/ppermute | solution.py:25
  13.5 1.1 fusion.19
  14.6 3.5 %collective-permute-start.1 = (bf16[2,1024,128]{2,1,0:T(8,128)(2,1)}, bf16[2,1024,128]{2,1,0:T(8,128)(2,1)S(1)}, u32[]{:S(2)}, u32[]{:S(2)}) collective-permute-start(bf16[2,1024,128]{2,1,0:T(8,128)(2,1)} %get-tuple-element.20), channel_id=1, source_target_pairs={{0,1},{1,0},{2,3},{3,2},{4,5},{5,4},{6,7},{7,6},{8,9},{9,8},{10,11... | collective-permute-start | bytes 1572872 | tf_op jit(solution)/shard_map/prefix/ppermute | solution.py:25
  18.1 1.9 %collective-permute-start = (bf16[2,1024,128]{2,1,0:T(8,128)(2,1)}, bf16[2,1024,128]{2,1,0:T(8,128)(2,1)S(1)}, u32[]{:S(2)}, u32[]{:S(2)}) collective-permute-start(bf16[2,1024,128]{2,1,0:T(8,128)(2,1)} %get-tuple-element.21), channel_id=1, source_target_pairs={{0,1},{1,0},{2,3},{3,2},{4,5},{5,4},{6,7},{7,6},{8,9},{9,8},{10,11... | collective-permute-start | bytes 1572872 | tf_op jit(solution)/shard_map/prefix/ppermute | solution.py:25
  20.9 5.1 %collective-permute-done.4 = bf16[4,256,128]{2,1,0:T(8,128)(2,1)} collective-permute-done((bf16[4,256,128]{2,1,0:T(8,128)(2,1)S(1)}, bf16[4,256,128]{2,1,0:T(8,128)(2,1)}, u32[]{:S(2)}, u32[]{:S(2)}) %collective-permute-start.4) | collective-permute-done | bytes 262176 | tf_op jit(solution)/shard_map/sum_x/ppermute | solution.py:25
  26.0 1.3 %fusion.18 = (bf16[4,256,128]{2,1,0:T(8,128)(2,1)S(1)}, f32[4,256,128]{2,1,0:T(8,128)S(1)}) fusion(bf16[4,256,128]{2,1,0:T(8,128)(2,1)} %collective-permute-done.4, bf16[4,256,128]{2,1,0:T(8,128)(2,1)} %collective-permute-done.3, f32[4,256,128]{2,1,0:T(8,128)S(1)} %get-tuple-element.14, bf16[4,256,128]{2,1,0:T(8,128)(2,1)} %collective-permute-done.2), kind=kLoop, calls=%fused_computation.42 | loop fusion | flops 917504 | bytes 2097152 | tf_op jit(solution)/shard_map/convert.12
  27.3 8.8 %collective-permute-start.5 = (bf16[256,128]{1,0:T(8,128)(2,1)S(1)}, bf16[256,128]{1,0:T(8,128)(2,1)S(1)}, u32[]{:S(2)}, u32[]{:S(2)}) collective-permute-start(bf16[256,128]{1,0:T(8,128)(2,1)S(1)} %get-tuple-element.26), channel_id=1, source_target_pairs={{0,4},{1,5},{2,6},{3,7},{4,0},{5,1},{6,2},{7,3},{8,12},{9,13},{10,... | collective-permute-start | bytes 196616 | tf_op jit(solution)/shard_map/sum_z/ppermute | solution.py:25
  36.1 10.6 %collective-permute-start.6 = (bf16[256,128]{1,0:T(8,128)(2,1)S(1)}, bf16[256,128]{1,0:T(8,128)(2,1)S(1)}, u32[]{:S(2)}, u32[]{:S(2)}) collective-permute-start(bf16[256,128]{1,0:T(8,128)(2,1)S(1)} %get-tuple-element.28), channel_id=1, source_target_pairs={{0,8},{1,9},{2,10},{3,11},{4,12},{5,13},{6,14},{7,15},{8,0},{9,1},... | collective-permute-start | bytes 196616 | tf_op jit(solution)/shard_map/sum_z/ppermute | solution.py:25
  46.8 1.9 %collective-permute-start.7 = (bf16[256,128]{1,0:T(8,128)(2,1)S(1)}, bf16[256,128]{1,0:T(8,128)(2,1)S(1)}, u32[]{:S(2)}, u32[]{:S(2)}) collective-permute-start(bf16[256,128]{1,0:T(8,128)(2,1)S(1)} %get-tuple-element.27), channel_id=1, source_target_pairs={{0,12},{1,13},{2,14},{3,15},{4,8},{5,9},{6,10},{7,11},{8,4},{9,5},... | collective-permute-start | bytes 196616 | tf_op jit(solution)/shard_map/sum_z/ppermute | solution.py:25
  48.7 1.2 collective-permute-done.6
  49.9 8.8 %collective-permute-done.7 = bf16[256,128]{1,0:T(8,128)(2,1)S(1)} collective-permute-done((bf16[256,128]{1,0:T(8,128)(2,1)S(1)}, bf16[256,128]{1,0:T(8,128)(2,1)S(1)}, u32[]{:S(2)}, u32[]{:S(2)}) %collective-permute-start.7) | collective-permute-done | bytes 65568 | tf_op jit(solution)/shard_map/sum_z/ppermute | solution.py:25
  59.4 0.7 collective-permute-start.9
  61.6 0.7 fusion.20
  69.9 4.9 %collective-permute-start.8 = (bf16[256,128]{1,0:T(8,128)(2,1)S(1)}, bf16[256,128]{1,0:T(8,128)(2,1)S(1)}, u32[]{:S(2)}, u32[]{:S(2)}) collective-permute-start(bf16[256,128]{1,0:T(8,128)(2,1)S(1)} %pad_maximum_fusion.1), channel_id=1, source_target_pairs={{0,1},{1,0},{2,3},{3,2},{4,5},{5,4},{6,7},{7,6},{8,9},{9,8},{10,11... | collective-permute-start | bytes 196616 | tf_op jit(solution)/shard_map/pair/ppermute | solution.py:25
  74.9 1.3 %collective-permute-start.12 = (bf16[256,128]{1,0:T(8,128)(2,1)S(1)}, bf16[256,128]{1,0:T(8,128)(2,1)S(1)}, u32[]{:S(2)}, u32[]{:S(2)}) collective-permute-start(bf16[256,128]{1,0:T(8,128)(2,1)S(1)} %get-tuple-element.25), channel_id=1, source_target_pairs={{0,256},{16,272},{32,288},{48,304},{64,320},{80,336},{96,352},{112... | collective-permute-start | bytes 196616 | tf_op jit(solution)/shard_map/handoff_z/ppermute | solution.py:29
  76.3 8.7 %attend_first.1 = (f32[256,1024]{1,0:T(8,128)S(1)}, f32[256,128]{1,0:T(8,128)S(1)}) custom-call(s32[1]{0:T(128)} %bitcast.5.refs_0_, bf16[256,1024]{1,0:T(8,128)(2,1)S(1)} %bitcast.55, bf16[2,2048,128]{2,1,0:T(8,128)(2,1)S(1)} %bitcast.53), custom_call_target="tpu_custom_call" | custom-call | flops 4294967296 | bytes 4194304 | tf_op jit(solution)/shard_map/attention/attend_first/pallas_call | solution.py:195
  85.0 1.0 copy-done.4
  88.2 1.3 %collective-permute-start.13 = (bf16[256,128]{1,0:T(8,128)(2,1)S(1)}, bf16[256,128]{1,0:T(8,128)(2,1)S(1)}, u32[]{:S(2)}, u32[]{:S(2)}) collective-permute-start(bf16[256,128]{1,0:T(8,128)(2,1)S(1)} %get-tuple-element.24), channel_id=1, source_target_pairs={{0,320},{16,336},{32,352},{48,368},{64,256},{80,272},{96,288},{112... | collective-permute-start | bytes 196616 | tf_op jit(solution)/shard_map/handoff_z/ppermute | solution.py:29
  89.5 1.3 %collective-permute-start.14 = (bf16[256,128]{1,0:T(8,128)(2,1)S(1)}, bf16[256,128]{1,0:T(8,128)(2,1)S(1)}, u32[]{:S(2)}, u32[]{:S(2)}) collective-permute-start(bf16[256,128]{1,0:T(8,128)(2,1)S(1)} %get-tuple-element.23), channel_id=1, source_target_pairs={{0,384},{16,400},{32,416},{48,432},{64,448},{80,464},{96,480},{112... | collective-permute-start | bytes 196616 | tf_op jit(solution)/shard_map/handoff_z/ppermute | solution.py:29
  90.8 1.3 %collective-permute-start.15 = (bf16[256,128]{1,0:T(8,128)(2,1)S(1)}, bf16[256,128]{1,0:T(8,128)(2,1)S(1)}, u32[]{:S(2)}, u32[]{:S(2)}) collective-permute-start(bf16[256,128]{1,0:T(8,128)(2,1)S(1)} %get-tuple-element.22), channel_id=1, source_target_pairs={{0,448},{16,464},{32,480},{48,496},{64,384},{80,400},{96,416},{112... | collective-permute-start | bytes 196616 | tf_op jit(solution)/shard_map/handoff_z/ppermute | solution.py:29
  92.2 1.8 %collective-permute-done.13 = bf16[256,128]{1,0:T(8,128)(2,1)S(1)} collective-permute-done((bf16[256,128]{1,0:T(8,128)(2,1)S(1)}, bf16[256,128]{1,0:T(8,128)(2,1)S(1)}, u32[]{:S(2)}, u32[]{:S(2)}) %collective-permute-start.13) | collective-permute-done | bytes 65568 | tf_op jit(solution)/shard_map/handoff_z/ppermute | solution.py:29
  94.0 2.1 %collective-permute-done.14 = bf16[256,128]{1,0:T(8,128)(2,1)S(1)} collective-permute-done((bf16[256,128]{1,0:T(8,128)(2,1)S(1)}, bf16[256,128]{1,0:T(8,128)(2,1)S(1)}, u32[]{:S(2)}, u32[]{:S(2)}) %collective-permute-start.14) | collective-permute-done | bytes 65568 | tf_op jit(solution)/shard_map/handoff_z/ppermute | solution.py:29
  96.0 10.7 %collective-permute-done.15 = bf16[256,128]{1,0:T(8,128)(2,1)S(1)} collective-permute-done((bf16[256,128]{1,0:T(8,128)(2,1)S(1)}, bf16[256,128]{1,0:T(8,128)(2,1)S(1)}, u32[]{:S(2)}, u32[]{:S(2)}) %collective-permute-start.15) | collective-permute-done | bytes 65568 | tf_op jit(solution)/shard_map/handoff_z/ppermute | solution.py:29
  106.7 0.7 fusion.17
  107.4 1.2 %copy-done.5 = f32[256,1024]{1,0:T(8,128)S(1)} copy-done((f32[256,1024]{1,0:T(8,128)S(1)}, f32[256,1024]{1,0:T(8,128)}, u32[]{:S(2)}) %copy-start.5) | copy-done | bytes 1048600
  108.6 5.3 %attend_more.1 = (f32[256,1024]{1,0:T(8,128)S(1)}, f32[256,128]{1,0:T(8,128)S(1)}) custom-call(s32[1]{0:T(128)} %bitcast.4.refs_0_, bf16[256,1024]{1,0:T(8,128)(2,1)S(1)} %bitcast.56, bf16[2,1024,128]{2,1,0:T(8,128)(2,1)S(1)} %collective-permute-done.1.refs_2_, f32[256,1024]{1,0:T(8,128)S(1)} %copy-done.5, f32[256,128]{1,0:T(8,128)S(1)} %get-tuple-element.11.refs_4_), custom_call_target="tpu_custom_call" | custom-call | flops 2147483648 | bytes 4194304 | tf_op jit(solution)/shard_map/attention/attend_more/pallas_call | solution.py:195
  113.9 6.7 %attend_last.1 = bf16[256,1024]{1,0:T(8,128)(2,1)} custom-call(s32[1]{0:T(128)} %bitcast.1.refs_0_, bf16[256,1024]{1,0:T(8,128)(2,1)S(1)} %bitcast.57, bf16[2,1024,128]{2,1,0:T(8,128)(2,1)S(1)} %collective-permute-done.refs_2_, f32[256,1024]{1,0:T(8,128)S(1)} %get-tuple-element.12.refs_3_, f32[256,128]{1,0:T(8,128)S(1)} %get-tuple-element.13.refs_4_, ...), custom_call_target="tpu_custom_call" | custom-call | flops 2684354560 | bytes 4194304 | tf_op jit(solution)/shard_map/attention/attend_last/pallas_call | solution.py:195
  (33 shorter events, 2.6 us)
Async XLA Ops:
  0.7 1.6 %copy-start = (bf16[512,2048]{1,0:T(8,128)(2,1)S(1)}, bf16[512,2048]{1,0:T(8,128)(2,1)}, u32[]{:S(2)}) copy-start(bf16[512,2048]{1,0:T(8,128)(2,1)} %w_ref.1) | copy-start | bytes 6291460
  2.3 0.9 copy-start.2
  3.3 10.3 %copy-start.1 = (bf16[1,1,1,2,2048,128]{5,4,3,2,1,0:T(8,128)(2,1)S(1)}, bf16[1,1,1,2,2048,128]{5,4,3,2,1,0:T(8,128)(2,1)}, u32[]{:S(2)}) copy-start(bf16[1,1,1,2,2048,128]{5,4,3,2,1,0:T(8,128)(2,1)} %param.8) | copy-start | bytes 3145732
  5.1 15.6 %collective-permute-start.2 = (bf16[4,256,128]{2,1,0:T(8,128)(2,1)S(1)}, bf16[4,256,128]{2,1,0:T(8,128)(2,1)}, u32[]{:S(2)}, u32[]{:S(2)}) collective-permute-start(bf16[4,256,128]{2,1,0:T(8,128)(2,1)S(1)} %get-tuple-element.15), channel_id=1, source_target_pairs={{0,1},{1,0},{2,3},{3,2},{4,5},{5,4},{6,7},{7,6},{8,9},{9,8},{10,11... | collective-permute-start | bytes 786440 | tf_op jit(solution)/shard_map/sum_x/ppermute | solution.py:25
  7.3 13.6 %collective-permute-start.3 = (bf16[4,256,128]{2,1,0:T(8,128)(2,1)S(1)}, bf16[4,256,128]{2,1,0:T(8,128)(2,1)}, u32[]{:S(2)}, u32[]{:S(2)}) collective-permute-start(bf16[4,256,128]{2,1,0:T(8,128)(2,1)S(1)} %get-tuple-element.16), channel_id=1, source_target_pairs={{0,2},{1,3},{2,0},{3,1},{4,6},{5,7},{6,4},{7,5},{8,10},{9,11},{10,... | collective-permute-start | bytes 786440 | tf_op jit(solution)/shard_map/sum_x/ppermute | solution.py:25
  11.4 14.6 %collective-permute-start.4 = (bf16[4,256,128]{2,1,0:T(8,128)(2,1)S(1)}, bf16[4,256,128]{2,1,0:T(8,128)(2,1)}, u32[]{:S(2)}, u32[]{:S(2)}) collective-permute-start(bf16[4,256,128]{2,1,0:T(8,128)(2,1)S(1)} %get-tuple-element.17), channel_id=1, source_target_pairs={{0,3},{1,2},{2,1},{3,0},{4,7},{5,6},{6,5},{7,4},{8,11},{9,10},{10,... | collective-permute-start | bytes 786440 | tf_op jit(solution)/shard_map/sum_x/ppermute | solution.py:25
  14.6 46.8 %copy-start.6 = (s32[16]{0:T(128)S(1)}, s32[16]{0:T(128)}, u32[]{:S(2)}) copy-start(s32[16]{0:T(128)} %param.10) | copy-start | bytes 196
  14.6 92.8 %collective-permute-start.1 = (bf16[2,1024,128]{2,1,0:T(8,128)(2,1)}, bf16[2,1024,128]{2,1,0:T(8,128)(2,1)S(1)}, u32[]{:S(2)}, u32[]{:S(2)}) collective-permute-start(bf16[2,1024,128]{2,1,0:T(8,128)(2,1)} %get-tuple-element.20), channel_id=1, source_target_pairs={{0,1},{1,0},{2,3},{3,2},{4,5},{5,4},{6,7},{7,6},{8,9},{9,8},{10,11... | collective-permute-start | bytes 1572872 | tf_op jit(solution)/shard_map/prefix/ppermute | solution.py:25
  18.1 95.8 %collective-permute-start = (bf16[2,1024,128]{2,1,0:T(8,128)(2,1)}, bf16[2,1024,128]{2,1,0:T(8,128)(2,1)S(1)}, u32[]{:S(2)}, u32[]{:S(2)}) collective-permute-start(bf16[2,1024,128]{2,1,0:T(8,128)(2,1)} %get-tuple-element.21), channel_id=1, source_target_pairs={{0,1},{1,0},{2,3},{3,2},{4,5},{5,4},{6,7},{7,6},{8,9},{9,8},{10,11... | collective-permute-start | bytes 1572872 | tf_op jit(solution)/shard_map/prefix/ppermute | solution.py:25
  26.0 50.3 %copy-start.3 = (bf16[1,1,256,1024]{3,2,1,0:T(8,128)(2,1)S(1)}, bf16[1,1,256,1024]{3,2,1,0:T(8,128)(2,1)}, u32[]{:S(2)}) copy-start(bf16[1,1,256,1024]{3,2,1,0:T(8,128)(2,1)} %param.7) | copy-start | bytes 1572868
  27.3 21.4 %collective-permute-start.5 = (bf16[256,128]{1,0:T(8,128)(2,1)S(1)}, bf16[256,128]{1,0:T(8,128)(2,1)S(1)}, u32[]{:S(2)}, u32[]{:S(2)}) collective-permute-start(bf16[256,128]{1,0:T(8,128)(2,1)S(1)} %get-tuple-element.26), channel_id=1, source_target_pairs={{0,4},{1,5},{2,6},{3,7},{4,0},{5,1},{6,2},{7,3},{8,12},{9,13},{10,... | collective-permute-start | bytes 196616 | tf_op jit(solution)/shard_map/sum_z/ppermute | solution.py:25
  36.1 13.8 %collective-permute-start.6 = (bf16[256,128]{1,0:T(8,128)(2,1)S(1)}, bf16[256,128]{1,0:T(8,128)(2,1)S(1)}, u32[]{:S(2)}, u32[]{:S(2)}) collective-permute-start(bf16[256,128]{1,0:T(8,128)(2,1)S(1)} %get-tuple-element.28), channel_id=1, source_target_pairs={{0,8},{1,9},{2,10},{3,11},{4,12},{5,13},{6,14},{7,15},{8,0},{9,1},... | collective-permute-start | bytes 196616 | tf_op jit(solution)/shard_map/sum_z/ppermute | solution.py:25
  46.8 11.9 %collective-permute-start.7 = (bf16[256,128]{1,0:T(8,128)(2,1)S(1)}, bf16[256,128]{1,0:T(8,128)(2,1)S(1)}, u32[]{:S(2)}, u32[]{:S(2)}) collective-permute-start(bf16[256,128]{1,0:T(8,128)(2,1)S(1)} %get-tuple-element.27), channel_id=1, source_target_pairs={{0,12},{1,13},{2,14},{3,15},{4,8},{5,9},{6,10},{7,11},{8,4},{9,5},... | collective-permute-start | bytes 196616 | tf_op jit(solution)/shard_map/sum_z/ppermute | solution.py:25
  59.4 10.4 %collective-permute-start.9 = (bf16[256,128]{1,0:T(8,128)(2,1)S(1)}, bf16[256,128]{1,0:T(8,128)(2,1)S(1)}, u32[]{:S(2)}, u32[]{:S(2)}) collective-permute-start(bf16[256,128]{1,0:T(8,128)(2,1)S(1)} %pad_maximum_fusion.1), channel_id=1, source_target_pairs={{0,16},{16,0},{32,48},{48,32},{64,80},{80,64},{96,112},{112,96},{1... | collective-permute-start | bytes 196616 | tf_op jit(solution)/shard_map/handoff_y/ppermute | solution.py:29
  60.1 14.7 %collective-permute-start.10 = (bf16[256,128]{1,0:T(8,128)(2,1)S(1)}, bf16[256,128]{1,0:T(8,128)(2,1)S(1)}, u32[]{:S(2)}, u32[]{:S(2)}) collective-permute-start(bf16[256,128]{1,0:T(8,128)(2,1)S(1)} %pad_maximum_fusion.1), channel_id=1, source_target_pairs={{0,32},{16,48},{32,0},{48,16},{64,96},{80,112},{96,64},{112,80},{1... | collective-permute-start | bytes 196616 | tf_op jit(solution)/shard_map/handoff_y/ppermute | solution.py:29
  60.8 14.0 %collective-permute-start.11 = (bf16[256,128]{1,0:T(8,128)(2,1)S(1)}, bf16[256,128]{1,0:T(8,128)(2,1)S(1)}, u32[]{:S(2)}, u32[]{:S(2)}) collective-permute-start(bf16[256,128]{1,0:T(8,128)(2,1)S(1)} %pad_maximum_fusion.1), channel_id=1, source_target_pairs={{0,48},{16,32},{32,16},{48,0},{64,112},{80,96},{96,80},{112,64},{1... | collective-permute-start | bytes 196616 | tf_op jit(solution)/shard_map/handoff_y/ppermute | solution.py:29
  69.9 19.7 %collective-permute-start.8 = (bf16[256,128]{1,0:T(8,128)(2,1)S(1)}, bf16[256,128]{1,0:T(8,128)(2,1)S(1)}, u32[]{:S(2)}, u32[]{:S(2)}) collective-permute-start(bf16[256,128]{1,0:T(8,128)(2,1)S(1)} %pad_maximum_fusion.1), channel_id=1, source_target_pairs={{0,1},{1,0},{2,3},{3,2},{4,5},{5,4},{6,7},{7,6},{8,9},{9,8},{10,11... | collective-permute-start | bytes 196616 | tf_op jit(solution)/shard_map/pair/ppermute | solution.py:25
  74.9 15.9 %collective-permute-start.12 = (bf16[256,128]{1,0:T(8,128)(2,1)S(1)}, bf16[256,128]{1,0:T(8,128)(2,1)S(1)}, u32[]{:S(2)}, u32[]{:S(2)}) collective-permute-start(bf16[256,128]{1,0:T(8,128)(2,1)S(1)} %get-tuple-element.25), channel_id=1, source_target_pairs={{0,256},{16,272},{32,288},{48,304},{64,320},{80,336},{96,352},{112... | collective-permute-start | bytes 196616 | tf_op jit(solution)/shard_map/handoff_z/ppermute | solution.py:29
  84.9 1.0 copy-start.4
  88.2 5.7 %collective-permute-start.13 = (bf16[256,128]{1,0:T(8,128)(2,1)S(1)}, bf16[256,128]{1,0:T(8,128)(2,1)S(1)}, u32[]{:S(2)}, u32[]{:S(2)}) collective-permute-start(bf16[256,128]{1,0:T(8,128)(2,1)S(1)} %get-tuple-element.24), channel_id=1, source_target_pairs={{0,320},{16,336},{32,352},{48,368},{64,256},{80,272},{96,288},{112... | collective-permute-start | bytes 196616 | tf_op jit(solution)/shard_map/handoff_z/ppermute | solution.py:29
  89.5 6.5 %collective-permute-start.14 = (bf16[256,128]{1,0:T(8,128)(2,1)S(1)}, bf16[256,128]{1,0:T(8,128)(2,1)S(1)}, u32[]{:S(2)}, u32[]{:S(2)}) collective-permute-start(bf16[256,128]{1,0:T(8,128)(2,1)S(1)} %get-tuple-element.23), channel_id=1, source_target_pairs={{0,384},{16,400},{32,416},{48,432},{64,448},{80,464},{96,480},{112... | collective-permute-start | bytes 196616 | tf_op jit(solution)/shard_map/handoff_z/ppermute | solution.py:29
  90.8 15.9 %collective-permute-start.15 = (bf16[256,128]{1,0:T(8,128)(2,1)S(1)}, bf16[256,128]{1,0:T(8,128)(2,1)S(1)}, u32[]{:S(2)}, u32[]{:S(2)}) collective-permute-start(bf16[256,128]{1,0:T(8,128)(2,1)S(1)} %get-tuple-element.22), channel_id=1, source_target_pairs={{0,448},{16,464},{32,480},{48,496},{64,384},{80,400},{96,416},{112... | collective-permute-start | bytes 196616 | tf_op jit(solution)/shard_map/handoff_z/ppermute | solution.py:29
  107.4 1.2 %copy-start.5 = (f32[256,1024]{1,0:T(8,128)S(1)}, f32[256,1024]{1,0:T(8,128)}, u32[]{:S(2)}) copy-start(f32[256,1024]{1,0:T(8,128)} %copy-done.4) | copy-start | bytes 3145732

commit v2 on v0

v2 whole, which is shorter than its diff:
```python
import functools
import math

import jax
import jax.numpy as jnp
from jax import lax
from jax.experimental import pallas as pl
from jax.experimental.pallas import tpu as pltpu
from jax.sharding import PartitionSpec as P

BLOCK = 128
HD = 128
TOK = 256
HALF = 2048
HEADS = 8
STEP_HEADS = 4
SUB = 512
FEATURES = 512
LOW = -1e30
SCALE = HD**-0.5 * math.log2(math.e)

SMEM = pl.BlockSpec(memory_space=pltpu.SMEM)
VMEM = pl.BlockSpec(memory_space=pltpu.VMEM)
HBM = pl.BlockSpec(memory_space=pltpu.HBM)
ANY = pl.BlockSpec(memory_space=pl.ANY)


def params(mib):
    return pltpu.CompilerParams(vmem_limit_bytes=mib * 1024 * 1024)


def struct(shape, dtype):
    return jax.ShapeDtypeStruct(shape, dtype)


def swap_tp(array, mask):
    return lax.ppermute(array, "tp", [(i, i ^ mask) for i in range(16)])


def role_inst(array, pairs):
    return lax.ppermute(array, ("role", "inst"), pairs)


def project_kernel(member_ref, hidden_hbm, w_hbm, own_ref, *rest):
    send_refs, (hidden, weights, hidden_sem, sems) = rest[:3], rest[3:]
    member = member_ref[0]
    order = [(j, k) for j in (2, 3, 1, 0) for k in range(4)]
    fetch_hidden = pltpu.make_async_copy(hidden_hbm, hidden, hidden_sem)
    fetch_hidden.start()
    copies = []
    for slot, (j, k) in enumerate(order):
        column = pl.multiple_of((member ^ (4 * k + j)) * HD, HD)
        copy = pltpu.make_async_copy(
            w_hbm.at[:, pl.ds(column, HD)], weights.at[slot], sems.at[slot]
        )
        copy.start()
        copies.append(copy)
    fetch_hidden.wait()
    for slot, (j, k) in enumerate(order):
        copies[slot].wait()
        part = jnp.dot(hidden[...], weights[slot], preferred_element_type=jnp.float32)
        if j == 0:
            own_ref[k] = part
        else:
            send_refs[j - 1][k] = part.astype(jnp.bfloat16)


def project(member, hidden, w_kv):
    return pl.pallas_call(
        project_kernel,
        out_shape=[struct((4, TOK, HD), jnp.float32)] + [struct((4, TOK, HD), jnp.bfloat16)] * 3,
        in_specs=[SMEM, HBM, HBM],
        out_specs=[VMEM] * 4,
        scratch_shapes=[
            pltpu.VMEM((TOK, FEATURES), jnp.bfloat16),
            pltpu.VMEM((16, FEATURES, HD), jnp.bfloat16),
            pltpu.SemaphoreType.DMA,
            pltpu.SemaphoreType.DMA((16,)),
        ],
        compiler_params=params(60),
        cost_estimate=pl.CostEstimate(
            flops=2 * TOK * FEATURES * 2048, bytes_accessed=4 << 20, transcendentals=0
        ),
        name="project",
    )(member, hidden, w_kv)


def sum_x_kernel(own_ref, a_ref, b_ref, c_ref, after_ref, keep_ref, *send_refs):
    for k in range(4):
        total = own_ref[k] + a_ref[k].astype(jnp.float32)
        total = total + b_ref[k].astype(jnp.float32) + c_ref[k].astype(jnp.float32)
        if k == 0:
            keep_ref[...] = total
        else:
            send_refs[k - 1][...] = total.astype(jnp.bfloat16)


def sum_x(own, arrived, after):
    return pl.pallas_call(
        sum_x_kernel,
        out_shape=[struct((TOK, HD), jnp.float32)] + [struct((TOK, HD), jnp.bfloat16)] * 3,
        in_specs=[VMEM] * 4 + [ANY],
        out_specs=[VMEM] * 4,
        compiler_params=params(8),
        name="sum_x",
    )(own, *arrived, after)


def finish_kernel(keep_ref, a_ref, b_ref, c_ref, cosine_ref, sine_ref, after_ref, out_ref):
    total = keep_ref[...] + a_ref[...].astype(jnp.float32)
    total = total + b_ref[...].astype(jnp.float32) + c_ref[...].astype(jnp.float32)
    turned = pltpu.roll(total, HD // 2, 1)
    out_ref[...] = (total * cosine_ref[...] + turned * sine_ref[...]).astype(jnp.bfloat16)


def finish(keep, arrived, cosine, sine, after):
    return pl.pallas_call(
        finish_kernel,
        out_shape=struct((TOK, HD), jnp.bfloat16),
        in_specs=[VMEM] * 6 + [ANY],
        out_specs=VMEM,
        compiler_params=params(8),
        name="finish",
    )(keep, *arrived, cosine, sine, after)


def source_of(pairing_ref, target):
    source = jnp.int32(0)
    for i in range(16):
        source = jnp.where(pairing_ref[i] == target, i, source)
    return source


def choose(index, refs):
    block = refs[0][...]
    for at in range(1, len(refs)):
        block = jnp.where(index == at, refs[at][...], block)
    return block


def offer_kernel(pairing_ref, inst_ref, *refs):
    column, outs = refs[:4], refs[4:]
    inst = inst_ref[0]
    for j in range(4):
        source = source_of(pairing_ref, inst ^ (4 * j))
        outs[j][...] = choose((source ^ inst) & 3, column)


def offer(pairing, inst, column):
    return pl.pallas_call(
        offer_kernel,
        out_shape=[struct((TOK, HD), jnp.bfloat16)] * 4,
        in_specs=[SMEM] * 2 + [VMEM] * 4,
        out_specs=[VMEM] * 4,
        compiler_params=params(8),
        name="offer",
    )(pairing, inst, *column)


def take_kernel(pairing_ref, inst_ref, role_ref, own_ref, *refs):
    offers, out_ref = refs[:4], refs[5]
    inst = inst_ref[0]
    source = source_of(pairing_ref, inst)
    handed = choose((source ^ inst) // 4, offers)
    out_ref[...] = jnp.where(role_ref[0] == 1, handed, own_ref[...])


def take(pairing, inst, role, own_kv, offers, after):
    return pl.pallas_call(
        take_kernel,
        out_shape=struct((TOK, HD), jnp.bfloat16),
        in_specs=[SMEM] * 3 + [VMEM] * 5 + [ANY],
        out_specs=VMEM,
        compiler_params=params(8),
        name="take",
    )(pairing, inst, role, own_kv, *offers, after)


def dot_rows(a, b):
    return lax.dot_general(a, b, (((1,), (1,)), ((), ())), preferred_element_type=jnp.float32)


def load_cache(valid, kv_ref, keys, values):
    inside = lax.broadcasted_iota(jnp.int32, (HALF, HD), 0) < valid
    rows = kv_ref[0]
    keys[...] = jnp.where(inside, rows, jnp.broadcast_to(rows[:1], rows.shape))
    values[:, :HD] = jnp.where(inside, kv_ref[1], 0)
    values[:, HD:] = jnp.where(inside, 1.0, 0.0).astype(jnp.bfloat16)


def update(top, ext, scores, values):
    peak = jnp.max(scores, axis=1, keepdims=True) * SCALE
    if top is not None:
        peak = jnp.maximum(top, peak)
    weights = jnp.exp2(scores * SCALE - peak).astype(jnp.bfloat16)
    term = jnp.dot(weights, values, preferred_element_type=jnp.float32)
    if top is not None:
        term = ext * jnp.exp2(top - peak) + term
    return peak, term


def over_cache(top, ext, queried, keys, values):
    for at in range(0, HALF, SUB):
        scores = dot_rows(queried, keys[at : at + SUB, :])
        top, ext = update(top, ext, scores, values[at : at + SUB, :])
    return top, ext


def own_half_kernel(aliased, length_ref, member_ref, q_ref, kv_ref, *refs):
    refs = refs[3:] if aliased else refs[1:]
    acc_ref, stat_ref, keys, values = refs
    limit = length_ref[0] * BLOCK
    low = jnp.minimum(limit, HALF)
    valid = jnp.where(member_ref[0] % 2 == 0, low, limit - low)
    lane = lax.broadcasted_iota(jnp.int32, (TOK, HD), 1)

    @pl.when(valid > 0)
    def some():
        load_cache(valid, kv_ref, keys, values)
        stats = jnp.zeros((TOK, HD), jnp.float32)
        for at in range(STEP_HEADS):
            span = slice(at * HD, (at + 1) * HD)
            top, ext = over_cache(None, None, q_ref[:, span], keys, values)
            acc_ref[:, span] = ext[:, :HD]
            stats = jnp.where(lane == at, jnp.broadcast_to(top, (TOK, HD)), stats)
            stats = jnp.where(lane == at + STEP_HEADS, ext[:, HD:], stats)
        stat_ref[...] = stats

    @pl.when(valid <= 0)
    def none():
        acc_ref[...] = jnp.zeros_like(acc_ref)
        stat_ref[...] = jnp.where(lane < STEP_HEADS, LOW, 0.0)


def own_half(length, member, queries, cache, group, after, state=None):
    wide = STEP_HEADS * HD
    groups = HEADS // STEP_HEADS
    in_specs = [
        SMEM,
        SMEM,
        pl.BlockSpec((TOK, wide), lambda i: (0, group)),
        pl.BlockSpec((2, HALF, HD), lambda i: (0, 0, 0)),
        ANY,
    ]
    args = [length, member, queries, cache, after]
    aliases = {}
    if state is not None:
        aliases = {len(args): 0, len(args) + 1: 1}
        in_specs += [ANY, ANY]
        args += list(state)
    return pl.pallas_call(
        functools.partial(own_half_kernel, state is not None),
        grid=(1,),
        out_shape=[
            struct((TOK, HEADS * HD), jnp.float32),
            struct((TOK, groups * HD), jnp.float32),
        ],
        in_specs=in_specs,
        out_specs=[
            pl.BlockSpec((TOK, wide), lambda i: (0, group)),
            pl.BlockSpec((TOK, HD), lambda i: (0, group)),
        ],
        scratch_shapes=[
            pltpu.VMEM((HALF, HD), jnp.bfloat16),
            pltpu.VMEM((HALF, 2 * HD), jnp.bfloat16),
        ],
        input_output_aliases=aliases,
        compiler_params=params(24),
        cost_estimate=pl.CostEstimate(
            flops=8 * TOK * STEP_HEADS * HALF * HD,
            bytes_accessed=2 << 20,
            transcendentals=TOK * STEP_HEADS * HALF,
        ),
        name="own_half",
    )(*args)


def other_half_kernel(
    length_ref, member_ref, q_ref, kv_ref, acc_ref, stat_ref, mine_ref, theirs_ref,
    after_ref, out_ref, keys, values, new_keys, new_values,
):
    limit = length_ref[0] * BLOCK
    low = jnp.minimum(limit, HALF)
    is_key = member_ref[0] % 2 == 0
    valid = jnp.where(is_key, limit - low, low)
    lane = lax.broadcasted_iota(jnp.int32, (TOK, HD), 1)

    @pl.when(pl.program_id(0) == 0)
    def prepare():
        load_cache(valid, kv_ref, keys, values)
        new_keys[...] = jnp.where(is_key, mine_ref[...], theirs_ref[...])
        new_values[:, :HD] = jnp.where(is_key, theirs_ref[...], mine_ref[...])
        new_values[:, HD:] = jnp.ones((TOK, HD), jnp.bfloat16)

    def run(with_cache):
        stats = stat_ref[...]
        row = lax.broadcasted_iota(jnp.int32, (TOK, TOK), 0)
        column = lax.broadcasted_iota(jnp.int32, (TOK, TOK), 1)
        for at in range(STEP_HEADS):
            span = slice(at * HD, (at + 1) * HD)
            queried = q_ref[:, span]
            top = stats[:, at : at + 1]
            total = stats[:, at + STEP_HEADS : at + STEP_HEADS + 1]
            ext = jnp.concatenate(
                [acc_ref[:, span], jnp.broadcast_to(total, (TOK, HD))], axis=1
            )
            if with_cache:
                top, ext = over_cache(top, ext, queried, keys, values)
            scores = jnp.where(column <= row, dot_rows(queried, new_keys[...]), LOW)
            top, ext = update(top, ext, scores, new_values[...])
            out_ref[:, span] = (ext[:, :HD] / ext[:, HD:]).astype(jnp.bfloat16)

    pl.when(valid > 0)(lambda: run(True))
    pl.when(valid <= 0)(lambda: run(False))


def other_half(length, member, queries, cache, state, mine, theirs, after):
    wide = STEP_HEADS * HD
    heads_spec = pl.BlockSpec((TOK, wide), lambda g: (0, g))
    whole = pl.BlockSpec((TOK, HD), lambda g: (0, 0))
    return pl.pallas_call(
        other_half_kernel,
        grid=(HEADS // STEP_HEADS,),
        out_shape=struct((TOK, HEADS * HD), jnp.bfloat16),
        in_specs=[
            SMEM,
            SMEM,
            heads_spec,
            pl.BlockSpec((2, HALF, HD), lambda g: (0, 0, 0)),
            heads_spec,
            pl.BlockSpec((TOK, HD), lambda g: (0, g)),
            whole,
            whole,
            ANY,
        ],
        out_specs=heads_spec,
        scratch_shapes=[
            pltpu.VMEM((HALF, HD), jnp.bfloat16),
            pltpu.VMEM((HALF, 2 * HD), jnp.bfloat16),
            pltpu.VMEM((TOK, HD), jnp.bfloat16),
            pltpu.VMEM((TOK, 2 * HD), jnp.bfloat16),
        ],
        compiler_params=params(32),
        cost_estimate=pl.CostEstimate(
            flops=8 * TOK * HEADS * (HALF + TOK) * HD,
            bytes_accessed=3 << 20,
            transcendentals=TOK * HEADS * (HALF + TOK),
        ),
        name="other_half",
    )(length, member, queries, cache, *state, mine, theirs, after)


def rotation(length, is_key):
    half = HD // 2
    positions = (length * BLOCK + jnp.arange(TOK)).astype(jnp.float32)
    frequency = jnp.exp(jnp.arange(half).astype(jnp.float32) * (-2.0 * math.log(500000.0) / HD))
    angles = positions[:, None] * frequency[None, :]
    cosine = jnp.where(is_key, jnp.cos(angles), 1.0)
    sine = jnp.where(is_key, jnp.sin(angles), 0.0)
    return jnp.concatenate([cosine, cosine], 1), jnp.concatenate([-sine, sine], 1)


def per_device(hidden, queries, prefix_cache, lengths, pairing, w_kv):
    member = lax.axis_index("tp").astype(jnp.int32)
    inst = lax.axis_index("inst").astype(jnp.int32).reshape(1)
    role = lax.axis_index("role").astype(jnp.int32).reshape(1)
    length = lengths.reshape(1)
    resident = prefix_cache[0, 0, 0]
    queried = queries[0, 0]
    cosine, sine = rotation(lengths[0, 0], member % 2 == 0)
    member = member.reshape(1)

    own, *sends = project(member, hidden[0, 0], w_kv)
    with jax.named_scope("sum_x"):
        arrived = [swap_tp(sends[j - 1], j) for j in (1, 2, 3)]
    with jax.named_scope("prefix"):
        across = swap_tp(resident, 1)
    state = own_half(length, member, queried, resident, 0, sends[0])
    keep, *sends = sum_x(own, arrived, state[1])
    with jax.named_scope("sum_z"):
        arrived = [swap_tp(sends[k - 1], 4 * k) for k in (1, 2, 3)]
    state = own_half(length, member, queried, resident, 1, sends[0], state)
    own_kv = finish(keep, arrived, cosine, sine, state[1])

    with jax.named_scope("handoff_y"):
        column = [own_kv] + [
            role_inst(own_kv, [(i, i ^ j) for i in range(16)]) for j in (1, 2, 3)
        ]
    with jax.named_scope("pair"):
        other_kv = swap_tp(own_kv, 1)
    offers = offer(pairing, inst, column)
    with jax.named_scope("handoff_z"):
        offered = [
            role_inst(offers[j], [(i, 16 + (i ^ (4 * j))) for i in range(16)]) for j in range(4)
        ]
    attended = other_half(
        length, member, queried, across, state, own_kv, other_kv, offers[0]
    )
    layer_kv = take(pairing, inst, role, own_kv, offered, attended)
    return attended[None, None], layer_kv[None, None]


def solution(mesh):
    in_specs = (
        P("role", "inst", None, "tp"),
        P("role", "inst", None, "tp"),
        P("role", "inst", "tp", None, None, None),
        P("role", "inst"),
        P(),
        P("tp", None),
    )
    out_specs = (P("role", "inst", None, "tp"), P("role", "inst", None, "tp"))
    return jax.shard_map(
        per_device, mesh=mesh, in_specs=in_specs, out_specs=out_specs, check_vma=False
    )
```

time: 394 us -> 112 us (0.28)
  the two profiles are of different devices: /device:TPU:20 before, /device:TPU:40 now
where the time goes in v2:
time: 112 us; the launch traced here: 111 us
  starting transfers between devices  51.7 us (46%)
  Pallas kernels  28.4 us (25%)
  waiting for transfers between devices  22.3 us (20%)
  local copies, waits for them, and re-layouts  6.28 us (6%)
  between operations  1.6 us (1%)
    ppermute x8, starting transfers between devices, swap_tp(): return lax.ppermute(array, 'tp', [(i, i ^ mask) for i in range(16)])  37.1 us
    ppermute x8, waiting for transfers between devices, swap_tp(): return lax.ppermute(array, 'tp', [(i, i ^ mask) for i in range(16)])  18.7 us
    ppermute x7, starting transfers between devices, role_inst(): return lax.ppermute(array, ('role', 'inst'), pairs)  14.6 us
    pallas_call x1, Pallas kernels, other_half(): pl.pallas_call(other_half_kernel, grid=(HEADS // STEP_HEADS,), out_shape=...  13.9 us
    unnamed x18, local copies, waits for them, and re-layouts  6.28 us
    pallas_call x2, Pallas kernels, own_half(): pl.pallas_call(functools.partial(own_half_kernel, state is not None), gri...  6.22 us
    pallas_call x1, Pallas kernels, project(): pl.pallas_call(project_kernel, out_shape=[struct((4, TOK, HD), jnp.float3...  6.18 us
    ppermute x7, waiting for transfers between devices, role_inst(): return lax.ppermute(array, ('role', 'inst'), pairs)  3.57 us
  transfers between devices with their start and end apart: 15, of which 4 were waited for; matrix products, arithmetic and copies ran while one was open for 1% of the time, Pallas kernels for 25%

profile of v2, /device:TPU:40, one launch (start us, length us, event | category | flops | bytes accessed | tf_op | source)
XLA Modules:
  0.0 110.9 jit_solution(11945090668090812573)
XLA Ops:
  0.6 3.5 %collective-permute-start = (bf16[2,2048,128]{2,1,0:T(8,128)(2,1)}, bf16[2,2048,128]{2,1,0:T(8,128)(2,1)S(1)}, u32[]{:S(2)}, u32[]{:S(2)}) collective-permute-start(bf16[2,2048,128]{2,1,0:T(8,128)(2,1)} %bitcast.14), channel_id=1, source_target_pairs={{0,1},{1,0},{2,3},{3,2},{4,5},{5,4},{6,7},{7,6},{8,9},{9,8},{10,11... | collective-permute-start | bytes 3145736 | tf_op jit(solution)/shard_map/prefix/ppermute | solution.py:37
  4.2 6.2 %project.1 = (f32[4,256,128]{2,1,0:T(8,128)}, bf16[4,256,128]{2,1,0:T(8,128)(2,1)}, bf16[4,256,128]{2,1,0:T(8,128)(2,1)}, bf16[4,256,128]{2,1,0:T(8,128)(2,1)}) custom-call(s32[1]{0:T(128)} %bitcast.1.member_ref, bf16[256,512]{1,0:T(8,128)(2,1)} %bitcast.20, bf16[512,2048]{1,0:T(8,128)(2,1)} %w_hbm.1), custom_call_target="tpu_custom_call" | custom-call | flops 536870912 | bytes 4194304 | tf_op jit(solution)/shard_map/project/pallas_call | solution.py:69
  10.4 2.5 %collective-permute-start.1 = (bf16[4,256,128]{2,1,0:T(8,128)(2,1)}, bf16[4,256,128]{2,1,0:T(8,128)(2,1)S(1)}, u32[]{:S(2)}, u32[]{:S(2)}) collective-permute-start(bf16[4,256,128]{2,1,0:T(8,128)(2,1)} %get-tuple-element.19.refs_0_), channel_id=1, source_target_pairs={{0,1},{1,0},{2,3},{3,2},{4,5},{5,4},{6,7},{7,6},{8,9},{9,8},{10,11... | collective-permute-start | bytes 786440 | tf_op jit(solution)/shard_map/sum_x/ppermute | solution.py:37
  12.8 4.9 %collective-permute-start.2 = (bf16[4,256,128]{2,1,0:T(8,128)(2,1)}, bf16[4,256,128]{2,1,0:T(8,128)(2,1)S(1)}, u32[]{:S(2)}, u32[]{:S(2)}) collective-permute-start(bf16[4,256,128]{2,1,0:T(8,128)(2,1)} %get-tuple-element.20), channel_id=1, source_target_pairs={{0,2},{1,3},{2,0},{3,1},{4,6},{5,7},{6,4},{7,5},{8,10},{9,11},{10,... | collective-permute-start | bytes 786440 | tf_op jit(solution)/shard_map/sum_x/ppermute | solution.py:37
  17.8 3.0 %collective-permute-start.3 = (bf16[4,256,128]{2,1,0:T(8,128)(2,1)}, bf16[4,256,128]{2,1,0:T(8,128)(2,1)S(1)}, u32[]{:S(2)}, u32[]{:S(2)}) collective-permute-start(bf16[4,256,128]{2,1,0:T(8,128)(2,1)} %get-tuple-element.21), channel_id=1, source_target_pairs={{0,3},{1,2},{2,1},{3,0},{4,7},{5,6},{6,5},{7,4},{8,11},{9,10},{10,... | collective-permute-start | bytes 786440 | tf_op jit(solution)/shard_map/sum_x/ppermute | solution.py:37
  21.5 0.5 fusion.2
  22.2 1.0 copy-done.4
  23.3 0.9 copy-done.6
  24.2 3.1 %own_half.2 = (f32[256,1024]{1,0:T(8,128)S(1)}, f32[256,256]{1,0:T(8,128)S(1)}) custom-call(s32[1]{0:T(128)} %bitcast.10.length_ref, s32[1]{0:T(128)} %bitcast.1.member_ref, bf16[256,1024]{1,0:T(8,128)(2,1)S(1)} %bitcast.17, bf16[2,2048,128]{2,1,0:T(8,128)(2,1)S(1)} %bitcast.15, bf16[4,256,128]{2,1,0:T(8,128)(2,1)S(1)} %copy-done.6), custom_call_target="tpu_custom_call" | custom-call | flops 2147483648 | bytes 2097152 | tf_op jit(solution)/shard_map/own_half/pallas_call | solution.py:251
  27.3 7.2 %collective-permute-done.1.a_ref = bf16[4,256,128]{2,1,0:T(8,128)(2,1)S(1)} collective-permute-done((bf16[4,256,128]{2,1,0:T(8,128)(2,1)}, bf16[4,256,128]{2,1,0:T(8,128)(2,1)S(1)}, u32[]{:S(2)}, u32[]{:S(2)}) %collective-permute-start.1) | collective-permute-done | bytes 262176 | tf_op jit(solution)/shard_map/sum_x/ppermute | solution.py:37
  34.5 6.7 %collective-permute-done.2.b_ref = bf16[4,256,128]{2,1,0:T(8,128)(2,1)S(1)} collective-permute-done((bf16[4,256,128]{2,1,0:T(8,128)(2,1)}, bf16[4,256,128]{2,1,0:T(8,128)(2,1)S(1)}, u32[]{:S(2)}, u32[]{:S(2)}) %collective-permute-start.2) | collective-permute-done | bytes 262176 | tf_op jit(solution)/shard_map/sum_x/ppermute | solution.py:37
  41.4 9.1 %collective-permute-start.4 = (bf16[256,128]{1,0:T(8,128)(2,1)S(1)}, bf16[256,128]{1,0:T(8,128)(2,1)S(1)}, u32[]{:S(2)}, u32[]{:S(2)}) collective-permute-start(bf16[256,128]{1,0:T(8,128)(2,1)S(1)} %get-tuple-element.23.refs_0_), channel_id=1, source_target_pairs={{0,4},{1,5},{2,6},{3,7},{4,0},{5,1},{6,2},{7,3},{8,12},{9,13},{10,... | collective-permute-start | bytes 196616 | tf_op jit(solution)/shard_map/sum_z/ppermute | solution.py:37
  50.5 10.0 %collective-permute-start.5 = (bf16[256,128]{1,0:T(8,128)(2,1)S(1)}, bf16[256,128]{1,0:T(8,128)(2,1)S(1)}, u32[]{:S(2)}, u32[]{:S(2)}) collective-permute-start(bf16[256,128]{1,0:T(8,128)(2,1)S(1)} %get-tuple-element.28), channel_id=1, source_target_pairs={{0,8},{1,9},{2,10},{3,11},{4,12},{5,13},{6,14},{7,15},{8,0},{9,1},... | collective-permute-start | bytes 196616 | tf_op jit(solution)/shard_map/sum_z/ppermute | solution.py:37
  60.5 1.9 %collective-permute-start.6 = (bf16[256,128]{1,0:T(8,128)(2,1)S(1)}, bf16[256,128]{1,0:T(8,128)(2,1)S(1)}, u32[]{:S(2)}, u32[]{:S(2)}) collective-permute-start(bf16[256,128]{1,0:T(8,128)(2,1)S(1)} %get-tuple-element.29), channel_id=1, source_target_pairs={{0,12},{1,13},{2,14},{3,15},{4,8},{5,9},{6,10},{7,11},{8,4},{9,5},... | collective-permute-start | bytes 196616 | tf_op jit(solution)/shard_map/sum_z/ppermute | solution.py:37
  62.4 3.1 %own_half.3 = (f32[256,1024]{1,0:T(8,128)S(1)}, f32[256,256]{1,0:T(8,128)S(1)}) custom-call(s32[1]{0:T(128)} %bitcast.11.length_ref, s32[1]{0:T(128)} %bitcast.1.member_ref, bf16[256,1024]{1,0:T(8,128)(2,1)S(1)} %bitcast.18, bf16[2,2048,128]{2,1,0:T(8,128)(2,1)S(1)} %bitcast.16, ...), custom_call_target="tpu_custom_call", output_to_operand_aliasing={{0}: (5, {}), {1}: (6, {})} | custom-call | flops 2147483648 | bytes 2097152 | tf_op jit(solution)/shard_map/own_half/pallas_call | solution.py:251
  65.6 1.0 copy-done.7
  66.5 4.8 %collective-permute-done.6.c_ref = bf16[256,128]{1,0:T(8,128)(2,1)S(1)} collective-permute-done((bf16[256,128]{1,0:T(8,128)(2,1)S(1)}, bf16[256,128]{1,0:T(8,128)(2,1)S(1)}, u32[]{:S(2)}, u32[]{:S(2)}) %collective-permute-start.6) | collective-permute-done | bytes 65568 | tf_op jit(solution)/shard_map/sum_z/ppermute | solution.py:37
  71.5 3.5 %collective-permute-start.10 = (bf16[256,128]{1,0:T(8,128)(2,1)S(1)}, bf16[256,128]{1,0:T(8,128)(2,1)S(1)}, u32[]{:S(2)}, u32[]{:S(2)}) collective-permute-start(bf16[256,128]{1,0:T(8,128)(2,1)S(1)} %finish.1.refs_0_.mine_ref.own_ref), channel_id=1, source_target_pairs={{0,48},{16,32},{32,16},{48,0},{64,112},{80,96},{96,80},{112,64},{1... | collective-permute-start | bytes 196616 | tf_op jit(solution)/shard_map/handoff_y/ppermute | solution.py:41
  75.0 3.8 %collective-permute-start.8 = (bf16[256,128]{1,0:T(8,128)(2,1)S(1)}, bf16[256,128]{1,0:T(8,128)(2,1)S(1)}, u32[]{:S(2)}, u32[]{:S(2)}) collective-permute-start(bf16[256,128]{1,0:T(8,128)(2,1)S(1)} %finish.1.refs_0_.mine_ref.own_ref), channel_id=1, source_target_pairs={{0,16},{16,0},{32,48},{48,32},{64,80},{80,64},{96,112},{112,96},{1... | collective-permute-start | bytes 196616 | tf_op jit(solution)/shard_map/handoff_y/ppermute | solution.py:41
  78.8 1.9 %collective-permute-start.9 = (bf16[256,128]{1,0:T(8,128)(2,1)S(1)}, bf16[256,128]{1,0:T(8,128)(2,1)S(1)}, u32[]{:S(2)}, u32[]{:S(2)}) collective-permute-start(bf16[256,128]{1,0:T(8,128)(2,1)S(1)} %finish.1.refs_0_.mine_ref.own_ref), channel_id=1, source_target_pairs={{0,32},{16,48},{32,0},{48,16},{64,96},{80,112},{96,64},{112,80},{1... | collective-permute-start | bytes 196616 | tf_op jit(solution)/shard_map/handoff_y/ppermute | solution.py:41
  80.7 2.1 %collective-permute-start.7 = (bf16[256,128]{1,0:T(8,128)(2,1)S(1)}, bf16[256,128]{1,0:T(8,128)(2,1)S(1)}, u32[]{:S(2)}, u32[]{:S(2)}) collective-permute-start(bf16[256,128]{1,0:T(8,128)(2,1)S(1)} %finish.1.refs_0_.mine_ref.own_ref), channel_id=1, source_target_pairs={{0,1},{1,0},{2,3},{3,2},{4,5},{5,4},{6,7},{7,6},{8,9},{9,8},{10,11... | collective-permute-start | bytes 196616 | tf_op jit(solution)/shard_map/pair/ppermute | solution.py:37
  82.9 3.6 %collective-permute-done.9.refs_2_ = bf16[256,128]{1,0:T(8,128)(2,1)S(1)} collective-permute-done((bf16[256,128]{1,0:T(8,128)(2,1)S(1)}, bf16[256,128]{1,0:T(8,128)(2,1)S(1)}, u32[]{:S(2)}, u32[]{:S(2)}) %collective-permute-start.9) | collective-permute-done | bytes 65568 | tf_op jit(solution)/shard_map/handoff_y/ppermute | solution.py:41
  86.4 0.7 offer.1
  87.1 1.3 %collective-permute-start.11 = (bf16[256,128]{1,0:T(8,128)(2,1)S(1)}, bf16[256,128]{1,0:T(8,128)(2,1)S(1)}, u32[]{:S(2)}, u32[]{:S(2)}) collective-permute-start(bf16[256,128]{1,0:T(8,128)(2,1)S(1)} %get-tuple-element.30.after_ref), channel_id=1, source_target_pairs={{0,256},{16,272},{32,288},{48,304},{64,320},{80,336},{96,352},{112... | collective-permute-start | bytes 196616 | tf_op jit(solution)/shard_map/handoff_z/ppermute | solution.py:41
  88.4 1.3 %collective-permute-start.12 = (bf16[256,128]{1,0:T(8,128)(2,1)S(1)}, bf16[256,128]{1,0:T(8,128)(2,1)S(1)}, u32[]{:S(2)}, u32[]{:S(2)}) collective-permute-start(bf16[256,128]{1,0:T(8,128)(2,1)S(1)} %get-tuple-element.31), channel_id=1, source_target_pairs={{0,320},{16,336},{32,352},{48,368},{64,256},{80,272},{96,288},{112... | collective-permute-start | bytes 196616 | tf_op jit(solution)/shard_map/handoff_z/ppermute | solution.py:41
  89.7 1.3 %collective-permute-start.13 = (bf16[256,128]{1,0:T(8,128)(2,1)S(1)}, bf16[256,128]{1,0:T(8,128)(2,1)S(1)}, u32[]{:S(2)}, u32[]{:S(2)}) collective-permute-start(bf16[256,128]{1,0:T(8,128)(2,1)S(1)} %get-tuple-element.32), channel_id=1, source_target_pairs={{0,384},{16,400},{32,416},{48,432},{64,448},{80,464},{96,480},{112... | collective-permute-start | bytes 196616 | tf_op jit(solution)/shard_map/handoff_z/ppermute | solution.py:41
  91.0 1.5 %collective-permute-start.14 = (bf16[256,128]{1,0:T(8,128)(2,1)S(1)}, bf16[256,128]{1,0:T(8,128)(2,1)S(1)}, u32[]{:S(2)}, u32[]{:S(2)}) collective-permute-start(bf16[256,128]{1,0:T(8,128)(2,1)S(1)} %get-tuple-element.33), channel_id=1, source_target_pairs={{0,448},{16,464},{32,480},{48,496},{64,384},{80,400},{96,416},{112... | collective-permute-start | bytes 196616 | tf_op jit(solution)/shard_map/handoff_z/ppermute | solution.py:41
  92.5 1.0 copy-done.5
  93.6 1.2 %copy-done.8 = f32[256,1024]{1,0:T(8,128)S(1)} copy-done((f32[256,1024]{1,0:T(8,128)S(1)}, f32[256,1024]{1,0:T(8,128)}, u32[]{:S(2)}) %copy-start.8) | copy-done | bytes 1048600
  94.8 13.9 %other_half.1.refs_4_ = bf16[256,1024]{1,0:T(8,128)(2,1)} custom-call(s32[1]{0:T(128)} %bitcast.12.length_ref, s32[1]{0:T(128)} %bitcast.1.member_ref, bf16[256,1024]{1,0:T(8,128)(2,1)S(1)} %bitcast.19, bf16[2,2048,128]{2,1,0:T(8,128)(2,1)S(1)} %collective-permute-done.kv_ref, f32[256,1024]{1,0:T(8,128)S(1)} %copy-done.8, ...), custom_call_target="tpu_custom_call" | custom-call | flops 4831838208 | bytes 3145728 | tf_op jit(solution)/shard_map/other_half/pallas_call | solution.py:321
  108.7 1.0 copy-done.1
  109.7 1.2 %take.1 = bf16[256,128]{1,0:T(8,128)(2,1)} custom-call(s32[16]{0:T(128)S(1)} %copy-done.2, s32[1]{0:T(128)} %bitcast.6.inst_ref, s32[1]{0:T(128)} %bitcast.8.role_ref, bf16[256,128]{1,0:T(8,128)(2,1)S(1)} %finish.1.refs_0_.mine_ref.own_ref, bf16[256,128]{1,0:T(8,128)(2,1)S(1)} %collective-permute-done.11.refs_0_, ...), custom_call_target="tpu_custom_call" | custom-call | tf_op jit(solution)/shard_map/take/pallas_call | solution.py:169
  (28 shorter events, 0.5 us)
Async XLA Ops:
  0.6 21.6 %copy-start.3 = (bf16[1,1,1,2,2048,128]{5,4,3,2,1,0:T(8,128)(2,1)S(1)}, bf16[1,1,1,2,2048,128]{5,4,3,2,1,0:T(8,128)(2,1)}, u32[]{:S(2)}) copy-start(bf16[1,1,1,2,2048,128]{5,4,3,2,1,0:T(8,128)(2,1)} %param.8) | copy-start | bytes 3145732
  0.6 91.9 %collective-permute-start = (bf16[2,2048,128]{2,1,0:T(8,128)(2,1)}, bf16[2,2048,128]{2,1,0:T(8,128)(2,1)S(1)}, u32[]{:S(2)}, u32[]{:S(2)}) collective-permute-start(bf16[2,2048,128]{2,1,0:T(8,128)(2,1)} %bitcast.14), channel_id=1, source_target_pairs={{0,1},{1,0},{2,3},{3,2},{4,5},{5,4},{6,7},{7,6},{8,9},{9,8},{10,11... | collective-permute-start | bytes 3145736 | tf_op jit(solution)/shard_map/prefix/ppermute | solution.py:37
  10.4 24.2 %collective-permute-start.1 = (bf16[4,256,128]{2,1,0:T(8,128)(2,1)}, bf16[4,256,128]{2,1,0:T(8,128)(2,1)S(1)}, u32[]{:S(2)}, u32[]{:S(2)}) collective-permute-start(bf16[4,256,128]{2,1,0:T(8,128)(2,1)} %get-tuple-element.19.refs_0_), channel_id=1, source_target_pairs={{0,1},{1,0},{2,3},{3,2},{4,5},{5,4},{6,7},{7,6},{8,9},{9,8},{10,11... | collective-permute-start | bytes 786440 | tf_op jit(solution)/shard_map/sum_x/ppermute | solution.py:37
  12.8 28.4 %collective-permute-start.2 = (bf16[4,256,128]{2,1,0:T(8,128)(2,1)}, bf16[4,256,128]{2,1,0:T(8,128)(2,1)S(1)}, u32[]{:S(2)}, u32[]{:S(2)}) collective-permute-start(bf16[4,256,128]{2,1,0:T(8,128)(2,1)} %get-tuple-element.20), channel_id=1, source_target_pairs={{0,2},{1,3},{2,0},{3,1},{4,6},{5,7},{6,4},{7,5},{8,10},{9,11},{10,... | collective-permute-start | bytes 786440 | tf_op jit(solution)/shard_map/sum_x/ppermute | solution.py:37
  17.8 23.4 %collective-permute-start.3 = (bf16[4,256,128]{2,1,0:T(8,128)(2,1)}, bf16[4,256,128]{2,1,0:T(8,128)(2,1)S(1)}, u32[]{:S(2)}, u32[]{:S(2)}) collective-permute-start(bf16[4,256,128]{2,1,0:T(8,128)(2,1)} %get-tuple-element.21), channel_id=1, source_target_pairs={{0,3},{1,2},{2,1},{3,0},{4,7},{5,6},{6,5},{7,4},{8,11},{9,10},{10,... | collective-permute-start | bytes 786440 | tf_op jit(solution)/shard_map/sum_x/ppermute | solution.py:37
  22.2 1.0 copy-start.4
  23.3 0.9 copy-start.6
  24.2 17.0 %copy-start = (f32[4,256,128]{2,1,0:T(8,128)S(1)}, f32[4,256,128]{2,1,0:T(8,128)}, u32[]{:S(2)}) copy-start(f32[4,256,128]{2,1,0:T(8,128)} %get-tuple-element.18.own_ref) | copy-start | bytes 1572868
  41.4 25.2 %collective-permute-start.4 = (bf16[256,128]{1,0:T(8,128)(2,1)S(1)}, bf16[256,128]{1,0:T(8,128)(2,1)S(1)}, u32[]{:S(2)}, u32[]{:S(2)}) collective-permute-start(bf16[256,128]{1,0:T(8,128)(2,1)S(1)} %get-tuple-element.23.refs_0_), channel_id=1, source_target_pairs={{0,4},{1,5},{2,6},{3,7},{4,0},{5,1},{6,2},{7,3},{8,12},{9,13},{10,... | collective-permute-start | bytes 196616 | tf_op jit(solution)/shard_map/sum_z/ppermute | solution.py:37
  50.5 16.1 %collective-permute-start.5 = (bf16[256,128]{1,0:T(8,128)(2,1)S(1)}, bf16[256,128]{1,0:T(8,128)(2,1)S(1)}, u32[]{:S(2)}, u32[]{:S(2)}) collective-permute-start(bf16[256,128]{1,0:T(8,128)(2,1)S(1)} %get-tuple-element.28), channel_id=1, source_target_pairs={{0,8},{1,9},{2,10},{3,11},{4,12},{5,13},{6,14},{7,15},{8,0},{9,1},... | collective-permute-start | bytes 196616 | tf_op jit(solution)/shard_map/sum_z/ppermute | solution.py:37
  60.5 10.9 %collective-permute-start.6 = (bf16[256,128]{1,0:T(8,128)(2,1)S(1)}, bf16[256,128]{1,0:T(8,128)(2,1)S(1)}, u32[]{:S(2)}, u32[]{:S(2)}) collective-permute-start(bf16[256,128]{1,0:T(8,128)(2,1)S(1)} %get-tuple-element.29), channel_id=1, source_target_pairs={{0,12},{1,13},{2,14},{3,15},{4,8},{5,9},{6,10},{7,11},{8,4},{9,5},... | collective-permute-start | bytes 196616 | tf_op jit(solution)/shard_map/sum_z/ppermute | solution.py:37
  62.4 24.0 %copy-start.2 = (s32[16]{0:T(128)S(1)}, s32[16]{0:T(128)}, u32[]{:S(2)}) copy-start(s32[16]{0:T(128)} %pairing_ref.3) | copy-start | bytes 196
  65.5 1.0 copy-start.7
  71.5 11.4 %collective-permute-start.10 = (bf16[256,128]{1,0:T(8,128)(2,1)S(1)}, bf16[256,128]{1,0:T(8,128)(2,1)S(1)}, u32[]{:S(2)}, u32[]{:S(2)}) collective-permute-start(bf16[256,128]{1,0:T(8,128)(2,1)S(1)} %finish.1.refs_0_.mine_ref.own_ref), channel_id=1, source_target_pairs={{0,48},{16,32},{32,16},{48,0},{64,112},{80,96},{96,80},{112,64},{1... | collective-permute-start | bytes 196616 | tf_op jit(solution)/shard_map/handoff_y/ppermute | solution.py:41
  75.0 7.9 %collective-permute-start.8 = (bf16[256,128]{1,0:T(8,128)(2,1)S(1)}, bf16[256,128]{1,0:T(8,128)(2,1)S(1)}, u32[]{:S(2)}, u32[]{:S(2)}) collective-permute-start(bf16[256,128]{1,0:T(8,128)(2,1)S(1)} %finish.1.refs_0_.mine_ref.own_ref), channel_id=1, source_target_pairs={{0,16},{16,0},{32,48},{48,32},{64,80},{80,64},{96,112},{112,96},{1... | collective-permute-start | bytes 196616 | tf_op jit(solution)/shard_map/handoff_y/ppermute | solution.py:41
  78.8 7.7 %collective-permute-start.9 = (bf16[256,128]{1,0:T(8,128)(2,1)S(1)}, bf16[256,128]{1,0:T(8,128)(2,1)S(1)}, u32[]{:S(2)}, u32[]{:S(2)}) collective-permute-start(bf16[256,128]{1,0:T(8,128)(2,1)S(1)} %finish.1.refs_0_.mine_ref.own_ref), channel_id=1, source_target_pairs={{0,32},{16,48},{32,0},{48,16},{64,96},{80,112},{96,64},{112,80},{1... | collective-permute-start | bytes 196616 | tf_op jit(solution)/shard_map/handoff_y/ppermute | solution.py:41
  80.7 10.3 %collective-permute-start.7 = (bf16[256,128]{1,0:T(8,128)(2,1)S(1)}, bf16[256,128]{1,0:T(8,128)(2,1)S(1)}, u32[]{:S(2)}, u32[]{:S(2)}) collective-permute-start(bf16[256,128]{1,0:T(8,128)(2,1)S(1)} %finish.1.refs_0_.mine_ref.own_ref), channel_id=1, source_target_pairs={{0,1},{1,0},{2,3},{3,2},{4,5},{5,4},{6,7},{7,6},{8,9},{9,8},{10,11... | collective-permute-start | bytes 196616 | tf_op jit(solution)/shard_map/pair/ppermute | solution.py:37
  87.1 21.5 %collective-permute-start.11 = (bf16[256,128]{1,0:T(8,128)(2,1)S(1)}, bf16[256,128]{1,0:T(8,128)(2,1)S(1)}, u32[]{:S(2)}, u32[]{:S(2)}) collective-permute-start(bf16[256,128]{1,0:T(8,128)(2,1)S(1)} %get-tuple-element.30.after_ref), channel_id=1, source_target_pairs={{0,256},{16,272},{32,288},{48,304},{64,320},{80,336},{96,352},{112... | collective-permute-start | bytes 196616 | tf_op jit(solution)/shard_map/handoff_z/ppermute | solution.py:41
  88.4 20.2 %collective-permute-start.12 = (bf16[256,128]{1,0:T(8,128)(2,1)S(1)}, bf16[256,128]{1,0:T(8,128)(2,1)S(1)}, u32[]{:S(2)}, u32[]{:S(2)}) collective-permute-start(bf16[256,128]{1,0:T(8,128)(2,1)S(1)} %get-tuple-element.31), channel_id=1, source_target_pairs={{0,320},{16,336},{32,352},{48,368},{64,256},{80,272},{96,288},{112... | collective-permute-start | bytes 196616 | tf_op jit(solution)/shard_map/handoff_z/ppermute | solution.py:41
  89.7 18.9 %collective-permute-start.13 = (bf16[256,128]{1,0:T(8,128)(2,1)S(1)}, bf16[256,128]{1,0:T(8,128)(2,1)S(1)}, u32[]{:S(2)}, u32[]{:S(2)}) collective-permute-start(bf16[256,128]{1,0:T(8,128)(2,1)S(1)} %get-tuple-element.32), channel_id=1, source_target_pairs={{0,384},{16,400},{32,416},{48,432},{64,448},{80,464},{96,480},{112... | collective-permute-start | bytes 196616 | tf_op jit(solution)/shard_map/handoff_z/ppermute | solution.py:41
  91.0 17.6 %collective-permute-start.14 = (bf16[256,128]{1,0:T(8,128)(2,1)S(1)}, bf16[256,128]{1,0:T(8,128)(2,1)S(1)}, u32[]{:S(2)}, u32[]{:S(2)}) collective-permute-start(bf16[256,128]{1,0:T(8,128)(2,1)S(1)} %get-tuple-element.33), channel_id=1, source_target_pairs={{0,448},{16,464},{32,480},{48,496},{64,384},{80,400},{96,416},{112... | collective-permute-start | bytes 196616 | tf_op jit(solution)/shard_map/handoff_z/ppermute | solution.py:41
  92.5 1.0 copy-start.5
  93.6 1.2 %copy-start.8 = (f32[256,1024]{1,0:T(8,128)S(1)}, f32[256,1024]{1,0:T(8,128)}, u32[]{:S(2)}) copy-start(f32[256,1024]{1,0:T(8,128)} %copy-done.7) | copy-start | bytes 3145732
  108.7 1.0 copy-start.1

commit v3 on v2

v3 whole, which is shorter than its diff:
```python
import functools
import math

import jax
import jax.numpy as jnp
from jax import lax
from jax.experimental import pallas as pl
from jax.experimental.pallas import tpu as pltpu
from jax.sharding import PartitionSpec as P

BLOCK = 128
HD = 128
TOK = 256
HALF = 2048
HEADS = 8
STEP_HEADS = 4
SUB = 512
FEATURES = 512
W_PARTS = 4
LOW = -1e30
SCALE = HD**-0.5 * math.log2(math.e)

SMEM = pl.BlockSpec(memory_space=pltpu.SMEM)
VMEM = pl.BlockSpec(memory_space=pltpu.VMEM)
HBM = pl.BlockSpec(memory_space=pltpu.HBM)
ANY = pl.BlockSpec(memory_space=pl.ANY)


def params(mib):
    return pltpu.CompilerParams(vmem_limit_bytes=mib * 1024 * 1024)


def struct(shape, dtype):
    return jax.ShapeDtypeStruct(shape, dtype)


TOKEN = struct((8, HD), jnp.float32)


def in_hbm(array):
    return pltpu.with_memory_space_constraint(array, pltpu.HBM)


def swap_tp(array, mask):
    return lax.ppermute(array, "tp", [(i, i ^ mask) for i in range(16)])


def role_inst(array, pairs):
    return lax.ppermute(array, ("role", "inst"), pairs)


def project_kernel(member_ref, hidden_hbm, w_hbm, own_ref, *rest):
    send_refs, token_ref, (hidden_ref, w_ref, sems) = rest[:3], rest[3], rest[4:]
    member = member_ref[0]
    rows = FEATURES // W_PARTS
    copies = [pltpu.make_async_copy(hidden_hbm, hidden_ref, sems.at[W_PARTS])]
    for part in range(W_PARTS):
        span = pl.ds(part * rows, rows)
        copies.append(pltpu.make_async_copy(w_hbm.at[span], w_ref.at[span], sems.at[part]))
    for copy in copies:
        copy.start()
    for copy in copies:
        copy.wait()
    for j in (2, 3, 1, 0):
        for k in range(4):
            column = pl.multiple_of((member ^ (4 * k + j)) * HD, HD)
            part = jnp.dot(
                hidden_ref[...], w_ref[:, pl.ds(column, HD)], preferred_element_type=jnp.float32
            )
            if j == 0:
                own_ref[k] = part
            else:
                send_refs[j - 1][k] = part.astype(jnp.bfloat16)
    token_ref[...] = jnp.zeros_like(token_ref)


def project(member, hidden, w_kv):
    return pl.pallas_call(
        project_kernel,
        out_shape=[struct((4, TOK, HD), jnp.float32)]
        + [struct((4, TOK, HD), jnp.bfloat16)] * 3
        + [TOKEN],
        in_specs=[SMEM, ANY, ANY],
        out_specs=[VMEM] * 5,
        scratch_shapes=[
            pltpu.VMEM((TOK, FEATURES), jnp.bfloat16),
            pltpu.VMEM((FEATURES, 2048), jnp.bfloat16),
            pltpu.SemaphoreType.DMA((W_PARTS + 1,)),
        ],
        compiler_params=params(12),
        cost_estimate=pl.CostEstimate(
            flops=2 * TOK * FEATURES * 2048, bytes_accessed=4 << 20, transcendentals=0
        ),
        name="project",
    )(member, in_hbm(hidden), in_hbm(w_kv))


def sum_x_kernel(own_ref, a_ref, b_ref, c_ref, after_ref, cache_ref, keep_ref, *refs):
    send_refs, (cache_out, sem) = refs[:3], refs[3:]
    copy = pltpu.make_async_copy(cache_ref, cache_out, sem)
    copy.start()
    for k in range(4):
        total = own_ref[k] + a_ref[k].astype(jnp.float32)
        total = total + b_ref[k].astype(jnp.float32) + c_ref[k].astype(jnp.float32)
        if k == 0:
            keep_ref[...] = total
        else:
            send_refs[k - 1][...] = total.astype(jnp.bfloat16)
    copy.wait()


def sum_x(own, arrived, after, cache):
    return pl.pallas_call(
        sum_x_kernel,
        out_shape=[struct((TOK, HD), jnp.float32)]
        + [struct((TOK, HD), jnp.bfloat16)] * 3
        + [struct(cache.shape, cache.dtype)],
        in_specs=[VMEM] * 5 + [ANY],
        out_specs=[VMEM] * 4 + [ANY],
        scratch_shapes=[pltpu.SemaphoreType.DMA],
        compiler_params=params(8),
        name="sum_x",
    )(own, *arrived, after, cache)


def finish_kernel(keep_ref, a_ref, b_ref, c_ref, cosine_ref, sine_ref, out_ref):
    total = keep_ref[...] + a_ref[...].astype(jnp.float32)
    total = total + b_ref[...].astype(jnp.float32) + c_ref[...].astype(jnp.float32)
    turned = pltpu.roll(total, HD // 2, 1)
    out_ref[...] = (total * cosine_ref[...] + turned * sine_ref[...]).astype(jnp.bfloat16)


def finish(keep, arrived, cosine, sine):
    return pl.pallas_call(
        finish_kernel,
        out_shape=struct((TOK, HD), jnp.bfloat16),
        in_specs=[VMEM] * 6,
        out_specs=VMEM,
        compiler_params=params(8),
        name="finish",
    )(keep, *arrived, cosine, sine)


def source_of(pairing_ref, target):
    source = jnp.int32(0)
    for i in range(16):
        source = jnp.where(pairing_ref[i] == target, i, source)
    return source


def choose(index, refs):
    block = refs[0][...]
    for at in range(1, len(refs)):
        block = jnp.where(index == at, refs[at][...], block)
    return block


def offer_kernel(pairing_ref, inst_ref, *refs):
    column, outs = refs[:4], refs[4:]
    inst = inst_ref[0]
    for j in range(4):
        source = source_of(pairing_ref, inst ^ (4 * j))
        outs[j][...] = choose((source ^ inst) & 3, column)


def offer(pairing, inst, column):
    return pl.pallas_call(
        offer_kernel,
        out_shape=[struct((TOK, HD), jnp.bfloat16)] * 4,
        in_specs=[SMEM] * 2 + [VMEM] * 4,
        out_specs=[VMEM] * 4,
        compiler_params=params(8),
        name="offer",
    )(pairing, inst, *column)


def dot_rows(a, b):
    return lax.dot_general(a, b, (((1,), (1,)), ((), ())), preferred_element_type=jnp.float32)


def load_cache(valid, kv_ref, keys, values):
    inside = lax.broadcasted_iota(jnp.int32, (HALF, HD), 0) < valid
    rows = kv_ref[0]
    keys[...] = jnp.where(inside, rows, jnp.broadcast_to(rows[:1], rows.shape))
    values[:, :HD] = jnp.where(inside, kv_ref[1], 0)
    values[:, HD:] = jnp.where(inside, 1.0, 0.0).astype(jnp.bfloat16)


def update(top, ext, scores, values):
    peak = jnp.max(scores, axis=1, keepdims=True) * SCALE
    if top is not None:
        peak = jnp.maximum(top, peak)
    weights = jnp.exp2(scores * SCALE - peak).astype(jnp.bfloat16)
    term = jnp.dot(weights, values, preferred_element_type=jnp.float32)
    if top is not None:
        term = ext * jnp.exp2(top - peak) + term
    return peak, term


def over_cache(top, ext, queried, keys, values):
    for at in range(0, HALF, SUB):
        scores = dot_rows(queried, keys[at : at + SUB, :])
        top, ext = update(top, ext, scores, values[at : at + SUB, :])
    return top, ext


def valid_slots(length_ref, member_ref):
    limit = length_ref[0] * BLOCK
    low = jnp.minimum(limit, HALF)
    is_key = member_ref[0] % 2 == 0
    return jnp.where(is_key, low, limit - low), jnp.where(is_key, limit - low, low), is_key


def own_half_kernel(
    length_ref, member_ref, q_ref, kv_ref, after_ref, acc_ref, stat_ref, token_ref, keys, values
):
    token_ref[...] = after_ref[...]
    valid, _, _ = valid_slots(length_ref, member_ref)
    lane = lax.broadcasted_iota(jnp.int32, (TOK, HD), 1)

    @pl.when((valid > 0) & (pl.program_id(0) == 0))
    def prepare():
        load_cache(valid, kv_ref, keys, values)

    @pl.when(valid > 0)
    def some():
        stats = jnp.zeros((TOK, HD), jnp.float32)
        for at in range(STEP_HEADS):
            span = slice(at * HD, (at + 1) * HD)
            top, ext = over_cache(None, None, q_ref[:, span], keys, values)
            acc_ref[:, span] = ext[:, :HD]
            stats = jnp.where(lane == at, jnp.broadcast_to(top, (TOK, HD)), stats)
            stats = jnp.where(lane == at + STEP_HEADS, ext[:, HD:], stats)
        stat_ref[...] = stats

    @pl.when(valid <= 0)
    def none():
        acc_ref[...] = jnp.zeros_like(acc_ref)
        stat_ref[...] = jnp.where(lane < STEP_HEADS, LOW, 0.0)


HEADS_SPEC = pl.BlockSpec((TOK, STEP_HEADS * HD), lambda g: (0, g))
STAT_SPEC = pl.BlockSpec((TOK, HD), lambda g: (0, g))
CACHE_SPEC = pl.BlockSpec((2, HALF, HD), lambda g: (0, 0, 0))
ROWS_SPEC = pl.BlockSpec((TOK, HD), lambda g: (0, 0))
TOKEN_SPEC = pl.BlockSpec((8, HD), lambda g: (0, 0))


def own_half(length, member, queries, cache, after):
    groups = HEADS // STEP_HEADS
    return pl.pallas_call(
        own_half_kernel,
        grid=(groups,),
        out_shape=[
            pltpu.HBM((TOK, HEADS * HD), jnp.float32),
            pltpu.HBM((TOK, groups * HD), jnp.float32),
            TOKEN,
        ],
        in_specs=[SMEM, SMEM, HEADS_SPEC, CACHE_SPEC, TOKEN_SPEC],
        out_specs=[HEADS_SPEC, STAT_SPEC, TOKEN_SPEC],
        scratch_shapes=[
            pltpu.VMEM((HALF, HD), jnp.bfloat16),
            pltpu.VMEM((HALF, 2 * HD), jnp.bfloat16),
        ],
        compiler_params=params(16),
        cost_estimate=pl.CostEstimate(
            flops=8 * TOK * HEADS * HALF * HD,
            bytes_accessed=2 << 20,
            transcendentals=TOK * HEADS * HALF,
        ),
        name="own_half",
    )(length, member, in_hbm(queries), in_hbm(cache), after)


def other_half_kernel(
    length_ref, member_ref, pairing_ref, inst_ref, role_ref, q_ref, kv_ref, acc_ref, stat_ref,
    mine_ref, theirs_ref, *refs,
):
    offers, (out_ref, layer_ref, keys, values, new_keys, new_values) = refs[:4], refs[4:]
    _, valid, is_key = valid_slots(length_ref, member_ref)

    @pl.when(pl.program_id(0) == 0)
    def prepare():
        inst = inst_ref[0]
        handed = choose((source_of(pairing_ref, inst) ^ inst) // 4, offers)
        layer_ref[...] = jnp.where(role_ref[0] == 1, handed, mine_ref[...])
        load_cache(valid, kv_ref, keys, values)
        new_keys[...] = jnp.where(is_key, mine_ref[...], theirs_ref[...])
        new_values[:, :HD] = jnp.where(is_key, theirs_ref[...], mine_ref[...])
        new_values[:, HD:] = jnp.ones((TOK, HD), jnp.bfloat16)

    def run(with_cache):
        row = lax.broadcasted_iota(jnp.int32, (TOK, TOK), 0)
        column = lax.broadcasted_iota(jnp.int32, (TOK, TOK), 1)
        for at in range(STEP_HEADS):
            span = slice(at * HD, (at + 1) * HD)
            queried = q_ref[:, span]
            scores = jnp.where(column <= row, dot_rows(queried, new_keys[...]), LOW)
            top, ext = update(None, None, scores, new_values[...])
            if with_cache:
                top, ext = over_cache(top, ext, queried, keys, values)
            own_top = stat_ref[:, at : at + 1]
            own_total = stat_ref[:, at + STEP_HEADS : at + STEP_HEADS + 1]
            peak = jnp.maximum(top, own_top)
            scale, own_scale = jnp.exp2(top - peak), jnp.exp2(own_top - peak)
            total = ext[:, HD:] * scale + own_total * own_scale
            out = ext[:, :HD] * scale + acc_ref[:, span] * own_scale
            out_ref[:, span] = (out / total).astype(jnp.bfloat16)

    pl.when(valid > 0)(lambda: run(True))
    pl.when(valid <= 0)(lambda: run(False))


def other_half(length, member, pairing, inst, role, queries, cache, state, mine, theirs, offers):
    return pl.pallas_call(
        other_half_kernel,
        grid=(HEADS // STEP_HEADS,),
        out_shape=[
            struct((TOK, HEADS * HD), jnp.bfloat16),
            struct((TOK, HD), jnp.bfloat16),
        ],
        in_specs=[SMEM] * 5
        + [HEADS_SPEC, CACHE_SPEC, HEADS_SPEC, STAT_SPEC]
        + [ROWS_SPEC] * 6,
        out_specs=[HEADS_SPEC, ROWS_SPEC],
        scratch_shapes=[
            pltpu.VMEM((HALF, HD), jnp.bfloat16),
            pltpu.VMEM((HALF, 2 * HD), jnp.bfloat16),
            pltpu.VMEM((TOK, HD), jnp.bfloat16),
            pltpu.VMEM((TOK, 2 * HD), jnp.bfloat16),
        ],
        compiler_params=params(24),
        cost_estimate=pl.CostEstimate(
            flops=8 * TOK * HEADS * (HALF + TOK) * HD,
            bytes_accessed=3 << 20,
            transcendentals=TOK * HEADS * (HALF + TOK),
        ),
        name="other_half",
    )(
        length, member, pairing, inst, role, in_hbm(queries), cache,
        in_hbm(state[0]), in_hbm(state[1]), mine, theirs, *offers,
    )


def rotation(length, is_key):
    half = HD // 2
    positions = (length * BLOCK + jnp.arange(TOK)).astype(jnp.float32)
    frequency = jnp.exp(jnp.arange(half).astype(jnp.float32) * (-2.0 * math.log(500000.0) / HD))
    angles = positions[:, None] * frequency[None, :]
    cosine = jnp.where(is_key, jnp.cos(angles), 1.0)
    sine = jnp.where(is_key, jnp.sin(angles), 0.0)
    return jnp.concatenate([cosine, cosine], 1), jnp.concatenate([-sine, sine], 1)


def per_device(hidden, queries, prefix_cache, lengths, pairing, w_kv):
    member = lax.axis_index("tp").astype(jnp.int32)
    inst = lax.axis_index("inst").astype(jnp.int32).reshape(1)
    role = lax.axis_index("role").astype(jnp.int32).reshape(1)
    length = lengths.reshape(1)
    resident = prefix_cache[0, 0, 0]
    queried = queries[0, 0]
    cosine, sine = rotation(lengths[0, 0], member % 2 == 0)
    member = member.reshape(1)

    own, *sends, token = project(member, hidden[0, 0], w_kv)
    with jax.named_scope("sum_x"):
        arrived = [swap_tp(sends[j - 1], j) for j in (1, 2, 3)]
    *state, token = own_half(length, member, queried, resident, token)
    keep, *sends, resend = sum_x(own, arrived, token, resident)
    with jax.named_scope("prefix"):
        across = swap_tp(resend, 1)
    with jax.named_scope("sum_z"):
        arrived = [swap_tp(sends[k - 1], 4 * k) for k in (1, 2, 3)]
    own_kv = finish(keep, arrived, cosine, sine)

    with jax.named_scope("handoff_y"):
        column = [own_kv] + [
            role_inst(own_kv, [(i, i ^ j) for i in range(16)]) for j in (1, 2, 3)
        ]
    with jax.named_scope("pair"):
        other_kv = swap_tp(own_kv, 1)
    offers = offer(pairing, inst, column)
    with jax.named_scope("handoff_z"):
        offered = [
            role_inst(offers[j], [(i, 16 + (i ^ (4 * j))) for i in range(16)]) for j in range(4)
        ]
    attended, layer_kv = other_half(
        length, member, pairing, inst, role, queried, across, state, own_kv, other_kv, offered
    )
    return attended[None, None], layer_kv[None, None]


def solution(mesh):
    in_specs = (
        P("role", "inst", None, "tp"),
        P("role", "inst", None, "tp"),
        P("role", "inst", "tp", None, None, None),
        P("role", "inst"),
        P(),
        P("tp", None),
    )
    out_specs = (P("role", "inst", None, "tp"), P("role", "inst", None, "tp"))
    return jax.shard_map(
        per_device, mesh=mesh, in_specs=in_specs, out_specs=out_specs, check_vma=False
    )
```

time: 112 us -> 100 us (0.89)
  the two profiles are of different devices: /device:TPU:40 before, /device:TPU:3 now
where the time goes in v3:
time: 100 us; the launch traced here: 99.9 us
  starting transfers between devices  44.8 us (45%)
  waiting for transfers between devices  35.5 us (36%)
  Pallas kernels  17.4 us (17%)
  between operations  1.54 us (2%)
    ppermute x8, starting transfers between devices, swap_tp(): return lax.ppermute(array, 'tp', [(i, i ^ mask) for i in range(16)])  37.5 us
    ppermute x8, waiting for transfers between devices, swap_tp(): return lax.ppermute(array, 'tp', [(i, i ^ mask) for i in range(16)])  18.1 us
    ppermute x7, waiting for transfers between devices, role_inst(): return lax.ppermute(array, ('role', 'inst'), pairs)  17.4 us
    pallas_call x1, Pallas kernels, other_half(): pl.pallas_call(other_half_kernel, grid=(HEADS // STEP_HEADS,), out_shape=...  10.9 us
    ppermute x7, starting transfers between devices, role_inst(): return lax.ppermute(array, ('role', 'inst'), pairs)  7.34 us
    pallas_call x1, Pallas kernels, project(): pl.pallas_call(project_kernel, out_shape=[struct((4, TOK, HD), jnp.float3...  2.97 us
    pallas_call x1, Pallas kernels, own_half(): pl.pallas_call(own_half_kernel, grid=(groups,), out_shape=[pltpu.HBM((TOK...  2.54 us
  transfers between devices with their start and end apart: 15, of which 8 were waited for; matrix products, arithmetic and copies ran while one was open for 1% of the time, Pallas kernels for 3%

profile of v3, /device:TPU:3, one launch (start us, length us, event | category | flops | bytes accessed | tf_op | source)
XLA Modules:
  0.0 99.9 jit_solution(6647707373422826823)
XLA Ops:
  0.6 3.0 %project.1 = (f32[4,256,128]{2,1,0:T(8,128)S(1)}, bf16[4,256,128]{2,1,0:T(8,128)(2,1)S(1)}, bf16[4,256,128]{2,1,0:T(8,128)(2,1)S(1)}, bf16[4,256,128]{2,1,0:T(8,128)(2,1)S(1)}, f32[8,128]{1,0:T(8,128)S(1)}) custom-call(s32[1]{0:T(128)} %bitcast.1.member_ref, bf16[256,512]{1,0:T(8,128)(2,1)} %bitcast.14, bf16[512,2048]{1,0:T(8,128)(2,1)} %w_hbm.1), custom_call_target="tpu_custom_call" | custom-call | flops 536870912 | bytes 4194304 | tf_op jit(solution)/shard_map/project/pallas_call | solution.py:78
  3.6 1.9 %collective-permute-start = (bf16[4,256,128]{2,1,0:T(8,128)(2,1)S(1)}, bf16[4,256,128]{2,1,0:T(8,128)(2,1)S(1)}, u32[]{:S(2)}, u32[]{:S(2)}) collective-permute-start(bf16[4,256,128]{2,1,0:T(8,128)(2,1)S(1)} %get-tuple-element.22), channel_id=1, source_target_pairs={{0,1},{1,0},{2,3},{3,2},{4,5},{5,4},{6,7},{7,6},{8,9},{9,8},{10,11... | collective-permute-start | bytes 786440 | tf_op jit(solution)/shard_map/sum_x/ppermute | solution.py:45
  5.5 4.3 %collective-permute-start.1 = (bf16[4,256,128]{2,1,0:T(8,128)(2,1)S(1)}, bf16[4,256,128]{2,1,0:T(8,128)(2,1)S(1)}, u32[]{:S(2)}, u32[]{:S(2)}) collective-permute-start(bf16[4,256,128]{2,1,0:T(8,128)(2,1)S(1)} %get-tuple-element.23), channel_id=1, source_target_pairs={{0,2},{1,3},{2,0},{3,1},{4,6},{5,7},{6,4},{7,5},{8,10},{9,11},{10,... | collective-permute-start | bytes 786440 | tf_op jit(solution)/shard_map/sum_x/ppermute | solution.py:45
  9.8 2.2 %collective-permute-start.2 = (bf16[4,256,128]{2,1,0:T(8,128)(2,1)S(1)}, bf16[4,256,128]{2,1,0:T(8,128)(2,1)S(1)}, u32[]{:S(2)}, u32[]{:S(2)}) collective-permute-start(bf16[4,256,128]{2,1,0:T(8,128)(2,1)S(1)} %get-tuple-element.24), channel_id=1, source_target_pairs={{0,3},{1,2},{2,1},{3,0},{4,7},{5,6},{6,5},{7,4},{8,11},{9,10},{10,... | collective-permute-start | bytes 786440 | tf_op jit(solution)/shard_map/sum_x/ppermute | solution.py:45
  12.7 0.0 copy-start
  12.7 2.5 %own_half.1 = (f32[256,1024]{1,0:T(8,128)}, f32[256,256]{1,0:T(8,128)}, f32[8,128]{1,0:T(8,128)S(1)}) custom-call(s32[1]{0:T(128)} %bitcast.10.length_ref, s32[1]{0:T(128)} %bitcast.1.member_ref, bf16[256,1024]{1,0:T(8,128)(2,1)} %bitcast.15, bf16[2,2048,128]{2,1,0:T(8,128)(2,1)} %bitcast.12, f32[8,128]{1,0:T(8,128)S(1)} %get-tuple-element.25.after_ref), custom_call_target="tpu_custom_call" | custom-call | flops 4294967296 | bytes 2097152 | tf_op jit(solution)/shard_map/own_half/pallas_call | solution.py:251
  15.2 2.2 %collective-permute-done.1.b_ref = bf16[4,256,128]{2,1,0:T(8,128)(2,1)S(1)} collective-permute-done((bf16[4,256,128]{2,1,0:T(8,128)(2,1)S(1)}, bf16[4,256,128]{2,1,0:T(8,128)(2,1)S(1)}, u32[]{:S(2)}, u32[]{:S(2)}) %collective-permute-start.1) | collective-permute-done | bytes 262176 | tf_op jit(solution)/shard_map/sum_x/ppermute | solution.py:45
  17.4 5.9 %collective-permute-done.2.c_ref = bf16[4,256,128]{2,1,0:T(8,128)(2,1)S(1)} collective-permute-done((bf16[4,256,128]{2,1,0:T(8,128)(2,1)S(1)}, bf16[4,256,128]{2,1,0:T(8,128)(2,1)S(1)}, u32[]{:S(2)}, u32[]{:S(2)}) %collective-permute-start.2) | collective-permute-done | bytes 262176 | tf_op jit(solution)/shard_map/sum_x/ppermute | solution.py:45
  23.2 0.2 sum_x.1
  23.4 5.8 %collective-permute-start.3 = (bf16[2,2048,128]{2,1,0:T(8,128)(2,1)S(1)}, bf16[2,2048,128]{2,1,0:T(8,128)(2,1)S(1)}, u32[]{:S(2)}, u32[]{:S(2)}) collective-permute-start(bf16[2,2048,128]{2,1,0:T(8,128)(2,1)S(1)} %get-tuple-element.27), channel_id=1, source_target_pairs={{0,1},{1,0},{2,3},{3,2},{4,5},{5,4},{6,7},{7,6},{8,9},{9,8},{10,11... | collective-permute-start | bytes 3145736 | tf_op jit(solution)/shard_map/prefix/ppermute | solution.py:45
  29.3 0.5 fusion.2
  29.9 8.8 %collective-permute-start.4 = (bf16[256,128]{1,0:T(8,128)(2,1)S(1)}, bf16[256,128]{1,0:T(8,128)(2,1)S(1)}, u32[]{:S(2)}, u32[]{:S(2)}) collective-permute-start(bf16[256,128]{1,0:T(8,128)(2,1)S(1)} %get-tuple-element.31), channel_id=1, source_target_pairs={{0,4},{1,5},{2,6},{3,7},{4,0},{5,1},{6,2},{7,3},{8,12},{9,13},{10,... | collective-permute-start | bytes 196616 | tf_op jit(solution)/shard_map/sum_z/ppermute | solution.py:45
  38.7 10.6 %collective-permute-start.5 = (bf16[256,128]{1,0:T(8,128)(2,1)S(1)}, bf16[256,128]{1,0:T(8,128)(2,1)S(1)}, u32[]{:S(2)}, u32[]{:S(2)}) collective-permute-start(bf16[256,128]{1,0:T(8,128)(2,1)S(1)} %get-tuple-element.32), channel_id=1, source_target_pairs={{0,8},{1,9},{2,10},{3,11},{4,12},{5,13},{6,14},{7,15},{8,0},{9,1},... | collective-permute-start | bytes 196616 | tf_op jit(solution)/shard_map/sum_z/ppermute | solution.py:45
  49.3 1.9 %collective-permute-start.6 = (bf16[256,128]{1,0:T(8,128)(2,1)S(1)}, bf16[256,128]{1,0:T(8,128)(2,1)S(1)}, u32[]{:S(2)}, u32[]{:S(2)}) collective-permute-start(bf16[256,128]{1,0:T(8,128)(2,1)S(1)} %get-tuple-element.33), channel_id=1, source_target_pairs={{0,12},{1,13},{2,14},{3,15},{4,8},{5,9},{6,10},{7,11},{8,4},{9,5},... | collective-permute-start | bytes 196616 | tf_op jit(solution)/shard_map/sum_z/ppermute | solution.py:45
  51.3 0.1 pad_maximum_fusion
  51.4 1.1 %collective-permute-done.5.b_ref = bf16[256,128]{1,0:T(8,128)(2,1)S(1)} collective-permute-done((bf16[256,128]{1,0:T(8,128)(2,1)S(1)}, bf16[256,128]{1,0:T(8,128)(2,1)S(1)}, u32[]{:S(2)}, u32[]{:S(2)}) %collective-permute-start.5) | collective-permute-done | bytes 65568 | tf_op jit(solution)/shard_map/sum_z/ppermute | solution.py:45
  52.5 9.0 %collective-permute-done.6.c_ref = bf16[256,128]{1,0:T(8,128)(2,1)S(1)} collective-permute-done((bf16[256,128]{1,0:T(8,128)(2,1)S(1)}, bf16[256,128]{1,0:T(8,128)(2,1)S(1)}, u32[]{:S(2)}, u32[]{:S(2)}) %collective-permute-start.6) | collective-permute-done | bytes 65568 | tf_op jit(solution)/shard_map/sum_z/ppermute | solution.py:45
  61.5 0.1 finish.1.refs_0_.mine_ref
  61.6 0.7 collective-permute-start.8
  62.3 0.7 collective-permute-start.9
  62.9 0.7 collective-permute-start.10
  63.6 1.9 %collective-permute-start.7 = (bf16[256,128]{1,0:T(8,128)(2,1)S(1)}, bf16[256,128]{1,0:T(8,128)(2,1)S(1)}, u32[]{:S(2)}, u32[]{:S(2)}) collective-permute-start(bf16[256,128]{1,0:T(8,128)(2,1)S(1)} %finish.1.refs_0_.mine_ref), channel_id=1, source_target_pairs={{0,1},{1,0},{2,3},{3,2},{4,5},{5,4},{6,7},{7,6},{8,9},{9,8},{10,11... | collective-permute-start | bytes 196616 | tf_op jit(solution)/shard_map/pair/ppermute | solution.py:45
  65.6 0.7 offer.1
  66.3 1.3 %collective-permute-start.11 = (bf16[256,128]{1,0:T(8,128)(2,1)S(1)}, bf16[256,128]{1,0:T(8,128)(2,1)S(1)}, u32[]{:S(2)}, u32[]{:S(2)}) collective-permute-start(bf16[256,128]{1,0:T(8,128)(2,1)S(1)} %get-tuple-element.34), channel_id=1, source_target_pairs={{0,256},{16,272},{32,288},{48,304},{64,320},{80,336},{96,352},{112... | collective-permute-start | bytes 196616 | tf_op jit(solution)/shard_map/handoff_z/ppermute | solution.py:49
  67.6 1.3 %collective-permute-start.12 = (bf16[256,128]{1,0:T(8,128)(2,1)S(1)}, bf16[256,128]{1,0:T(8,128)(2,1)S(1)}, u32[]{:S(2)}, u32[]{:S(2)}) collective-permute-start(bf16[256,128]{1,0:T(8,128)(2,1)S(1)} %get-tuple-element.35), channel_id=1, source_target_pairs={{0,320},{16,336},{32,352},{48,368},{64,256},{80,272},{96,288},{112... | collective-permute-start | bytes 196616 | tf_op jit(solution)/shard_map/handoff_z/ppermute | solution.py:49
  68.9 1.3 %collective-permute-start.13 = (bf16[256,128]{1,0:T(8,128)(2,1)S(1)}, bf16[256,128]{1,0:T(8,128)(2,1)S(1)}, u32[]{:S(2)}, u32[]{:S(2)}) collective-permute-start(bf16[256,128]{1,0:T(8,128)(2,1)S(1)} %get-tuple-element.36), channel_id=1, source_target_pairs={{0,384},{16,400},{32,416},{48,432},{64,448},{80,464},{96,480},{112... | collective-permute-start | bytes 196616 | tf_op jit(solution)/shard_map/handoff_z/ppermute | solution.py:49
  70.2 1.5 %collective-permute-start.14 = (bf16[256,128]{1,0:T(8,128)(2,1)S(1)}, bf16[256,128]{1,0:T(8,128)(2,1)S(1)}, u32[]{:S(2)}, u32[]{:S(2)}) collective-permute-start(bf16[256,128]{1,0:T(8,128)(2,1)S(1)} %get-tuple-element.37), channel_id=1, source_target_pairs={{0,448},{16,464},{32,480},{48,496},{64,384},{80,400},{96,416},{112... | collective-permute-start | bytes 196616 | tf_op jit(solution)/shard_map/handoff_z/ppermute | solution.py:49
  71.7 8.9 %collective-permute-done.11.refs_0_ = bf16[256,128]{1,0:T(8,128)(2,1)S(1)} collective-permute-done((bf16[256,128]{1,0:T(8,128)(2,1)S(1)}, bf16[256,128]{1,0:T(8,128)(2,1)S(1)}, u32[]{:S(2)}, u32[]{:S(2)}) %collective-permute-start.11) | collective-permute-done | bytes 65568 | tf_op jit(solution)/shard_map/handoff_z/ppermute | solution.py:49
  80.6 3.4 %collective-permute-done.12.refs_1_ = bf16[256,128]{1,0:T(8,128)(2,1)S(1)} collective-permute-done((bf16[256,128]{1,0:T(8,128)(2,1)S(1)}, bf16[256,128]{1,0:T(8,128)(2,1)S(1)}, u32[]{:S(2)}, u32[]{:S(2)}) %collective-permute-start.12) | collective-permute-done | bytes 65568 | tf_op jit(solution)/shard_map/handoff_z/ppermute | solution.py:49
  84.0 2.3 %collective-permute-done.13.refs_2_ = bf16[256,128]{1,0:T(8,128)(2,1)S(1)} collective-permute-done((bf16[256,128]{1,0:T(8,128)(2,1)S(1)}, bf16[256,128]{1,0:T(8,128)(2,1)S(1)}, u32[]{:S(2)}, u32[]{:S(2)}) %collective-permute-start.13) | collective-permute-done | bytes 65568 | tf_op jit(solution)/shard_map/handoff_z/ppermute | solution.py:49
  86.3 2.8 %collective-permute-done.14.refs_3_ = bf16[256,128]{1,0:T(8,128)(2,1)S(1)} collective-permute-done((bf16[256,128]{1,0:T(8,128)(2,1)S(1)}, bf16[256,128]{1,0:T(8,128)(2,1)S(1)}, u32[]{:S(2)}, u32[]{:S(2)}) %collective-permute-start.14) | collective-permute-done | bytes 65568 | tf_op jit(solution)/shard_map/handoff_z/ppermute | solution.py:49
  89.0 10.9 %other_half.1 = (bf16[256,1024]{1,0:T(8,128)(2,1)}, bf16[256,128]{1,0:T(8,128)(2,1)}) custom-call(s32[1]{0:T(128)} %bitcast.11.length_ref, s32[1]{0:T(128)} %bitcast.1.member_ref, s32[16]{0:T(128)S(1)} %copy-done.1, s32[1]{0:T(128)} %bitcast.2.inst_ref, s32[1]{0:T(128)} %bitcast.3.role_ref, bf16[256,1024]{1,0:T(8,128)(2,1)} %bitcast.16, ...), custom_call_target="tpu_custom_call" | custom-call | flops 4831838208 | bytes 3145728 | tf_op jit(solution)/shard_map/other_half/pallas_call | solution.py:315
  (12 shorter events, 0.0 us)
Async XLA Ops:
  3.6 11.6 %collective-permute-start = (bf16[4,256,128]{2,1,0:T(8,128)(2,1)S(1)}, bf16[4,256,128]{2,1,0:T(8,128)(2,1)S(1)}, u32[]{:S(2)}, u32[]{:S(2)}) collective-permute-start(bf16[4,256,128]{2,1,0:T(8,128)(2,1)S(1)} %get-tuple-element.22), channel_id=1, source_target_pairs={{0,1},{1,0},{2,3},{3,2},{4,5},{5,4},{6,7},{7,6},{8,9},{9,8},{10,11... | collective-permute-start | bytes 786440 | tf_op jit(solution)/shard_map/sum_x/ppermute | solution.py:45
  5.5 11.8 %collective-permute-start.1 = (bf16[4,256,128]{2,1,0:T(8,128)(2,1)S(1)}, bf16[4,256,128]{2,1,0:T(8,128)(2,1)S(1)}, u32[]{:S(2)}, u32[]{:S(2)}) collective-permute-start(bf16[4,256,128]{2,1,0:T(8,128)(2,1)S(1)} %get-tuple-element.23), channel_id=1, source_target_pairs={{0,2},{1,3},{2,0},{3,1},{4,6},{5,7},{6,4},{7,5},{8,10},{9,11},{10,... | collective-permute-start | bytes 786440 | tf_op jit(solution)/shard_map/sum_x/ppermute | solution.py:45
  9.8 13.4 %collective-permute-start.2 = (bf16[4,256,128]{2,1,0:T(8,128)(2,1)S(1)}, bf16[4,256,128]{2,1,0:T(8,128)(2,1)S(1)}, u32[]{:S(2)}, u32[]{:S(2)}) collective-permute-start(bf16[4,256,128]{2,1,0:T(8,128)(2,1)S(1)} %get-tuple-element.24), channel_id=1, source_target_pairs={{0,3},{1,2},{2,1},{3,0},{4,7},{5,6},{6,5},{7,4},{8,11},{9,10},{10,... | collective-permute-start | bytes 786440 | tf_op jit(solution)/shard_map/sum_x/ppermute | solution.py:45
  12.7 10.6 %copy-start = (bf16[1,1,1,2,2048,128]{5,4,3,2,1,0:T(8,128)(2,1)S(1)}, bf16[1,1,1,2,2048,128]{5,4,3,2,1,0:T(8,128)(2,1)}, u32[]{:S(2)}) copy-start(bf16[1,1,1,2,2048,128]{5,4,3,2,1,0:T(8,128)(2,1)} %param.8) | copy-start | bytes 3145732
  15.2 50.4 %copy-start.1 = (s32[16]{0:T(128)S(1)}, s32[16]{0:T(128)}, u32[]{:S(2)}) copy-start(s32[16]{0:T(128)} %pairing_ref.3) | copy-start | bytes 196
  23.4 65.6 %collective-permute-start.3 = (bf16[2,2048,128]{2,1,0:T(8,128)(2,1)S(1)}, bf16[2,2048,128]{2,1,0:T(8,128)(2,1)S(1)}, u32[]{:S(2)}, u32[]{:S(2)}) collective-permute-start(bf16[2,2048,128]{2,1,0:T(8,128)(2,1)S(1)} %get-tuple-element.27), channel_id=1, source_target_pairs={{0,1},{1,0},{2,3},{3,2},{4,5},{5,4},{6,7},{7,6},{8,9},{9,8},{10,11... | collective-permute-start | bytes 3145736 | tf_op jit(solution)/shard_map/prefix/ppermute | solution.py:45
  29.9 21.5 %collective-permute-start.4 = (bf16[256,128]{1,0:T(8,128)(2,1)S(1)}, bf16[256,128]{1,0:T(8,128)(2,1)S(1)}, u32[]{:S(2)}, u32[]{:S(2)}) collective-permute-start(bf16[256,128]{1,0:T(8,128)(2,1)S(1)} %get-tuple-element.31), channel_id=1, source_target_pairs={{0,4},{1,5},{2,6},{3,7},{4,0},{5,1},{6,2},{7,3},{8,12},{9,13},{10,... | collective-permute-start | bytes 196616 | tf_op jit(solution)/shard_map/sum_z/ppermute | solution.py:45
  38.7 13.8 %collective-permute-start.5 = (bf16[256,128]{1,0:T(8,128)(2,1)S(1)}, bf16[256,128]{1,0:T(8,128)(2,1)S(1)}, u32[]{:S(2)}, u32[]{:S(2)}) collective-permute-start(bf16[256,128]{1,0:T(8,128)(2,1)S(1)} %get-tuple-element.32), channel_id=1, source_target_pairs={{0,8},{1,9},{2,10},{3,11},{4,12},{5,13},{6,14},{7,15},{8,0},{9,1},... | collective-permute-start | bytes 196616 | tf_op jit(solution)/shard_map/sum_z/ppermute | solution.py:45
  49.3 12.1 %collective-permute-start.6 = (bf16[256,128]{1,0:T(8,128)(2,1)S(1)}, bf16[256,128]{1,0:T(8,128)(2,1)S(1)}, u32[]{:S(2)}, u32[]{:S(2)}) collective-permute-start(bf16[256,128]{1,0:T(8,128)(2,1)S(1)} %get-tuple-element.33), channel_id=1, source_target_pairs={{0,12},{1,13},{2,14},{3,15},{4,8},{5,9},{6,10},{7,11},{8,4},{9,5},... | collective-permute-start | bytes 196616 | tf_op jit(solution)/shard_map/sum_z/ppermute | solution.py:45
  61.6 4.0 %collective-permute-start.8 = (bf16[256,128]{1,0:T(8,128)(2,1)S(1)}, bf16[256,128]{1,0:T(8,128)(2,1)S(1)}, u32[]{:S(2)}, u32[]{:S(2)}) collective-permute-start(bf16[256,128]{1,0:T(8,128)(2,1)S(1)} %finish.1.refs_0_.mine_ref), channel_id=1, source_target_pairs={{0,16},{16,0},{32,48},{48,32},{64,80},{80,64},{96,112},{112,96},{1... | collective-permute-start | bytes 196616 | tf_op jit(solution)/shard_map/handoff_y/ppermute | solution.py:49
  62.3 3.3 %collective-permute-start.9 = (bf16[256,128]{1,0:T(8,128)(2,1)S(1)}, bf16[256,128]{1,0:T(8,128)(2,1)S(1)}, u32[]{:S(2)}, u32[]{:S(2)}) collective-permute-start(bf16[256,128]{1,0:T(8,128)(2,1)S(1)} %finish.1.refs_0_.mine_ref), channel_id=1, source_target_pairs={{0,32},{16,48},{32,0},{48,16},{64,96},{80,112},{96,64},{112,80},{1... | collective-permute-start | bytes 196616 | tf_op jit(solution)/shard_map/handoff_y/ppermute | solution.py:49
  62.9 2.6 %collective-permute-start.10 = (bf16[256,128]{1,0:T(8,128)(2,1)S(1)}, bf16[256,128]{1,0:T(8,128)(2,1)S(1)}, u32[]{:S(2)}, u32[]{:S(2)}) collective-permute-start(bf16[256,128]{1,0:T(8,128)(2,1)S(1)} %finish.1.refs_0_.mine_ref), channel_id=1, source_target_pairs={{0,48},{16,32},{32,16},{48,0},{64,112},{80,96},{96,80},{112,64},{1... | collective-permute-start | bytes 196616 | tf_op jit(solution)/shard_map/handoff_y/ppermute | solution.py:49
  63.6 6.6 %collective-permute-start.7 = (bf16[256,128]{1,0:T(8,128)(2,1)S(1)}, bf16[256,128]{1,0:T(8,128)(2,1)S(1)}, u32[]{:S(2)}, u32[]{:S(2)}) collective-permute-start(bf16[256,128]{1,0:T(8,128)(2,1)S(1)} %finish.1.refs_0_.mine_ref), channel_id=1, source_target_pairs={{0,1},{1,0},{2,3},{3,2},{4,5},{5,4},{6,7},{7,6},{8,9},{9,8},{10,11... | collective-permute-start | bytes 196616 | tf_op jit(solution)/shard_map/pair/ppermute | solution.py:45
  66.3 14.3 %collective-permute-start.11 = (bf16[256,128]{1,0:T(8,128)(2,1)S(1)}, bf16[256,128]{1,0:T(8,128)(2,1)S(1)}, u32[]{:S(2)}, u32[]{:S(2)}) collective-permute-start(bf16[256,128]{1,0:T(8,128)(2,1)S(1)} %get-tuple-element.34), channel_id=1, source_target_pairs={{0,256},{16,272},{32,288},{48,304},{64,320},{80,336},{96,352},{112... | collective-permute-start | bytes 196616 | tf_op jit(solution)/shard_map/handoff_z/ppermute | solution.py:49
  67.6 16.4 %collective-permute-start.12 = (bf16[256,128]{1,0:T(8,128)(2,1)S(1)}, bf16[256,128]{1,0:T(8,128)(2,1)S(1)}, u32[]{:S(2)}, u32[]{:S(2)}) collective-permute-start(bf16[256,128]{1,0:T(8,128)(2,1)S(1)} %get-tuple-element.35), channel_id=1, source_target_pairs={{0,320},{16,336},{32,352},{48,368},{64,256},{80,272},{96,288},{112... | collective-permute-start | bytes 196616 | tf_op jit(solution)/shard_map/handoff_z/ppermute | solution.py:49
  68.9 17.4 %collective-permute-start.13 = (bf16[256,128]{1,0:T(8,128)(2,1)S(1)}, bf16[256,128]{1,0:T(8,128)(2,1)S(1)}, u32[]{:S(2)}, u32[]{:S(2)}) collective-permute-start(bf16[256,128]{1,0:T(8,128)(2,1)S(1)} %get-tuple-element.36), channel_id=1, source_target_pairs={{0,384},{16,400},{32,416},{48,432},{64,448},{80,464},{96,480},{112... | collective-permute-start | bytes 196616 | tf_op jit(solution)/shard_map/handoff_z/ppermute | solution.py:49
  70.2 18.9 %collective-permute-start.14 = (bf16[256,128]{1,0:T(8,128)(2,1)S(1)}, bf16[256,128]{1,0:T(8,128)(2,1)S(1)}, u32[]{:S(2)}, u32[]{:S(2)}) collective-permute-start(bf16[256,128]{1,0:T(8,128)(2,1)S(1)} %get-tuple-element.37), channel_id=1, source_target_pairs={{0,448},{16,464},{32,480},{48,496},{64,384},{80,400},{96,416},{112... | collective-permute-start | bytes 196616 | tf_op jit(solution)/shard_map/handoff_z/ppermute | solution.py:49

commit v4 on v3

v4 whole, which is shorter than its diff:
```python
import functools
import math

import jax
import jax.numpy as jnp
from jax import lax
from jax.experimental import pallas as pl
from jax.experimental.pallas import tpu as pltpu
from jax.sharding import PartitionSpec as P

BLOCK = 128
HD = 128
TOK = 256
HALF = 2048
HEADS = 8
STEP_HEADS = 4
SUB = 512
FEATURES = 512
LOW = -1e30
X_GROUPS = [[z * 4 + x for x in range(4)] for z in range(4)]
Y_GROUPS = [[zl * 4 + y for y in range(4)] for zl in range(4)]
Z_GROUPS = [[z * 4 + x for z in range(4)] for x in range(4)]
SCALE = HD**-0.5 * math.log2(math.e)

SMEM = pl.BlockSpec(memory_space=pltpu.SMEM)
VMEM = pl.BlockSpec(memory_space=pltpu.VMEM)
HBM = pl.BlockSpec(memory_space=pltpu.HBM)
ANY = pl.BlockSpec(memory_space=pl.ANY)


def params(mib):
    return pltpu.CompilerParams(vmem_limit_bytes=mib * 1024 * 1024)


def struct(shape, dtype):
    return jax.ShapeDtypeStruct(shape, dtype)


TOKEN = struct((8, HD), jnp.float32)


def in_hbm(array):
    return pltpu.with_memory_space_constraint(array, pltpu.HBM)


def swap_tp(array, mask):
    return lax.ppermute(array, "tp", [(i, i ^ mask) for i in range(16)])


def exchange_tp(array, groups):
    return lax.all_to_all(array, "tp", 0, 0, axis_index_groups=groups, tiled=True)


def role_inst(array, pairs):
    return lax.ppermute(array, ("role", "inst"), pairs)


def project_kernel(member_ref, hidden_hbm, w_hbm, send_ref, token_ref, hidden_ref, w_ref, sems):
    zh = member_ref[0] // 4
    width = 4 * HD
    copies = [pltpu.make_async_copy(hidden_hbm, hidden_ref, sems.at[4])]
    for k in range(4):
        column = pl.multiple_of((zh ^ k) * width, width)
        copies.append(
            pltpu.make_async_copy(w_hbm.at[:, pl.ds(column, width)], w_ref.at[k], sems.at[k])
        )
    for copy in copies:
        copy.start()
    copies[0].wait()
    token_ref[...] = jnp.zeros_like(token_ref)
    for k in range(4):
        copies[k + 1].wait()
        part = jnp.dot(hidden_ref[...], w_ref[k], preferred_element_type=jnp.float32)
        for x in range(4):
            send_ref[x, k] = part[:, x * HD : (x + 1) * HD].astype(jnp.bfloat16)


def project(member, hidden, w_kv):
    return pl.pallas_call(
        project_kernel,
        out_shape=[struct((4, 4, TOK, HD), jnp.bfloat16), TOKEN],
        in_specs=[SMEM, ANY, ANY],
        out_specs=[VMEM] * 2,
        scratch_shapes=[
            pltpu.VMEM((TOK, FEATURES), jnp.bfloat16),
            pltpu.VMEM((4, FEATURES, 4 * HD), jnp.bfloat16),
            pltpu.SemaphoreType.DMA((5,)),
        ],
        compiler_params=params(12),
        cost_estimate=pl.CostEstimate(
            flops=2 * TOK * FEATURES * 2048, bytes_accessed=4 << 20, transcendentals=0
        ),
        name="project",
    )(member, in_hbm(hidden), in_hbm(w_kv))


def sum_x_kernel(member_ref, parts_ref, after_ref, keep_ref, send_ref, token_ref):
    token_ref[...] = after_ref[...]
    zh = member_ref[0] // 4
    for k in range(4):
        total = parts_ref[0, k].astype(jnp.float32)
        for x in (1, 2, 3):
            total = total + parts_ref[x, k].astype(jnp.float32)
        if k == 0:
            keep_ref[...] = total
        send_ref[zh ^ k] = total.astype(jnp.bfloat16)


def sum_x(member, parts, after):
    return pl.pallas_call(
        sum_x_kernel,
        out_shape=[
            struct((TOK, HD), jnp.float32),
            struct((4, TOK, HD), jnp.bfloat16),
            TOKEN,
        ],
        in_specs=[SMEM] + [VMEM] * 2,
        out_specs=[VMEM] * 3,
        compiler_params=params(10),
        name="sum_x",
    )(member, parts, after)


def finish_kernel(member_ref, keep_ref, parts_ref, cosine_ref, sine_ref, after_ref, out_ref, send_ref):
    zh = member_ref[0] // 4
    total = keep_ref[...]
    for k in (1, 2, 3):
        total = total + parts_ref[zh ^ k].astype(jnp.float32)
    turned = pltpu.roll(total, HD // 2, 1)
    done = (total * cosine_ref[...] + turned * sine_ref[...]).astype(jnp.bfloat16)
    out_ref[...] = done
    for at in range(4):
        send_ref[at] = done


def finish(member, keep, parts, cosine, sine, after):
    return pl.pallas_call(
        finish_kernel,
        out_shape=[struct((TOK, HD), jnp.bfloat16), struct((4, TOK, HD), jnp.bfloat16)],
        in_specs=[SMEM] + [VMEM] * 5,
        out_specs=[VMEM] * 2,
        compiler_params=params(8),
        name="finish",
    )(member, keep, parts, cosine, sine, after)


def source_of(pairing_ref, target):
    source = jnp.int32(0)
    for i in range(16):
        source = jnp.where(pairing_ref[i] == target, i, source)
    return source


def choose(index, refs):
    block = refs[0][...]
    for at in range(1, len(refs)):
        block = jnp.where(index == at, refs[at][...], block)
    return block


def offer_kernel(pairing_ref, inst_ref, *refs):
    column, outs = refs[0], refs[1:]
    inst = inst_ref[0]
    for j in range(4):
        source = source_of(pairing_ref, inst ^ (4 * j))
        outs[j][...] = column[source & 3]


def offer(pairing, inst, column):
    return pl.pallas_call(
        offer_kernel,
        out_shape=[struct((TOK, HD), jnp.bfloat16)] * 4,
        in_specs=[SMEM] * 2 + [VMEM],
        out_specs=[VMEM] * 4,
        compiler_params=params(8),
        name="offer",
    )(pairing, inst, column)


def take_kernel(pairing_ref, inst_ref, role_ref, own_ref, *refs):
    offers, out_ref = refs[:4], refs[5]
    inst = inst_ref[0]
    handed = choose((source_of(pairing_ref, inst) ^ inst) // 4, offers)
    out_ref[...] = jnp.where(role_ref[0] == 1, handed, own_ref[...])


def take(pairing, inst, role, own_kv, offers, after):
    return pl.pallas_call(
        take_kernel,
        out_shape=struct((TOK, HD), jnp.bfloat16),
        in_specs=[SMEM] * 3 + [VMEM] * 6,
        out_specs=VMEM,
        compiler_params=params(8),
        name="take",
    )(pairing, inst, role, own_kv, *offers, after)


def dot_rows(a, b):
    return lax.dot_general(a, b, (((1,), (1,)), ((), ())), preferred_element_type=jnp.float32)


def load_cache(valid, kv_ref, keys, values):
    inside = lax.broadcasted_iota(jnp.int32, keys.shape, 0) < valid
    rows = kv_ref[0]
    keys[...] = jnp.where(inside, rows, jnp.broadcast_to(rows[:1], rows.shape))
    values[:, :HD] = jnp.where(inside, kv_ref[1], 0)
    values[:, HD:] = jnp.where(inside, 1.0, 0.0).astype(jnp.bfloat16)


def update(top, ext, scores, values):
    peak = jnp.max(scores, axis=1, keepdims=True) * SCALE
    if top is not None:
        peak = jnp.maximum(top, peak)
    weights = jnp.exp2(scores * SCALE - peak).astype(jnp.bfloat16)
    term = jnp.dot(weights, values, preferred_element_type=jnp.float32)
    if top is not None:
        term = ext * jnp.exp2(top - peak) + term
    return peak, term


def over_cache(top, ext, queried, keys, values):
    for at in range(0, keys.shape[0], SUB):
        scores = dot_rows(queried, keys[at : at + SUB, :])
        top, ext = update(top, ext, scores, values[at : at + SUB, :])
    return top, ext


def merge(state, other):
    (top, total, acc), (other_top, other_total, other_acc) = state, other
    peak = jnp.maximum(top, other_top)
    scale, other_scale = jnp.exp2(top - peak), jnp.exp2(other_top - peak)
    return peak, total * scale + other_total * other_scale, acc * scale + other_acc * other_scale


def valid_slots(length_ref, member_ref, own, at, count):
    limit = length_ref[0] * BLOCK
    low = jnp.minimum(limit, HALF)
    first_half = (member_ref[0] % 2 == 0) == own
    return jnp.clip(jnp.where(first_half, low, limit - low) - at, 0, count)


def cache_part_kernel(own, at_slot, length_ref, member_ref, q_ref, kv_ref, after_ref, *refs):
    if own:
        before, (top_ref, total_ref, acc_ref, token_ref, chunk_ref, keys, values) = (), refs

        @pl.when(pl.program_id(0) == 0)
        def pass_on():
            chunk_ref[...] = kv_ref[:, : chunk_ref.shape[1], :]

    else:
        before, (top_ref, total_ref, acc_ref, token_ref, keys, values) = refs[:3], refs[3:]
    valid = valid_slots(length_ref, member_ref, own, at_slot, keys.shape[0])

    @pl.when(pl.program_id(0) == 0)
    def prepare():
        token_ref[...] = after_ref[...]
        load_cache(valid, kv_ref, keys, values)

    @pl.when(valid > 0)
    def some():
        for at in range(STEP_HEADS):
            span = slice(at * HD, (at + 1) * HD)
            top, ext = over_cache(None, None, q_ref[:, span], keys, values)
            state = jnp.broadcast_to(top, (TOK, HD)), ext[:, HD:], ext[:, :HD]
            if before:
                state = merge(state, [ref[:, span] for ref in before])
            top_ref[:, span], total_ref[:, span], acc_ref[:, span] = state

    @pl.when(valid <= 0)
    def none():
        for at, ref in enumerate((top_ref, total_ref, acc_ref)):
            ref[...] = before[at][...] if before else jnp.full(ref.shape, 0.0 if at else LOW)


HEADS_SPEC = pl.BlockSpec((TOK, STEP_HEADS * HD), lambda g: (0, g))
ROWS_SPEC = pl.BlockSpec((TOK, HD), lambda g: (0, 0))
TOKEN_SPEC = pl.BlockSpec((8, HD), lambda g: (0, 0))


def cache_part(length, member, queries, cache, after, own, at, state=()):
    count = cache.shape[1]
    return pl.pallas_call(
        functools.partial(cache_part_kernel, own, at),
        grid=(HEADS // STEP_HEADS,),
        out_shape=[pltpu.HBM((TOK, HEADS * HD), jnp.float32)] * 3
        + [TOKEN]
        + [struct((2, HALF, HD), jnp.bfloat16)] * own,
        in_specs=[
            SMEM, SMEM, HEADS_SPEC, pl.BlockSpec(cache.shape, lambda g: (0, 0, 0)), TOKEN_SPEC,
        ]
        + [HEADS_SPEC] * len(state),
        out_specs=[HEADS_SPEC] * 3
        + [TOKEN_SPEC]
        + [pl.BlockSpec((2, HALF, HD), lambda g: (0, 0, 0))] * own,
        scratch_shapes=[
            pltpu.VMEM((count, HD), jnp.bfloat16),
            pltpu.VMEM((count, 2 * HD), jnp.bfloat16),
        ],
        compiler_params=params(20),
        cost_estimate=pl.CostEstimate(
            flops=8 * TOK * HEADS * count * HD,
            bytes_accessed=2 << 20,
            transcendentals=TOK * HEADS * count,
        ),
        name="own_half" if own else "other_part",
    )(length, member, in_hbm(queries), cache, after, *(in_hbm(part) for part in state))


def last_kernel(length_ref, member_ref, q_ref, kv_ref, *refs):
    before, (mine_ref, theirs_ref) = refs[:3], refs[3:5]
    out_ref, token_ref, keys, values, new_keys, new_values = refs[5:]
    is_key = member_ref[0] % 2 == 0
    valid = valid_slots(length_ref, member_ref, False, 0, HALF)

    @pl.when(pl.program_id(0) == 0)
    def prepare():
        token_ref[...] = jnp.zeros_like(token_ref)
        load_cache(valid, kv_ref, keys, values)
        new_keys[...] = jnp.where(is_key, mine_ref[...], theirs_ref[...])
        new_values[:, :HD] = jnp.where(is_key, theirs_ref[...], mine_ref[...])
        new_values[:, HD:] = jnp.ones((TOK, HD), jnp.bfloat16)

    def run(with_cache):
        row = lax.broadcasted_iota(jnp.int32, (TOK, TOK), 0)
        column = lax.broadcasted_iota(jnp.int32, (TOK, TOK), 1)
        for at in range(STEP_HEADS):
            span = slice(at * HD, (at + 1) * HD)
            queried = q_ref[:, span]
            scores = jnp.where(column <= row, dot_rows(queried, new_keys[...]), LOW)
            top, ext = update(None, None, scores, new_values[...])
            if with_cache:
                top, ext = over_cache(top, ext, queried, keys, values)
            state = jnp.broadcast_to(top, (TOK, HD)), ext[:, HD:], ext[:, :HD]
            _, total, acc = merge(state, [ref[:, span] for ref in before])
            out_ref[:, span] = (acc / total).astype(jnp.bfloat16)

    pl.when(valid > 0)(lambda: run(True))
    pl.when(valid <= 0)(lambda: run(False))


def last(length, member, queries, cache, state, mine, theirs):
    slots = HALF + TOK
    return pl.pallas_call(
        last_kernel,
        grid=(HEADS // STEP_HEADS,),
        out_shape=[struct((TOK, HEADS * HD), jnp.bfloat16), TOKEN],
        in_specs=[SMEM] * 2
        + [HEADS_SPEC, pl.BlockSpec(cache.shape, lambda g: (0, 0, 0))]
        + [HEADS_SPEC] * 3
        + [ROWS_SPEC] * 2,
        out_specs=[HEADS_SPEC, TOKEN_SPEC],
        scratch_shapes=[
            pltpu.VMEM((HALF, HD), jnp.bfloat16),
            pltpu.VMEM((HALF, 2 * HD), jnp.bfloat16),
            pltpu.VMEM((TOK, HD), jnp.bfloat16),
            pltpu.VMEM((TOK, 2 * HD), jnp.bfloat16),
        ],
        compiler_params=params(24),
        cost_estimate=pl.CostEstimate(
            flops=8 * TOK * HEADS * slots * HD,
            bytes_accessed=3 << 20,
            transcendentals=TOK * HEADS * slots,
        ),
        name="last",
    )(
        length, member, in_hbm(queries), cache, *(in_hbm(part) for part in state), mine, theirs,
    )


def rotation(length, is_key):
    half = HD // 2
    positions = (length * BLOCK + jnp.arange(TOK)).astype(jnp.float32)
    frequency = jnp.exp(jnp.arange(half).astype(jnp.float32) * (-2.0 * math.log(500000.0) / HD))
    angles = positions[:, None] * frequency[None, :]
    cosine = jnp.where(is_key, jnp.cos(angles), 1.0)
    sine = jnp.where(is_key, jnp.sin(angles), 0.0)
    return jnp.concatenate([cosine, cosine], 1), jnp.concatenate([-sine, sine], 1)


def per_device(hidden, queries, prefix_cache, lengths, pairing, w_kv):
    member = lax.axis_index("tp").astype(jnp.int32)
    inst = lax.axis_index("inst").astype(jnp.int32).reshape(1)
    role = lax.axis_index("role").astype(jnp.int32).reshape(1)
    length = lengths.reshape(1)
    resident = prefix_cache[0, 0, 0]
    queried = queries[0, 0]
    cosine, sine = rotation(lengths[0, 0], member % 2 == 0)
    member = member.reshape(1)

    parts, token = project(member, hidden[0, 0], w_kv)
    with jax.named_scope("sum_x"):
        parts = exchange_tp(parts, X_GROUPS)
    *state, token, chunk = cache_part(length, member, queried, in_hbm(resident), token, True, 0)
    with jax.named_scope("prefix_first"):
        across = swap_tp(chunk, 1)
    keep, parts, token = sum_x(member, parts, token)
    with jax.named_scope("sum_z"):
        parts = exchange_tp(parts, Z_GROUPS)
    own_kv, sends = finish(member, keep, parts, cosine, sine, token)

    with jax.named_scope("handoff_y"):
        column = lax.all_to_all(
            sends, "inst", 0, 0, axis_index_groups=Y_GROUPS, tiled=True
        )
    with jax.named_scope("pair"):
        other_kv = swap_tp(own_kv, 1)
    offers = offer(pairing, inst, column)
    with jax.named_scope("handoff_z"):
        offered = [
            role_inst(offers[j], [(i, 16 + (i ^ (4 * j))) for i in range(16)]) for j in range(4)
        ]
    attended, token = last(length, member, queried, across, state, own_kv, other_kv)
    layer_kv = take(pairing, inst, role, own_kv, offered, token)
    return attended[None, None], layer_kv[None, None]


def solution(mesh):
    in_specs = (
        P("role", "inst", None, "tp"),
        P("role", "inst", None, "tp"),
        P("role", "inst", "tp", None, None, None),
        P("role", "inst"),
        P(),
        P("tp", None),
    )
    out_specs = (P("role", "inst", None, "tp"), P("role", "inst", None, "tp"))
    return jax.shard_map(
        per_device, mesh=mesh, in_specs=in_specs, out_specs=out_specs, check_vma=False
    )
```

time: 100 us -> 87.8 us (0.88)
  the two profiles are of different devices: /device:TPU:3 before, /device:TPU:32 now
where the time goes in v4:
time: 87.8 us; the launch traced here: 87.3 us
  starting transfers between devices  34.6 us (39%)
  Pallas kernels  25.8 us (29%)
  waiting for transfers between devices  24.8 us (28%)
  between operations  1.41 us (2%)
    all_to_all x2, waiting for transfers between devices, exchange_tp(): lax.all_to_all(array, 'tp', 0, 0, axis_index_groups=groups, tiled=True)  20.6 us
    all_to_all x2, starting transfers between devices, exchange_tp(): lax.all_to_all(array, 'tp', 0, 0, axis_index_groups=groups, tiled=True)  18.5 us
    pallas_call x1, Pallas kernels, last(): pl.pallas_call(last_kernel, grid=(HEADS // STEP_HEADS,), out_shape=[struc...  10.1 us
    pallas_call x1, Pallas kernels, cache_part(): pl.pallas_call(functools.partial(cache_part_kernel, own, at), grid=(HEADS...  8.79 us
    ppermute x2, starting transfers between devices, swap_tp(): return lax.ppermute(array, 'tp', [(i, i ^ mask) for i in range(16)])  6.51 us
    ppermute x4, starting transfers between devices, role_inst(): return lax.ppermute(array, ('role', 'inst'), pairs)  5.17 us
    all_to_all x1, starting transfers between devices, per_device(): lax.all_to_all(sends, 'inst', 0, 0, axis_index_groups=Y_GROUPS, tiled=True)  4.46 us
    all_to_all x1, waiting for transfers between devices, per_device(): lax.all_to_all(sends, 'inst', 0, 0, axis_index_groups=Y_GROUPS, tiled=True)  4.2 us
  transfers between devices with their start and end apart: 9, of which 3 were waited for; matrix products, arithmetic and copies ran while one was open for 1% of the time, Pallas kernels for 24%

profile of v4, /device:TPU:32, one launch (start us, length us, event | category | flops | bytes accessed | tf_op | source)
XLA Modules:
  0.0 87.3 jit_solution(7893069375556192060)
XLA Ops:
  0.6 3.4 %project.1 = (bf16[4,4,256,128]{3,2,1,0:T(8,128)(2,1)}, f32[8,128]{1,0:T(8,128)S(1)}) custom-call(s32[1]{0:T(128)} %bitcast.1.member_ref, bf16[256,512]{1,0:T(8,128)(2,1)} %bitcast.12, bf16[512,2048]{1,0:T(8,128)(2,1)} %w_hbm.1), custom_call_target="tpu_custom_call" | custom-call | flops 536870912 | bytes 4194304 | tf_op jit(solution)/shard_map/project/pallas_call | solution.py:79
  4.0 4.3 %all-to-all-start = ((bf16[4,4,256,128]{3,2,1,0:T(8,128)(2,1)}), bf16[4,4,256,128]{3,2,1,0:T(8,128)(2,1)S(1)}, u32[]{:S(2)}, u32[]{:S(2)}) async-start(bf16[4,4,256,128]{3,2,1,0:T(8,128)(2,1)} %get-tuple-element.25), calls=%async_computation | async-start | bytes 2097152 | tf_op jit(solution)/shard_map/sum_x/all_to_all | solution.py:51
  9.0 8.8 %own_half.1 = (f32[256,1024]{1,0:T(8,128)}, f32[256,1024]{1,0:T(8,128)}, f32[256,1024]{1,0:T(8,128)}, f32[8,128]{1,0:T(8,128)S(1)}, bf16[2,2048,128]{2,1,0:T(8,128)(2,1)S(1)}) custom-call(s32[1]{0:T(128)} %bitcast.10.length_ref, s32[1]{0:T(128)} %bitcast.1.member_ref, bf16[256,1024]{1,0:T(8,128)(2,1)} %bitcast.15, bf16[2,2048,128]{2,1,0:T(8,128)(2,1)} %bitcast.14, ...), custom_call_target="tpu_custom_call" | custom-call | flops 4294967296 | bytes 2097152 | tf_op jit(solution)/shard_map/own_half/pallas_call | solution.py:282
  17.8 0.0 copy-start
  17.8 4.1 %collective-permute-start = (bf16[2,2048,128]{2,1,0:T(8,128)(2,1)S(1)}, bf16[2,2048,128]{2,1,0:T(8,128)(2,1)S(1)}, u32[]{:S(2)}, u32[]{:S(2)}) collective-permute-start(bf16[2,2048,128]{2,1,0:T(8,128)(2,1)S(1)} %get-tuple-element.21), channel_id=1, source_target_pairs={{0,1},{1,0},{2,3},{3,2},{4,5},{5,4},{6,7},{7,6},{8,9},{9,8},{10,11... | collective-permute-start | bytes 3145736 | tf_op jit(solution)/shard_map/prefix_first/ppermute | solution.py:47
  21.8 1.6 %all-to-all-done.parts_ref = bf16[4,4,256,128]{3,2,1,0:T(8,128)(2,1)S(1)} async-done(((bf16[4,4,256,128]{3,2,1,0:T(8,128)(2,1)}), bf16[4,4,256,128]{3,2,1,0:T(8,128)(2,1)S(1)}, u32[]{:S(2)}, u32[]{:S(2)}) %all-to-all-start) | async-done | bytes 1048608 | tf_op jit(solution)/shard_map/sum_x/all_to_all | solution.py:51
  23.4 0.8 sum_x.1
  24.2 14.2 %all-to-all-start.1 = ((bf16[4,256,128]{2,1,0:T(8,128)(2,1)}), bf16[4,256,128]{2,1,0:T(8,128)(2,1)S(1)}, u32[]{:S(2)}, u32[]{:S(2)}) async-start(bf16[4,256,128]{2,1,0:T(8,128)(2,1)} %get-tuple-element.28), calls=%async_computation.1 | async-start | bytes 524288 | tf_op jit(solution)/shard_map/sum_z/all_to_all | solution.py:51
  38.4 0.6 fusion.2
  39.0 0.1 pad_maximum_fusion
  39.1 19.0 %all-to-all-done.1.parts_ref = bf16[4,256,128]{2,1,0:T(8,128)(2,1)S(1)} async-done(((bf16[4,256,128]{2,1,0:T(8,128)(2,1)}), bf16[4,256,128]{2,1,0:T(8,128)(2,1)S(1)}, u32[]{:S(2)}, u32[]{:S(2)}) %all-to-all-start.1) | async-done | bytes 262176 | tf_op jit(solution)/shard_map/sum_z/all_to_all | solution.py:51
  58.2 0.8 finish.1
  59.0 4.5 %all-to-all-start.2 = ((bf16[4,256,128]{2,1,0:T(8,128)(2,1)}), bf16[4,256,128]{2,1,0:T(8,128)(2,1)S(1)}, u32[]{:S(2)}, u32[]{:S(2)}) async-start(bf16[4,256,128]{2,1,0:T(8,128)(2,1)} %get-tuple-element.32), calls=%async_computation.2 | async-start | bytes 524288 | tf_op jit(solution)/shard_map/handoff_y/all_to_all | solution.py:402
  63.4 2.5 %collective-permute-start.1 = (bf16[256,128]{1,0:T(8,128)(2,1)S(1)}, bf16[256,128]{1,0:T(8,128)(2,1)S(1)}, u32[]{:S(2)}, u32[]{:S(2)}) collective-permute-start(bf16[256,128]{1,0:T(8,128)(2,1)S(1)} %get-tuple-element.30.refs_3_.own_ref), channel_id=1, source_target_pairs={{0,1},{1,0},{2,3},{3,2},{4,5},{5,4},{6,7},{7,6},{8,9},{9,8},{10,11... | collective-permute-start | bytes 196616 | tf_op jit(solution)/shard_map/pair/ppermute | solution.py:47
  65.9 4.2 %all-to-all-done.2.refs_0_ = bf16[4,256,128]{2,1,0:T(8,128)(2,1)S(1)} async-done(((bf16[4,256,128]{2,1,0:T(8,128)(2,1)}), bf16[4,256,128]{2,1,0:T(8,128)(2,1)S(1)}, u32[]{:S(2)}, u32[]{:S(2)}) %all-to-all-start.2) | async-done | bytes 262176 | tf_op jit(solution)/shard_map/handoff_y/all_to_all | solution.py:402
  70.1 0.0 copy-done
  70.1 0.6 offer.1
  70.7 1.3 %collective-permute-start.2 = (bf16[256,128]{1,0:T(8,128)(2,1)S(1)}, bf16[256,128]{1,0:T(8,128)(2,1)S(1)}, u32[]{:S(2)}, u32[]{:S(2)}) collective-permute-start(bf16[256,128]{1,0:T(8,128)(2,1)S(1)} %get-tuple-element.33), channel_id=1, source_target_pairs={{0,256},{16,272},{32,288},{48,304},{64,320},{80,336},{96,352},{112... | collective-permute-start | bytes 196616 | tf_op jit(solution)/shard_map/handoff_z/ppermute | solution.py:55
  72.0 1.3 %collective-permute-start.3 = (bf16[256,128]{1,0:T(8,128)(2,1)S(1)}, bf16[256,128]{1,0:T(8,128)(2,1)S(1)}, u32[]{:S(2)}, u32[]{:S(2)}) collective-permute-start(bf16[256,128]{1,0:T(8,128)(2,1)S(1)} %get-tuple-element.34), channel_id=1, source_target_pairs={{0,320},{16,336},{32,352},{48,368},{64,256},{80,272},{96,288},{112... | collective-permute-start | bytes 196616 | tf_op jit(solution)/shard_map/handoff_z/ppermute | solution.py:55
  73.3 1.3 %collective-permute-start.4 = (bf16[256,128]{1,0:T(8,128)(2,1)S(1)}, bf16[256,128]{1,0:T(8,128)(2,1)S(1)}, u32[]{:S(2)}, u32[]{:S(2)}) collective-permute-start(bf16[256,128]{1,0:T(8,128)(2,1)S(1)} %get-tuple-element.35), channel_id=1, source_target_pairs={{0,384},{16,400},{32,416},{48,432},{64,448},{80,464},{96,480},{112... | collective-permute-start | bytes 196616 | tf_op jit(solution)/shard_map/handoff_z/ppermute | solution.py:55
  74.6 0.0 collective-permute-done.kv_ref
  74.6 1.3 %collective-permute-start.5 = (bf16[256,128]{1,0:T(8,128)(2,1)S(1)}, bf16[256,128]{1,0:T(8,128)(2,1)S(1)}, u32[]{:S(2)}, u32[]{:S(2)}) collective-permute-start(bf16[256,128]{1,0:T(8,128)(2,1)S(1)} %get-tuple-element.36), channel_id=1, source_target_pairs={{0,448},{16,464},{32,480},{48,496},{64,384},{80,400},{96,416},{112... | collective-permute-start | bytes 196616 | tf_op jit(solution)/shard_map/handoff_z/ppermute | solution.py:55
  75.9 0.0 collective-permute-done.1.refs_4_
  75.9 10.1 %last.1 = (bf16[256,1024]{1,0:T(8,128)(2,1)}, f32[8,128]{1,0:T(8,128)S(1)}) custom-call(s32[1]{0:T(128)} %bitcast.11.length_ref, s32[1]{0:T(128)} %bitcast.1.member_ref, bf16[256,1024]{1,0:T(8,128)(2,1)} %bitcast.16, bf16[2,2048,128]{2,1,0:T(8,128)(2,1)S(1)} %collective-permute-done.kv_ref, f32[256,1024]{1,0:T(8,128)} %get-tuple-element.22.refs_0_, ...), custom_call_target="tpu_custom_call" | custom-call | flops 4831838208 | bytes 3145728 | tf_op jit(solution)/shard_map/last/pallas_call | solution.py:343
  86.1 0.0 collective-permute-done.2.refs_0_
  86.1 0.0 collective-permute-done.3.refs_1_
  86.1 0.0 collective-permute-done.4.refs_2_
  86.1 0.0 collective-permute-done.5.refs_3_
  86.1 1.2 %take.1 = bf16[256,128]{1,0:T(8,128)(2,1)} custom-call(s32[16]{0:T(128)S(1)} %copy-done, s32[1]{0:T(128)} %bitcast.7.inst_ref, s32[1]{0:T(128)} %bitcast.8.role_ref, bf16[256,128]{1,0:T(8,128)(2,1)S(1)} %get-tuple-element.30.refs_3_.own_ref, bf16[256,128]{1,0:T(8,128)(2,1)S(1)} %collective-permute-done.2.refs_0_, ...), custom_call_target="tpu_custom_call" | custom-call | tf_op jit(solution)/shard_map/take/pallas_call | solution.py:188
  (2 shorter events, 0.0 us)
Async XLA Ops:
  4.0 19.4 %all-to-all-start = ((bf16[4,4,256,128]{3,2,1,0:T(8,128)(2,1)}), bf16[4,4,256,128]{3,2,1,0:T(8,128)(2,1)S(1)}, u32[]{:S(2)}, u32[]{:S(2)}) async-start(bf16[4,4,256,128]{3,2,1,0:T(8,128)(2,1)} %get-tuple-element.25), calls=%async_computation | async-start | bytes 2097152 | tf_op jit(solution)/shard_map/sum_x/all_to_all | solution.py:51
  17.8 52.4 %copy-start = (s32[16]{0:T(128)S(1)}, s32[16]{0:T(128)}, u32[]{:S(2)}) copy-start(s32[16]{0:T(128)} %pairing_ref.3) | copy-start | bytes 196
  17.8 56.9 %collective-permute-start = (bf16[2,2048,128]{2,1,0:T(8,128)(2,1)S(1)}, bf16[2,2048,128]{2,1,0:T(8,128)(2,1)S(1)}, u32[]{:S(2)}, u32[]{:S(2)}) collective-permute-start(bf16[2,2048,128]{2,1,0:T(8,128)(2,1)S(1)} %get-tuple-element.21), channel_id=1, source_target_pairs={{0,1},{1,0},{2,3},{3,2},{4,5},{5,4},{6,7},{7,6},{8,9},{9,8},{10,11... | collective-permute-start | bytes 3145736 | tf_op jit(solution)/shard_map/prefix_first/ppermute | solution.py:47
  24.2 33.9 %all-to-all-start.1 = ((bf16[4,256,128]{2,1,0:T(8,128)(2,1)}), bf16[4,256,128]{2,1,0:T(8,128)(2,1)S(1)}, u32[]{:S(2)}, u32[]{:S(2)}) async-start(bf16[4,256,128]{2,1,0:T(8,128)(2,1)} %get-tuple-element.28), calls=%async_computation.1 | async-start | bytes 524288 | tf_op jit(solution)/shard_map/sum_z/all_to_all | solution.py:51
  59.0 11.1 %all-to-all-start.2 = ((bf16[4,256,128]{2,1,0:T(8,128)(2,1)}), bf16[4,256,128]{2,1,0:T(8,128)(2,1)S(1)}, u32[]{:S(2)}, u32[]{:S(2)}) async-start(bf16[4,256,128]{2,1,0:T(8,128)(2,1)} %get-tuple-element.32), calls=%async_computation.2 | async-start | bytes 524288 | tf_op jit(solution)/shard_map/handoff_y/all_to_all | solution.py:402
  63.4 12.5 %collective-permute-start.1 = (bf16[256,128]{1,0:T(8,128)(2,1)S(1)}, bf16[256,128]{1,0:T(8,128)(2,1)S(1)}, u32[]{:S(2)}, u32[]{:S(2)}) collective-permute-start(bf16[256,128]{1,0:T(8,128)(2,1)S(1)} %get-tuple-element.30.refs_3_.own_ref), channel_id=1, source_target_pairs={{0,1},{1,0},{2,3},{3,2},{4,5},{5,4},{6,7},{7,6},{8,9},{9,8},{10,11... | collective-permute-start | bytes 196616 | tf_op jit(solution)/shard_map/pair/ppermute | solution.py:47
  70.7 15.4 %collective-permute-start.2 = (bf16[256,128]{1,0:T(8,128)(2,1)S(1)}, bf16[256,128]{1,0:T(8,128)(2,1)S(1)}, u32[]{:S(2)}, u32[]{:S(2)}) collective-permute-start(bf16[256,128]{1,0:T(8,128)(2,1)S(1)} %get-tuple-element.33), channel_id=1, source_target_pairs={{0,256},{16,272},{32,288},{48,304},{64,320},{80,336},{96,352},{112... | collective-permute-start | bytes 196616 | tf_op jit(solution)/shard_map/handoff_z/ppermute | solution.py:55
  72.0 14.1 %collective-permute-start.3 = (bf16[256,128]{1,0:T(8,128)(2,1)S(1)}, bf16[256,128]{1,0:T(8,128)(2,1)S(1)}, u32[]{:S(2)}, u32[]{:S(2)}) collective-permute-start(bf16[256,128]{1,0:T(8,128)(2,1)S(1)} %get-tuple-element.34), channel_id=1, source_target_pairs={{0,320},{16,336},{32,352},{48,368},{64,256},{80,272},{96,288},{112... | collective-permute-start | bytes 196616 | tf_op jit(solution)/shard_map/handoff_z/ppermute | solution.py:55
  73.3 12.8 %collective-permute-start.4 = (bf16[256,128]{1,0:T(8,128)(2,1)S(1)}, bf16[256,128]{1,0:T(8,128)(2,1)S(1)}, u32[]{:S(2)}, u32[]{:S(2)}) collective-permute-start(bf16[256,128]{1,0:T(8,128)(2,1)S(1)} %get-tuple-element.35), channel_id=1, source_target_pairs={{0,384},{16,400},{32,416},{48,432},{64,448},{80,464},{96,480},{112... | collective-permute-start | bytes 196616 | tf_op jit(solution)/shard_map/handoff_z/ppermute | solution.py:55
  74.6 11.5 %collective-permute-start.5 = (bf16[256,128]{1,0:T(8,128)(2,1)S(1)}, bf16[256,128]{1,0:T(8,128)(2,1)S(1)}, u32[]{:S(2)}, u32[]{:S(2)}) collective-permute-start(bf16[256,128]{1,0:T(8,128)(2,1)S(1)} %get-tuple-element.36), channel_id=1, source_target_pairs={{0,448},{16,464},{32,480},{48,496},{64,384},{80,400},{96,416},{112... | collective-permute-start | bytes 196616 | tf_op jit(solution)/shard_map/handoff_z/ppermute | solution.py:55

commit v5 on v4

--- a/solution.py
+++ b/solution.py
@@ -306,65 +306,48 @@
     )(length, member, in_hbm(queries), cache, after, *(in_hbm(part) for part in state))
 
 
-def last_kernel(length_ref, member_ref, q_ref, kv_ref, *refs):
+def last_kernel(member_ref, q_ref, *refs):
     before, (mine_ref, theirs_ref) = refs[:3], refs[3:5]
-    out_ref, token_ref, keys, values, new_keys, new_values = refs[5:]
+    out_ref, token_ref, new_keys, new_values = refs[5:]
     is_key = member_ref[0] % 2 == 0
-    valid = valid_slots(length_ref, member_ref, False, 0, HALF)
 
     @pl.when(pl.program_id(0) == 0)
     def prepare():
         token_ref[...] = jnp.zeros_like(token_ref)
-        load_cache(valid, kv_ref, keys, values)
         new_keys[...] = jnp.where(is_key, mine_ref[...], theirs_ref[...])
         new_values[:, :HD] = jnp.where(is_key, theirs_ref[...], mine_ref[...])
         new_values[:, HD:] = jnp.ones((TOK, HD), jnp.bfloat16)
 
-    def run(with_cache):
-        row = lax.broadcasted_iota(jnp.int32, (TOK, TOK), 0)
-        column = lax.broadcasted_iota(jnp.int32, (TOK, TOK), 1)
-        for at in range(STEP_HEADS):
-            span = slice(at * HD, (at + 1) * HD)
-            queried = q_ref[:, span]
-            scores = jnp.where(column <= row, dot_rows(queried, new_keys[...]), LOW)
-            top, ext = update(None, None, scores, new_values[...])
-            if with_cache:
-                top, ext = over_cache(top, ext, queried, keys, values)
-            state = jnp.broadcast_to(top, (TOK, HD)), ext[:, HD:], ext[:, :HD]
-            _, total, acc = merge(state, [ref[:, span] for ref in before])
-            out_ref[:, span] = (acc / total).astype(jnp.bfloat16)
-
-    pl.when(valid > 0)(lambda: run(True))
-    pl.when(valid <= 0)(lambda: run(False))
-
-
-def last(length, member, queries, cache, state, mine, theirs):
-    slots = HALF + TOK
+    row = lax.broadcasted_iota(jnp.int32, (TOK, TOK), 0)
+    column = lax.broadcasted_iota(jnp.int32, (TOK, TOK), 1)
+    for at in range(STEP_HEADS):
+        span = slice(at * HD, (at + 1) * HD)
+        scores = jnp.where(column <= row, dot_rows(q_ref[:, span], new_keys[...]), LOW)
+        top, ext = update(None, None, scores, new_values[...])
+        state = jnp.broadcast_to(top, (TOK, HD)), ext[:, HD:], ext[:, :HD]
+        _, total, acc = merge(state, [ref[:, span] for ref in before])
+        out_ref[:, span] = (acc / total).astype(jnp.bfloat16)
+
+
+def last(member, queries, state, mine, theirs):
     return pl.pallas_call(
         last_kernel,
         grid=(HEADS // STEP_HEADS,),
         out_shape=[struct((TOK, HEADS * HD), jnp.bfloat16), TOKEN],
-        in_specs=[SMEM] * 2
-        + [HEADS_SPEC, pl.BlockSpec(cache.shape, lambda g: (0, 0, 0))]
-        + [HEADS_SPEC] * 3
-        + [ROWS_SPEC] * 2,
+        in_specs=[SMEM] + [HEADS_SPEC] * 4 + [ROWS_SPEC] * 2,
         out_specs=[HEADS_SPEC, TOKEN_SPEC],
         scratch_shapes=[
-            pltpu.VMEM((HALF, HD), jnp.bfloat16),
-            pltpu.VMEM((HALF, 2 * HD), jnp.bfloat16),
             pltpu.VMEM((TOK, HD), jnp.bfloat16),
             pltpu.VMEM((TOK, 2 * HD), jnp.bfloat16),
         ],
-        compiler_params=params(24),
+        compiler_params=params(16),
         cost_estimate=pl.CostEstimate(
-            flops=8 * TOK * HEADS * slots * HD,
+            flops=8 * TOK * HEADS * TOK * HD,
             bytes_accessed=3 << 20,
-            transcendentals=TOK * HEADS * slots,
+            transcendentals=TOK * HEADS * TOK,
         ),
         name="last",
-    )(
-        length, member, in_hbm(queries), cache, *(in_hbm(part) for part in state), mine, theirs,
-    )
+    )(member, in_hbm(queries), *(in_hbm(part) for part in state), mine, theirs)
 
 
 def rotation(length, is_key):
@@ -396,6 +379,7 @@
     keep, parts, token = sum_x(member, parts, token)
     with jax.named_scope("sum_z"):
         parts = exchange_tp(parts, Z_GROUPS)
+    *state, token = cache_part(length, member, queried, across, token, False, 0, state)
     own_kv, sends = finish(member, keep, parts, cosine, sine, token)
 
     with jax.named_scope("handoff_y"):
@@ -409,7 +393,7 @@
         offered = [
             role_inst(offers[j], [(i, 16 + (i ^ (4 * j))) for i in range(16)]) for j in range(4)
         ]
-    attended, token = last(length, member, queried, across, state, own_kv, other_kv)
+    attended, token = last(member, queried, state, own_kv, other_kv)
     layer_kv = take(pairing, inst, role, own_kv, offered, token)
     return attended[None, None], layer_kv[None, None]
 

time: 87.8 us -> 82.6 us (0.941)
  the two profiles are of different devices: /device:TPU:32 before, /device:TPU:1 now
where the time goes in v5:
time: 82.6 us; the launch traced here: 82 us
  starting transfers between devices  37.9 us (46%)
  Pallas kernels  23 us (28%)
  waiting for transfers between devices  19 us (23%)
  between operations  1.41 us (2%)
    all_to_all x2, starting transfers between devices, exchange_tp(): lax.all_to_all(array, 'tp', 0, 0, axis_index_groups=groups, tiled=True)  22.4 us
    pallas_call x2, Pallas kernels, cache_part(): pl.pallas_call(functools.partial(cache_part_kernel, own, at), grid=(HEADS...  12.5 us
    all_to_all x2, waiting for transfers between devices, exchange_tp(): lax.all_to_all(array, 'tp', 0, 0, axis_index_groups=groups, tiled=True)  7.97 us
    ppermute x4, waiting for transfers between devices, role_inst(): return lax.ppermute(array, ('role', 'inst'), pairs)  7.6 us
    all_to_all x1, starting transfers between devices, per_device(): lax.all_to_all(sends, 'inst', 0, 0, axis_index_groups=Y_GROUPS, tiled=True)  5.53 us
    ppermute x4, starting transfers between devices, role_inst(): return lax.ppermute(array, ('role', 'inst'), pairs)  5.17 us
    ppermute x2, starting transfers between devices, swap_tp(): return lax.ppermute(array, 'tp', [(i, i ^ mask) for i in range(16)])  4.83 us
    pallas_call x1, Pallas kernels, last(): pl.pallas_call(last_kernel, grid=(HEADS // STEP_HEADS,), out_shape=[struc...  3.68 us
  transfers between devices with their start and end apart: 9, of which 5 were waited for; matrix products, arithmetic and copies ran while one was open for 1% of the time, Pallas kernels for 21%

profile of v5, /device:TPU:1, one launch (start us, length us, event | category | flops | bytes accessed | tf_op | source)
XLA Modules:
  0.0 82.0 jit_solution(11113475154772482118)
XLA Ops:
  0.6 3.4 %project.1 = (bf16[4,4,256,128]{3,2,1,0:T(8,128)(2,1)}, f32[8,128]{1,0:T(8,128)S(1)}) custom-call(s32[1]{0:T(128)} %bitcast.member_ref, bf16[256,512]{1,0:T(8,128)(2,1)} %bitcast.15, bf16[512,2048]{1,0:T(8,128)(2,1)} %w_hbm.1), custom_call_target="tpu_custom_call" | custom-call | flops 536870912 | bytes 4194304 | tf_op jit(solution)/shard_map/project/pallas_call | solution.py:79
  4.0 4.9 %all-to-all-start = ((bf16[4,4,256,128]{3,2,1,0:T(8,128)(2,1)}), bf16[4,4,256,128]{3,2,1,0:T(8,128)(2,1)S(1)}, u32[]{:S(2)}, u32[]{:S(2)}) async-start(bf16[4,4,256,128]{3,2,1,0:T(8,128)(2,1)} %get-tuple-element.26), calls=%async_computation | async-start | bytes 2097152 | tf_op jit(solution)/shard_map/sum_x/all_to_all | solution.py:51
  9.5 8.8 %own_half.1 = (f32[256,1024]{1,0:T(8,128)}, f32[256,1024]{1,0:T(8,128)}, f32[256,1024]{1,0:T(8,128)}, f32[8,128]{1,0:T(8,128)S(1)}, bf16[2,2048,128]{2,1,0:T(8,128)(2,1)S(1)}) custom-call(s32[1]{0:T(128)} %bitcast.10.length_ref, s32[1]{0:T(128)} %bitcast.member_ref, bf16[256,1024]{1,0:T(8,128)(2,1)} %bitcast.12, bf16[2,2048,128]{2,1,0:T(8,128)(2,1)} %bitcast.17, ...), custom_call_target="tpu_custom_call" | custom-call | flops 4294967296 | bytes 2097152 | tf_op jit(solution)/shard_map/own_half/pallas_call | solution.py:282
  18.3 1.9 %collective-permute-start = (bf16[2,2048,128]{2,1,0:T(8,128)(2,1)S(1)}, bf16[2,2048,128]{2,1,0:T(8,128)(2,1)S(1)}, u32[]{:S(2)}, u32[]{:S(2)}) collective-permute-start(bf16[2,2048,128]{2,1,0:T(8,128)(2,1)S(1)} %get-tuple-element.25), channel_id=1, source_target_pairs={{0,1},{1,0},{2,3},{3,2},{4,5},{5,4},{6,7},{7,6},{8,9},{9,8},{10,11... | collective-permute-start | bytes 3145736 | tf_op jit(solution)/shard_map/prefix_first/ppermute | solution.py:47
  20.3 0.0 all-to-all-done.parts_ref
  20.3 0.8 %sum_x.1 = (f32[256,128]{1,0:T(8,128)S(1)}, bf16[4,256,128]{2,1,0:T(8,128)(2,1)}, f32[8,128]{1,0:T(8,128)S(1)}) custom-call(s32[1]{0:T(128)} %bitcast.member_ref, bf16[4,4,256,128]{3,2,1,0:T(8,128)(2,1)S(1)} %all-to-all-done.parts_ref, f32[8,128]{1,0:T(8,128)S(1)} %get-tuple-element.27.after_ref), custom_call_target="tpu_custom_call" | custom-call | tf_op jit(solution)/shard_map/sum_x/pallas_call | solution.py:110
  21.1 17.6 %all-to-all-start.1 = ((bf16[4,256,128]{2,1,0:T(8,128)(2,1)}), bf16[4,256,128]{2,1,0:T(8,128)(2,1)S(1)}, u32[]{:S(2)}, u32[]{:S(2)}) async-start(bf16[4,256,128]{2,1,0:T(8,128)(2,1)} %get-tuple-element.36), calls=%async_computation.1 | async-start | bytes 524288 | tf_op jit(solution)/shard_map/sum_z/all_to_all | solution.py:51
  38.7 0.5 fusion.2
  39.2 0.1 pad_maximum_fusion
  39.4 0.8 %collective-permute-done.kv_ref = bf16[2,2048,128]{2,1,0:T(8,128)(2,1)S(1)} collective-permute-done((bf16[2,2048,128]{2,1,0:T(8,128)(2,1)S(1)}, bf16[2,2048,128]{2,1,0:T(8,128)(2,1)S(1)}, u32[]{:S(2)}, u32[]{:S(2)}) %collective-permute-start) | collective-permute-done | bytes 1048608 | tf_op jit(solution)/shard_map/prefix_first/ppermute | solution.py:47
  40.2 0.0 copy-start
  40.2 3.7 %other_part.1 = (f32[256,1024]{1,0:T(8,128)}, f32[256,1024]{1,0:T(8,128)}, f32[256,1024]{1,0:T(8,128)}, f32[8,128]{1,0:T(8,128)S(1)}) custom-call(s32[1]{0:T(128)} %bitcast.11.length_ref, s32[1]{0:T(128)} %bitcast.member_ref, bf16[256,1024]{1,0:T(8,128)(2,1)} %bitcast.13, bf16[2,2048,128]{2,1,0:T(8,128)(2,1)S(1)} %collective-permute-done.kv_ref, ...), custom_call_target="tpu_custom_call" | custom-call | flops 4294967296 | bytes 2097152 | tf_op jit(solution)/shard_map/other_part/pallas_call | solution.py:282
  43.9 8.0 %all-to-all-done.1.parts_ref = bf16[4,256,128]{2,1,0:T(8,128)(2,1)S(1)} async-done(((bf16[4,256,128]{2,1,0:T(8,128)(2,1)}), bf16[4,256,128]{2,1,0:T(8,128)(2,1)S(1)}, u32[]{:S(2)}, u32[]{:S(2)}) %all-to-all-start.1) | async-done | bytes 262176 | tf_op jit(solution)/shard_map/sum_z/all_to_all | solution.py:51
  51.8 0.8 finish.1
  52.7 5.5 %all-to-all-start.2 = ((bf16[4,256,128]{2,1,0:T(8,128)(2,1)}), bf16[4,256,128]{2,1,0:T(8,128)(2,1)S(1)}, u32[]{:S(2)}, u32[]{:S(2)}) async-start(bf16[4,256,128]{2,1,0:T(8,128)(2,1)} %get-tuple-element.40), calls=%async_computation.2 | async-start | bytes 524288 | tf_op jit(solution)/shard_map/handoff_y/all_to_all | solution.py:386
  58.2 2.9 %collective-permute-start.1 = (bf16[256,128]{1,0:T(8,128)(2,1)S(1)}, bf16[256,128]{1,0:T(8,128)(2,1)S(1)}, u32[]{:S(2)}, u32[]{:S(2)}) collective-permute-start(bf16[256,128]{1,0:T(8,128)(2,1)S(1)} %get-tuple-element.38.refs_3_.own_ref), channel_id=1, source_target_pairs={{0,1},{1,0},{2,3},{3,2},{4,5},{5,4},{6,7},{7,6},{8,9},{9,8},{10,11... | collective-permute-start | bytes 196616 | tf_op jit(solution)/shard_map/pair/ppermute | solution.py:47
  61.1 2.6 %all-to-all-done.2.refs_0_ = bf16[4,256,128]{2,1,0:T(8,128)(2,1)S(1)} async-done(((bf16[4,256,128]{2,1,0:T(8,128)(2,1)}), bf16[4,256,128]{2,1,0:T(8,128)(2,1)S(1)}, u32[]{:S(2)}, u32[]{:S(2)}) %all-to-all-start.2) | async-done | bytes 262176 | tf_op jit(solution)/shard_map/handoff_y/all_to_all | solution.py:386
  63.7 0.0 copy-done
  63.7 0.6 offer.1
  64.3 1.3 %collective-permute-start.2 = (bf16[256,128]{1,0:T(8,128)(2,1)S(1)}, bf16[256,128]{1,0:T(8,128)(2,1)S(1)}, u32[]{:S(2)}, u32[]{:S(2)}) collective-permute-start(bf16[256,128]{1,0:T(8,128)(2,1)S(1)} %get-tuple-element.41), channel_id=1, source_target_pairs={{0,256},{16,272},{32,288},{48,304},{64,320},{80,336},{96,352},{112... | collective-permute-start | bytes 196616 | tf_op jit(solution)/shard_map/handoff_z/ppermute | solution.py:55
  65.6 1.3 %collective-permute-start.3 = (bf16[256,128]{1,0:T(8,128)(2,1)S(1)}, bf16[256,128]{1,0:T(8,128)(2,1)S(1)}, u32[]{:S(2)}, u32[]{:S(2)}) collective-permute-start(bf16[256,128]{1,0:T(8,128)(2,1)S(1)} %get-tuple-element.42), channel_id=1, source_target_pairs={{0,320},{16,336},{32,352},{48,368},{64,256},{80,272},{96,288},{112... | collective-permute-start | bytes 196616 | tf_op jit(solution)/shard_map/handoff_z/ppermute | solution.py:55
  66.9 1.3 %collective-permute-start.4 = (bf16[256,128]{1,0:T(8,128)(2,1)S(1)}, bf16[256,128]{1,0:T(8,128)(2,1)S(1)}, u32[]{:S(2)}, u32[]{:S(2)}) collective-permute-start(bf16[256,128]{1,0:T(8,128)(2,1)S(1)} %get-tuple-element.43), channel_id=1, source_target_pairs={{0,384},{16,400},{32,416},{48,432},{64,448},{80,464},{96,480},{112... | collective-permute-start | bytes 196616 | tf_op jit(solution)/shard_map/handoff_z/ppermute | solution.py:55
  68.2 1.3 %collective-permute-start.5 = (bf16[256,128]{1,0:T(8,128)(2,1)S(1)}, bf16[256,128]{1,0:T(8,128)(2,1)S(1)}, u32[]{:S(2)}, u32[]{:S(2)}) collective-permute-start(bf16[256,128]{1,0:T(8,128)(2,1)S(1)} %get-tuple-element.44), channel_id=1, source_target_pairs={{0,448},{16,464},{32,480},{48,496},{64,384},{80,400},{96,416},{112... | collective-permute-start | bytes 196616 | tf_op jit(solution)/shard_map/handoff_z/ppermute | solution.py:55
  69.5 0.0 collective-permute-done.1.refs_4_
  69.5 3.7 %last.1 = (bf16[256,1024]{1,0:T(8,128)(2,1)}, f32[8,128]{1,0:T(8,128)S(1)}) custom-call(s32[1]{0:T(128)} %bitcast.member_ref, bf16[256,1024]{1,0:T(8,128)(2,1)} %bitcast.14, f32[256,1024]{1,0:T(8,128)} %get-tuple-element.32.refs_0_, f32[256,1024]{1,0:T(8,128)} %get-tuple-element.33.refs_1_, f32[256,1024]{1,0:T(8,128)} %get-tuple-element.34.refs_2_, ...), custom_call_target="tpu_custom_call" | custom-call | flops 536870912 | bytes 3145728 | tf_op jit(solution)/shard_map/last/pallas_call | solution.py:333
  73.2 0.0 collective-permute-done.2.refs_0_
  73.2 5.0 %collective-permute-done.3.refs_1_ = bf16[256,128]{1,0:T(8,128)(2,1)S(1)} collective-permute-done((bf16[256,128]{1,0:T(8,128)(2,1)S(1)}, bf16[256,128]{1,0:T(8,128)(2,1)S(1)}, u32[]{:S(2)}, u32[]{:S(2)}) %collective-permute-start.3) | collective-permute-done | bytes 65568 | tf_op jit(solution)/shard_map/handoff_z/ppermute | solution.py:55
  78.3 2.6 %collective-permute-done.4.refs_2_ = bf16[256,128]{1,0:T(8,128)(2,1)S(1)} collective-permute-done((bf16[256,128]{1,0:T(8,128)(2,1)S(1)}, bf16[256,128]{1,0:T(8,128)(2,1)S(1)}, u32[]{:S(2)}, u32[]{:S(2)}) %collective-permute-start.4) | collective-permute-done | bytes 65568 | tf_op jit(solution)/shard_map/handoff_z/ppermute | solution.py:55
  80.8 0.0 collective-permute-done.5.refs_3_
  80.8 1.2 %take.1 = bf16[256,128]{1,0:T(8,128)(2,1)} custom-call(s32[16]{0:T(128)S(1)} %copy-done, s32[1]{0:T(128)} %bitcast.7.inst_ref, s32[1]{0:T(128)} %bitcast.8.role_ref, bf16[256,128]{1,0:T(8,128)(2,1)S(1)} %get-tuple-element.38.refs_3_.own_ref, bf16[256,128]{1,0:T(8,128)(2,1)S(1)} %collective-permute-done.2.refs_0_, ...), custom_call_target="tpu_custom_call" | custom-call | tf_op jit(solution)/shard_map/take/pallas_call | solution.py:188
  (2 shorter events, 0.0 us)
Async XLA Ops:
  4.0 16.3 %all-to-all-start = ((bf16[4,4,256,128]{3,2,1,0:T(8,128)(2,1)}), bf16[4,4,256,128]{3,2,1,0:T(8,128)(2,1)S(1)}, u32[]{:S(2)}, u32[]{:S(2)}) async-start(bf16[4,4,256,128]{3,2,1,0:T(8,128)(2,1)} %get-tuple-element.26), calls=%async_computation | async-start | bytes 2097152 | tf_op jit(solution)/shard_map/sum_x/all_to_all | solution.py:51
  18.3 21.9 %collective-permute-start = (bf16[2,2048,128]{2,1,0:T(8,128)(2,1)S(1)}, bf16[2,2048,128]{2,1,0:T(8,128)(2,1)S(1)}, u32[]{:S(2)}, u32[]{:S(2)}) collective-permute-start(bf16[2,2048,128]{2,1,0:T(8,128)(2,1)S(1)} %get-tuple-element.25), channel_id=1, source_target_pairs={{0,1},{1,0},{2,3},{3,2},{4,5},{5,4},{6,7},{7,6},{8,9},{9,8},{10,11... | collective-permute-start | bytes 3145736 | tf_op jit(solution)/shard_map/prefix_first/ppermute | solution.py:47
  21.1 30.7 %all-to-all-start.1 = ((bf16[4,256,128]{2,1,0:T(8,128)(2,1)}), bf16[4,256,128]{2,1,0:T(8,128)(2,1)S(1)}, u32[]{:S(2)}, u32[]{:S(2)}) async-start(bf16[4,256,128]{2,1,0:T(8,128)(2,1)} %get-tuple-element.36), calls=%async_computation.1 | async-start | bytes 524288 | tf_op jit(solution)/shard_map/sum_z/all_to_all | solution.py:51
  40.2 23.5 %copy-start = (s32[16]{0:T(128)S(1)}, s32[16]{0:T(128)}, u32[]{:S(2)}) copy-start(s32[16]{0:T(128)} %pairing_ref.3) | copy-start | bytes 196
  52.7 11.1 %all-to-all-start.2 = ((bf16[4,256,128]{2,1,0:T(8,128)(2,1)}), bf16[4,256,128]{2,1,0:T(8,128)(2,1)S(1)}, u32[]{:S(2)}, u32[]{:S(2)}) async-start(bf16[4,256,128]{2,1,0:T(8,128)(2,1)} %get-tuple-element.40), calls=%async_computation.2 | async-start | bytes 524288 | tf_op jit(solution)/shard_map/handoff_y/all_to_all | solution.py:386
  58.2 11.3 %collective-permute-start.1 = (bf16[256,128]{1,0:T(8,128)(2,1)S(1)}, bf16[256,128]{1,0:T(8,128)(2,1)S(1)}, u32[]{:S(2)}, u32[]{:S(2)}) collective-permute-start(bf16[256,128]{1,0:T(8,128)(2,1)S(1)} %get-tuple-element.38.refs_3_.own_ref), channel_id=1, source_target_pairs={{0,1},{1,0},{2,3},{3,2},{4,5},{5,4},{6,7},{7,6},{8,9},{9,8},{10,11... | collective-permute-start | bytes 196616 | tf_op jit(solution)/shard_map/pair/ppermute | solution.py:47
  64.3 8.9 %collective-permute-start.2 = (bf16[256,128]{1,0:T(8,128)(2,1)S(1)}, bf16[256,128]{1,0:T(8,128)(2,1)S(1)}, u32[]{:S(2)}, u32[]{:S(2)}) collective-permute-start(bf16[256,128]{1,0:T(8,128)(2,1)S(1)} %get-tuple-element.41), channel_id=1, source_target_pairs={{0,256},{16,272},{32,288},{48,304},{64,320},{80,336},{96,352},{112... | collective-permute-start | bytes 196616 | tf_op jit(solution)/shard_map/handoff_z/ppermute | solution.py:55
  65.6 12.6 %collective-permute-start.3 = (bf16[256,128]{1,0:T(8,128)(2,1)S(1)}, bf16[256,128]{1,0:T(8,128)(2,1)S(1)}, u32[]{:S(2)}, u32[]{:S(2)}) collective-permute-start(bf16[256,128]{1,0:T(8,128)(2,1)S(1)} %get-tuple-element.42), channel_id=1, source_target_pairs={{0,320},{16,336},{32,352},{48,368},{64,256},{80,272},{96,288},{112... | collective-permute-start | bytes 196616 | tf_op jit(solution)/shard_map/handoff_z/ppermute | solution.py:55
  66.9 13.9 %collective-permute-start.4 = (bf16[256,128]{1,0:T(8,128)(2,1)S(1)}, bf16[256,128]{1,0:T(8,128)(2,1)S(1)}, u32[]{:S(2)}, u32[]{:S(2)}) collective-permute-start(bf16[256,128]{1,0:T(8,128)(2,1)S(1)} %get-tuple-element.43), channel_id=1, source_target_pairs={{0,384},{16,400},{32,416},{48,432},{64,448},{80,464},{96,480},{112... | collective-permute-start | bytes 196616 | tf_op jit(solution)/shard_map/handoff_z/ppermute | solution.py:55
  68.2 12.6 %collective-permute-start.5 = (bf16[256,128]{1,0:T(8,128)(2,1)S(1)}, bf16[256,128]{1,0:T(8,128)(2,1)S(1)}, u32[]{:S(2)}, u32[]{:S(2)}) collective-permute-start(bf16[256,128]{1,0:T(8,128)(2,1)S(1)} %get-tuple-element.44), channel_id=1, source_target_pairs={{0,448},{16,464},{32,480},{48,496},{64,384},{80,400},{96,416},{112... | collective-permute-start | bytes 196616 | tf_op jit(solution)/shard_map/handoff_z/ppermute | solution.py:55

commit v6 on v5

--- a/solution.py
+++ b/solution.py
@@ -180,7 +180,7 @@
 def take_kernel(pairing_ref, inst_ref, role_ref, own_ref, *refs):
     offers, out_ref = refs[:4], refs[5]
     inst = inst_ref[0]
-    handed = choose((source_of(pairing_ref, inst) ^ inst) // 4, offers)
+    handed = choose((source_of(pairing_ref, inst) ^ inst) // 4, offers[::-1])
     out_ref[...] = jnp.where(role_ref[0] == 1, handed, own_ref[...])
 
 
@@ -394,7 +394,7 @@
             role_inst(offers[j], [(i, 16 + (i ^ (4 * j))) for i in range(16)]) for j in range(4)
         ]
     attended, token = last(member, queried, state, own_kv, other_kv)
-    layer_kv = take(pairing, inst, role, own_kv, offered, token)
+    layer_kv = take(pairing, inst, role, own_kv, offered[::-1], token)
     return attended[None, None], layer_kv[None, None]
 
 

time: 82.6 us -> 81.4 us (0.985)
  the two profiles are of different devices: /device:TPU:1 before, /device:TPU:32 now
where the time goes in v6:
time: 81.4 us; the launch traced here: 80.9 us
  starting transfers between devices  32.5 us (40%)
  waiting for transfers between devices  23.3 us (29%)
  Pallas kernels  23 us (28%)
  between operations  1.42 us (2%)
    all_to_all x2, starting transfers between devices, exchange_tp(): lax.all_to_all(array, 'tp', 0, 0, axis_index_groups=groups, tiled=True)  18.5 us
    all_to_all x2, waiting for transfers between devices, exchange_tp(): lax.all_to_all(array, 'tp', 0, 0, axis_index_groups=groups, tiled=True)  13.8 us
    pallas_call x2, Pallas kernels, cache_part(): pl.pallas_call(functools.partial(cache_part_kernel, own, at), grid=(HEADS...  12.5 us
    ppermute x2, waiting for transfers between devices, swap_tp(): return lax.ppermute(array, 'tp', [(i, i ^ mask) for i in range(16)])  5.25 us
    ppermute x4, starting transfers between devices, role_inst(): return lax.ppermute(array, ('role', 'inst'), pairs)  5.17 us
    all_to_all x1, starting transfers between devices, per_device(): lax.all_to_all(sends, 'inst', 0, 0, axis_index_groups=Y_GROUPS, tiled=True)  4.46 us
    ppermute x2, starting transfers between devices, swap_tp(): return lax.ppermute(array, 'tp', [(i, i ^ mask) for i in range(16)])  4.37 us
    all_to_all x1, waiting for transfers between devices, per_device(): lax.all_to_all(sends, 'inst', 0, 0, axis_index_groups=Y_GROUPS, tiled=True)  4.21 us
  transfers between devices with their start and end apart: 9, of which 4 were waited for; matrix products, arithmetic and copies ran while one was open for 1% of the time, Pallas kernels for 22%

profile of v6, /device:TPU:32, one launch (start us, length us, event | category | flops | bytes accessed | tf_op | source)
XLA Modules:
  0.0 80.9 jit_solution(10654725311644612116)
XLA Ops:
  0.6 3.4 %project.1 = (bf16[4,4,256,128]{3,2,1,0:T(8,128)(2,1)}, f32[8,128]{1,0:T(8,128)S(1)}) custom-call(s32[1]{0:T(128)} %bitcast.member_ref, bf16[256,512]{1,0:T(8,128)(2,1)} %bitcast.15, bf16[512,2048]{1,0:T(8,128)(2,1)} %w_hbm.1), custom_call_target="tpu_custom_call" | custom-call | flops 536870912 | bytes 4194304 | tf_op jit(solution)/shard_map/project/pallas_call | solution.py:79
  4.0 4.3 %all-to-all-start = ((bf16[4,4,256,128]{3,2,1,0:T(8,128)(2,1)}), bf16[4,4,256,128]{3,2,1,0:T(8,128)(2,1)S(1)}, u32[]{:S(2)}, u32[]{:S(2)}) async-start(bf16[4,4,256,128]{3,2,1,0:T(8,128)(2,1)} %get-tuple-element.26), calls=%async_computation | async-start | bytes 2097152 | tf_op jit(solution)/shard_map/sum_x/all_to_all | solution.py:51
  9.0 8.8 %own_half.1 = (f32[256,1024]{1,0:T(8,128)}, f32[256,1024]{1,0:T(8,128)}, f32[256,1024]{1,0:T(8,128)}, f32[8,128]{1,0:T(8,128)S(1)}, bf16[2,2048,128]{2,1,0:T(8,128)(2,1)S(1)}) custom-call(s32[1]{0:T(128)} %bitcast.10.length_ref, s32[1]{0:T(128)} %bitcast.member_ref, bf16[256,1024]{1,0:T(8,128)(2,1)} %bitcast.12, bf16[2,2048,128]{2,1,0:T(8,128)(2,1)} %bitcast.17, ...), custom_call_target="tpu_custom_call" | custom-call | flops 4294967296 | bytes 2097152 | tf_op jit(solution)/shard_map/own_half/pallas_call | solution.py:282
  17.8 1.9 %collective-permute-start = (bf16[2,2048,128]{2,1,0:T(8,128)(2,1)S(1)}, bf16[2,2048,128]{2,1,0:T(8,128)(2,1)S(1)}, u32[]{:S(2)}, u32[]{:S(2)}) collective-permute-start(bf16[2,2048,128]{2,1,0:T(8,128)(2,1)S(1)} %get-tuple-element.25), channel_id=1, source_target_pairs={{0,1},{1,0},{2,3},{3,2},{4,5},{5,4},{6,7},{7,6},{8,9},{9,8},{10,11... | collective-permute-start | bytes 3145736 | tf_op jit(solution)/shard_map/prefix_first/ppermute | solution.py:47
  19.7 3.7 %all-to-all-done.parts_ref = bf16[4,4,256,128]{3,2,1,0:T(8,128)(2,1)S(1)} async-done(((bf16[4,4,256,128]{3,2,1,0:T(8,128)(2,1)}), bf16[4,4,256,128]{3,2,1,0:T(8,128)(2,1)S(1)}, u32[]{:S(2)}, u32[]{:S(2)}) %all-to-all-start) | async-done | bytes 1048608 | tf_op jit(solution)/shard_map/sum_x/all_to_all | solution.py:51
  23.4 0.8 %sum_x.1 = (f32[256,128]{1,0:T(8,128)S(1)}, bf16[4,256,128]{2,1,0:T(8,128)(2,1)}, f32[8,128]{1,0:T(8,128)S(1)}) custom-call(s32[1]{0:T(128)} %bitcast.member_ref, bf16[4,4,256,128]{3,2,1,0:T(8,128)(2,1)S(1)} %all-to-all-done.parts_ref, f32[8,128]{1,0:T(8,128)S(1)} %get-tuple-element.27.after_ref), custom_call_target="tpu_custom_call" | custom-call | tf_op jit(solution)/shard_map/sum_x/pallas_call | solution.py:110
  24.2 14.2 %all-to-all-start.1 = ((bf16[4,256,128]{2,1,0:T(8,128)(2,1)}), bf16[4,256,128]{2,1,0:T(8,128)(2,1)S(1)}, u32[]{:S(2)}, u32[]{:S(2)}) async-start(bf16[4,256,128]{2,1,0:T(8,128)(2,1)} %get-tuple-element.36), calls=%async_computation.1 | async-start | bytes 524288 | tf_op jit(solution)/shard_map/sum_z/all_to_all | solution.py:51
  38.4 0.5 fusion.2
  39.0 0.1 pad_maximum_fusion
  39.1 5.2 %collective-permute-done.kv_ref = bf16[2,2048,128]{2,1,0:T(8,128)(2,1)S(1)} collective-permute-done((bf16[2,2048,128]{2,1,0:T(8,128)(2,1)S(1)}, bf16[2,2048,128]{2,1,0:T(8,128)(2,1)S(1)}, u32[]{:S(2)}, u32[]{:S(2)}) %collective-permute-start) | collective-permute-done | bytes 1048608 | tf_op jit(solution)/shard_map/prefix_first/ppermute | solution.py:47
  44.4 0.0 copy-start
  44.4 3.7 %other_part.1 = (f32[256,1024]{1,0:T(8,128)}, f32[256,1024]{1,0:T(8,128)}, f32[256,1024]{1,0:T(8,128)}, f32[8,128]{1,0:T(8,128)S(1)}) custom-call(s32[1]{0:T(128)} %bitcast.11.length_ref, s32[1]{0:T(128)} %bitcast.member_ref, bf16[256,1024]{1,0:T(8,128)(2,1)} %bitcast.13, bf16[2,2048,128]{2,1,0:T(8,128)(2,1)S(1)} %collective-permute-done.kv_ref, ...), custom_call_target="tpu_custom_call" | custom-call | flops 4294967296 | bytes 2097152 | tf_op jit(solution)/shard_map/other_part/pallas_call | solution.py:282
  48.0 10.1 %all-to-all-done.1.parts_ref = bf16[4,256,128]{2,1,0:T(8,128)(2,1)S(1)} async-done(((bf16[4,256,128]{2,1,0:T(8,128)(2,1)}), bf16[4,256,128]{2,1,0:T(8,128)(2,1)S(1)}, u32[]{:S(2)}, u32[]{:S(2)}) %all-to-all-start.1) | async-done | bytes 262176 | tf_op jit(solution)/shard_map/sum_z/all_to_all | solution.py:51
  58.2 0.8 %finish.1 = (bf16[256,128]{1,0:T(8,128)(2,1)S(1)}, bf16[4,256,128]{2,1,0:T(8,128)(2,1)}) custom-call(s32[1]{0:T(128)} %bitcast.member_ref, f32[256,128]{1,0:T(8,128)S(1)} %get-tuple-element.35.keep_ref, bf16[4,256,128]{2,1,0:T(8,128)(2,1)S(1)} %all-to-all-done.1.parts_ref, f32[256,128]{1,0:T(8,128)S(1)} %get-tuple-element.49.cosine_ref, ...), custom_call_target="tpu_custom_call" | custom-call | tf_op jit(solution)/shard_map/finish/pallas_call | solution.py:137
  59.0 4.5 %all-to-all-start.2 = ((bf16[4,256,128]{2,1,0:T(8,128)(2,1)}), bf16[4,256,128]{2,1,0:T(8,128)(2,1)S(1)}, u32[]{:S(2)}, u32[]{:S(2)}) async-start(bf16[4,256,128]{2,1,0:T(8,128)(2,1)} %get-tuple-element.40), calls=%async_computation.2 | async-start | bytes 524288 | tf_op jit(solution)/shard_map/handoff_y/all_to_all | solution.py:386
  63.4 2.5 %collective-permute-start.1 = (bf16[256,128]{1,0:T(8,128)(2,1)S(1)}, bf16[256,128]{1,0:T(8,128)(2,1)S(1)}, u32[]{:S(2)}, u32[]{:S(2)}) collective-permute-start(bf16[256,128]{1,0:T(8,128)(2,1)S(1)} %get-tuple-element.38.refs_3_.own_ref), channel_id=1, source_target_pairs={{0,1},{1,0},{2,3},{3,2},{4,5},{5,4},{6,7},{7,6},{8,9},{9,8},{10,11... | collective-permute-start | bytes 196616 | tf_op jit(solution)/shard_map/pair/ppermute | solution.py:47
  65.9 4.2 %all-to-all-done.2.refs_0_ = bf16[4,256,128]{2,1,0:T(8,128)(2,1)S(1)} async-done(((bf16[4,256,128]{2,1,0:T(8,128)(2,1)}), bf16[4,256,128]{2,1,0:T(8,128)(2,1)S(1)}, u32[]{:S(2)}, u32[]{:S(2)}) %all-to-all-start.2) | async-done | bytes 262176 | tf_op jit(solution)/shard_map/handoff_y/all_to_all | solution.py:386
  70.1 0.0 copy-done
  70.1 0.6 offer.1
  70.7 1.3 %collective-permute-start.2 = (bf16[256,128]{1,0:T(8,128)(2,1)S(1)}, bf16[256,128]{1,0:T(8,128)(2,1)S(1)}, u32[]{:S(2)}, u32[]{:S(2)}) collective-permute-start(bf16[256,128]{1,0:T(8,128)(2,1)S(1)} %get-tuple-element.41), channel_id=1, source_target_pairs={{0,448},{16,464},{32,480},{48,496},{64,384},{80,400},{96,416},{112... | collective-permute-start | bytes 196616 | tf_op jit(solution)/shard_map/handoff_z/ppermute | solution.py:55
  72.0 1.3 %collective-permute-start.3 = (bf16[256,128]{1,0:T(8,128)(2,1)S(1)}, bf16[256,128]{1,0:T(8,128)(2,1)S(1)}, u32[]{:S(2)}, u32[]{:S(2)}) collective-permute-start(bf16[256,128]{1,0:T(8,128)(2,1)S(1)} %get-tuple-element.42), channel_id=1, source_target_pairs={{0,384},{16,400},{32,416},{48,432},{64,448},{80,464},{96,480},{112... | collective-permute-start | bytes 196616 | tf_op jit(solution)/shard_map/handoff_z/ppermute | solution.py:55
  73.3 1.3 %collective-permute-start.4 = (bf16[256,128]{1,0:T(8,128)(2,1)S(1)}, bf16[256,128]{1,0:T(8,128)(2,1)S(1)}, u32[]{:S(2)}, u32[]{:S(2)}) collective-permute-start(bf16[256,128]{1,0:T(8,128)(2,1)S(1)} %get-tuple-element.43), channel_id=1, source_target_pairs={{0,320},{16,336},{32,352},{48,368},{64,256},{80,272},{96,288},{112... | collective-permute-start | bytes 196616 | tf_op jit(solution)/shard_map/handoff_z/ppermute | solution.py:55
  74.6 1.3 %collective-permute-start.5 = (bf16[256,128]{1,0:T(8,128)(2,1)S(1)}, bf16[256,128]{1,0:T(8,128)(2,1)S(1)}, u32[]{:S(2)}, u32[]{:S(2)}) collective-permute-start(bf16[256,128]{1,0:T(8,128)(2,1)S(1)} %get-tuple-element.44), channel_id=1, source_target_pairs={{0,256},{16,272},{32,288},{48,304},{64,320},{80,336},{96,352},{112... | collective-permute-start | bytes 196616 | tf_op jit(solution)/shard_map/handoff_z/ppermute | solution.py:55
  75.9 0.0 collective-permute-done.1.refs_4_
  75.9 3.7 %last.1 = (bf16[256,1024]{1,0:T(8,128)(2,1)}, f32[8,128]{1,0:T(8,128)S(1)}) custom-call(s32[1]{0:T(128)} %bitcast.member_ref, bf16[256,1024]{1,0:T(8,128)(2,1)} %bitcast.14, f32[256,1024]{1,0:T(8,128)} %get-tuple-element.32.refs_0_, f32[256,1024]{1,0:T(8,128)} %get-tuple-element.33.refs_1_, f32[256,1024]{1,0:T(8,128)} %get-tuple-element.34.refs_2_, ...), custom_call_target="tpu_custom_call" | custom-call | flops 536870912 | bytes 3145728 | tf_op jit(solution)/shard_map/last/pallas_call | solution.py:333
  79.6 0.0 collective-permute-done.2.refs_0_
  79.6 0.0 collective-permute-done.3.refs_1_
  79.6 0.0 collective-permute-done.4.refs_2_
  79.6 0.0 collective-permute-done.5.refs_3_
  79.6 1.2 %take.1 = bf16[256,128]{1,0:T(8,128)(2,1)} custom-call(s32[16]{0:T(128)S(1)} %copy-done, s32[1]{0:T(128)} %bitcast.7.inst_ref, s32[1]{0:T(128)} %bitcast.8.role_ref, bf16[256,128]{1,0:T(8,128)(2,1)S(1)} %get-tuple-element.38.refs_3_.own_ref, bf16[256,128]{1,0:T(8,128)(2,1)S(1)} %collective-permute-done.2.refs_0_, ...), custom_call_target="tpu_custom_call" | custom-call | tf_op jit(solution)/shard_map/take/pallas_call | solution.py:188
  (2 shorter events, 0.0 us)
Async XLA Ops:
  4.0 19.4 %all-to-all-start = ((bf16[4,4,256,128]{3,2,1,0:T(8,128)(2,1)}), bf16[4,4,256,128]{3,2,1,0:T(8,128)(2,1)S(1)}, u32[]{:S(2)}, u32[]{:S(2)}) async-start(bf16[4,4,256,128]{3,2,1,0:T(8,128)(2,1)} %get-tuple-element.26), calls=%async_computation | async-start | bytes 2097152 | tf_op jit(solution)/shard_map/sum_x/all_to_all | solution.py:51
  17.8 26.6 %collective-permute-start = (bf16[2,2048,128]{2,1,0:T(8,128)(2,1)S(1)}, bf16[2,2048,128]{2,1,0:T(8,128)(2,1)S(1)}, u32[]{:S(2)}, u32[]{:S(2)}) collective-permute-start(bf16[2,2048,128]{2,1,0:T(8,128)(2,1)S(1)} %get-tuple-element.25), channel_id=1, source_target_pairs={{0,1},{1,0},{2,3},{3,2},{4,5},{5,4},{6,7},{7,6},{8,9},{9,8},{10,11... | collective-permute-start | bytes 3145736 | tf_op jit(solution)/shard_map/prefix_first/ppermute | solution.py:47
  24.2 33.9 %all-to-all-start.1 = ((bf16[4,256,128]{2,1,0:T(8,128)(2,1)}), bf16[4,256,128]{2,1,0:T(8,128)(2,1)S(1)}, u32[]{:S(2)}, u32[]{:S(2)}) async-start(bf16[4,256,128]{2,1,0:T(8,128)(2,1)} %get-tuple-element.36), calls=%async_computation.1 | async-start | bytes 524288 | tf_op jit(solution)/shard_map/sum_z/all_to_all | solution.py:51
  44.4 25.7 %copy-start = (s32[16]{0:T(128)S(1)}, s32[16]{0:T(128)}, u32[]{:S(2)}) copy-start(s32[16]{0:T(128)} %pairing_ref.3) | copy-start | bytes 196
  59.0 11.1 %all-to-all-start.2 = ((bf16[4,256,128]{2,1,0:T(8,128)(2,1)}), bf16[4,256,128]{2,1,0:T(8,128)(2,1)S(1)}, u32[]{:S(2)}, u32[]{:S(2)}) async-start(bf16[4,256,128]{2,1,0:T(8,128)(2,1)} %get-tuple-element.40), calls=%async_computation.2 | async-start | bytes 524288 | tf_op jit(solution)/shard_map/handoff_y/all_to_all | solution.py:386
  63.4 12.5 %collective-permute-start.1 = (bf16[256,128]{1,0:T(8,128)(2,1)S(1)}, bf16[256,128]{1,0:T(8,128)(2,1)S(1)}, u32[]{:S(2)}, u32[]{:S(2)}) collective-permute-start(bf16[256,128]{1,0:T(8,128)(2,1)S(1)} %get-tuple-element.38.refs_3_.own_ref), channel_id=1, source_target_pairs={{0,1},{1,0},{2,3},{3,2},{4,5},{5,4},{6,7},{7,6},{8,9},{9,8},{10,11... | collective-permute-start | bytes 196616 | tf_op jit(solution)/shard_map/pair/ppermute | solution.py:47
  70.7 8.9 %collective-permute-start.2 = (bf16[256,128]{1,0:T(8,128)(2,1)S(1)}, bf16[256,128]{1,0:T(8,128)(2,1)S(1)}, u32[]{:S(2)}, u32[]{:S(2)}) collective-permute-start(bf16[256,128]{1,0:T(8,128)(2,1)S(1)} %get-tuple-element.41), channel_id=1, source_target_pairs={{0,448},{16,464},{32,480},{48,496},{64,384},{80,400},{96,416},{112... | collective-permute-start | bytes 196616 | tf_op jit(solution)/shard_map/handoff_z/ppermute | solution.py:55
  72.0 7.6 %collective-permute-start.3 = (bf16[256,128]{1,0:T(8,128)(2,1)S(1)}, bf16[256,128]{1,0:T(8,128)(2,1)S(1)}, u32[]{:S(2)}, u32[]{:S(2)}) collective-permute-start(bf16[256,128]{1,0:T(8,128)(2,1)S(1)} %get-tuple-element.42), channel_id=1, source_target_pairs={{0,384},{16,400},{32,416},{48,432},{64,448},{80,464},{96,480},{112... | collective-permute-start | bytes 196616 | tf_op jit(solution)/shard_map/handoff_z/ppermute | solution.py:55
  73.3 6.3 %collective-permute-start.4 = (bf16[256,128]{1,0:T(8,128)(2,1)S(1)}, bf16[256,128]{1,0:T(8,128)(2,1)S(1)}, u32[]{:S(2)}, u32[]{:S(2)}) collective-permute-start(bf16[256,128]{1,0:T(8,128)(2,1)S(1)} %get-tuple-element.43), channel_id=1, source_target_pairs={{0,320},{16,336},{32,352},{48,368},{64,256},{80,272},{96,288},{112... | collective-permute-start | bytes 196616 | tf_op jit(solution)/shard_map/handoff_z/ppermute | solution.py:55
  74.6 5.0 %collective-permute-start.5 = (bf16[256,128]{1,0:T(8,128)(2,1)S(1)}, bf16[256,128]{1,0:T(8,128)(2,1)S(1)}, u32[]{:S(2)}, u32[]{:S(2)}) collective-permute-start(bf16[256,128]{1,0:T(8,128)(2,1)S(1)} %get-tuple-element.44), channel_id=1, source_target_pairs={{0,256},{16,272},{32,288},{48,304},{64,320},{80,336},{96,352},{112... | collective-permute-start | bytes 196616 | tf_op jit(solution)/shard_map/handoff_z/ppermute | solution.py:55

commit v7 on v6

--- a/solution.py
+++ b/solution.py
@@ -303,7 +303,10 @@
             transcendentals=TOK * HEADS * count,
         ),
         name="own_half" if own else "other_part",
-    )(length, member, in_hbm(queries), cache, after, *(in_hbm(part) for part in state))
+    )(
+        length, member, queries if own else in_hbm(queries), cache, after,
+        *(in_hbm(part) for part in state),
+    )
 
 
 def last_kernel(member_ref, q_ref, *refs):
@@ -373,7 +376,7 @@
     parts, token = project(member, hidden[0, 0], w_kv)
     with jax.named_scope("sum_x"):
         parts = exchange_tp(parts, X_GROUPS)
-    *state, token, chunk = cache_part(length, member, queried, in_hbm(resident), token, True, 0)
+    *state, token, chunk = cache_part(length, member, queried, resident, token, True, 0)
     with jax.named_scope("prefix_first"):
         across = swap_tp(chunk, 1)
     keep, parts, token = sum_x(member, parts, token)

time: 81.4 us -> 81.5 us (level)
  starting transfers between devices: 32.5 us -> 33.5 us
    all_to_all x1, starting transfers between devices: 4.46 us -> 5.56 us  [per_device(): lax.all_to_all(sends, 'inst', 0, 0, axis_index_groups=Y_GROUPS, tiled=True)]
    pallas_call x2, Pallas kernels: 12.5 us -> 11.7 us  [cache_part(): pl.pallas_call(functools.partial(cache_part_kernel, own, at), grid=(HEADS...]
  transfers between devices with their start and end apart: 9 -> 9, of which waited for: 4 -> 4; matrix products, arithmetic and copies ran while one was open for 1% -> 1% of each run, Pallas kernels for 22% -> 21%
where the time goes in v7:
time: 81.5 us; the launch traced here: 81.2 us
  starting transfers between devices  33.5 us (41%)
  waiting for transfers between devices  23.2 us (28%)
  Pallas kernels  22.3 us (27%)
  between operations  1.45 us (2%)
    all_to_all x2, starting transfers between devices, exchange_tp(): lax.all_to_all(array, 'tp', 0, 0, axis_index_groups=groups, tiled=True)  18.5 us
    all_to_all x2, waiting for transfers between devices, exchange_tp(): lax.all_to_all(array, 'tp', 0, 0, axis_index_groups=groups, tiled=True)  14.3 us
    pallas_call x2, Pallas kernels, cache_part(): pl.pallas_call(functools.partial(cache_part_kernel, own, at), grid=(HEADS...  11.7 us
    all_to_all x1, starting transfers between devices, per_device(): lax.all_to_all(sends, 'inst', 0, 0, axis_index_groups=Y_GROUPS, tiled=True)  5.56 us
    ppermute x4, starting transfers between devices, role_inst(): return lax.ppermute(array, ('role', 'inst'), pairs)  5.17 us
    ppermute x2, waiting for transfers between devices, swap_tp(): return lax.ppermute(array, 'tp', [(i, i ^ mask) for i in range(16)])  4.59 us
    all_to_all x1, waiting for transfers between devices, per_device(): lax.all_to_all(sends, 'inst', 0, 0, axis_index_groups=Y_GROUPS, tiled=True)  4.29 us
    ppermute x2, starting transfers between devices, swap_tp(): return lax.ppermute(array, 'tp', [(i, i ^ mask) for i in range(16)])  4.29 us
  transfers between devices with their start and end apart: 9, of which 4 were waited for; matrix products, arithmetic and copies ran while one was open for 1% of the time, Pallas kernels for 21%

profile of v7, /device:TPU:32, one launch (start us, length us, event | category | flops | bytes accessed | tf_op | source)
XLA Modules:
  0.0 81.2 jit_solution(17605582975147403468)
XLA Ops:
  0.6 0.0 copy-start
  0.6 0.0 copy-start.2
  0.7 3.5 %project.1 = (bf16[4,4,256,128]{3,2,1,0:T(8,128)(2,1)}, f32[8,128]{1,0:T(8,128)S(1)}) custom-call(s32[1]{0:T(128)} %bitcast.member_ref, bf16[256,512]{1,0:T(8,128)(2,1)} %bitcast.16, bf16[512,2048]{1,0:T(8,128)(2,1)} %w_hbm.1), custom_call_target="tpu_custom_call" | custom-call | flops 536870912 | bytes 4194304 | tf_op jit(solution)/shard_map/project/pallas_call | solution.py:79
  4.1 4.3 %all-to-all-start = ((bf16[4,4,256,128]{3,2,1,0:T(8,128)(2,1)}), bf16[4,4,256,128]{3,2,1,0:T(8,128)(2,1)S(1)}, u32[]{:S(2)}, u32[]{:S(2)}) async-start(bf16[4,4,256,128]{3,2,1,0:T(8,128)(2,1)} %get-tuple-element.26), calls=%async_computation | async-start | bytes 2097152 | tf_op jit(solution)/shard_map/sum_x/all_to_all | solution.py:51
  9.1 0.0 copy-done
  9.1 0.0 copy-done.2
  9.1 7.9 %own_half.1 = (f32[256,1024]{1,0:T(8,128)}, f32[256,1024]{1,0:T(8,128)}, f32[256,1024]{1,0:T(8,128)}, f32[8,128]{1,0:T(8,128)S(1)}, bf16[2,2048,128]{2,1,0:T(8,128)(2,1)}) custom-call(s32[1]{0:T(128)} %bitcast.10.length_ref, s32[1]{0:T(128)} %bitcast.member_ref, bf16[256,1024]{1,0:T(8,128)(2,1)S(1)} %bitcast.14, bf16[2,2048,128]{2,1,0:T(8,128)(2,1)S(1)} %bitcast.15, ...), custom_call_target="tpu_custom_call" | custom-call | flops 4294967296 | bytes 2097152 | tf_op jit(solution)/shard_map/own_half/pallas_call | solution.py:282
  17.0 1.9 %collective-permute-start = (bf16[2,2048,128]{2,1,0:T(8,128)(2,1)}, bf16[2,2048,128]{2,1,0:T(8,128)(2,1)S(1)}, u32[]{:S(2)}, u32[]{:S(2)}) collective-permute-start(bf16[2,2048,128]{2,1,0:T(8,128)(2,1)} %get-tuple-element.25), channel_id=1, source_target_pairs={{0,1},{1,0},{2,3},{3,2},{4,5},{5,4},{6,7},{7,6},{8,9},{9,8},{10,11... | collective-permute-start | bytes 3145736 | tf_op jit(solution)/shard_map/prefix_first/ppermute | solution.py:47
  19.0 5.2 %all-to-all-done.parts_ref = bf16[4,4,256,128]{3,2,1,0:T(8,128)(2,1)S(1)} async-done(((bf16[4,4,256,128]{3,2,1,0:T(8,128)(2,1)}), bf16[4,4,256,128]{3,2,1,0:T(8,128)(2,1)S(1)}, u32[]{:S(2)}, u32[]{:S(2)}) %all-to-all-start) | async-done | bytes 1048608 | tf_op jit(solution)/shard_map/sum_x/all_to_all | solution.py:51
  24.2 0.8 %sum_x.1 = (f32[256,128]{1,0:T(8,128)S(1)}, bf16[4,256,128]{2,1,0:T(8,128)(2,1)}, f32[8,128]{1,0:T(8,128)S(1)}) custom-call(s32[1]{0:T(128)} %bitcast.member_ref, bf16[4,4,256,128]{3,2,1,0:T(8,128)(2,1)S(1)} %all-to-all-done.parts_ref, f32[8,128]{1,0:T(8,128)S(1)} %get-tuple-element.27.after_ref), custom_call_target="tpu_custom_call" | custom-call | tf_op jit(solution)/shard_map/sum_x/pallas_call | solution.py:110
  25.0 14.2 %all-to-all-start.1 = ((bf16[4,256,128]{2,1,0:T(8,128)(2,1)}), bf16[4,256,128]{2,1,0:T(8,128)(2,1)S(1)}, u32[]{:S(2)}, u32[]{:S(2)}) async-start(bf16[4,256,128]{2,1,0:T(8,128)(2,1)} %get-tuple-element.36), calls=%async_computation.1 | async-start | bytes 524288 | tf_op jit(solution)/shard_map/sum_z/all_to_all | solution.py:51
  39.2 0.5 fusion.2
  39.8 0.1 pad_maximum_fusion
  39.9 4.6 %collective-permute-done.kv_ref = bf16[2,2048,128]{2,1,0:T(8,128)(2,1)S(1)} collective-permute-done((bf16[2,2048,128]{2,1,0:T(8,128)(2,1)}, bf16[2,2048,128]{2,1,0:T(8,128)(2,1)S(1)}, u32[]{:S(2)}, u32[]{:S(2)}) %collective-permute-start) | collective-permute-done | bytes 1048608 | tf_op jit(solution)/shard_map/prefix_first/ppermute | solution.py:47
  44.5 3.7 %other_part.1 = (f32[256,1024]{1,0:T(8,128)}, f32[256,1024]{1,0:T(8,128)}, f32[256,1024]{1,0:T(8,128)}, f32[8,128]{1,0:T(8,128)S(1)}) custom-call(s32[1]{0:T(128)} %bitcast.11.length_ref, s32[1]{0:T(128)} %bitcast.member_ref, bf16[256,1024]{1,0:T(8,128)(2,1)} %bitcast.12, bf16[2,2048,128]{2,1,0:T(8,128)(2,1)S(1)} %collective-permute-done.kv_ref, ...), custom_call_target="tpu_custom_call" | custom-call | flops 4294967296 | bytes 2097152 | tf_op jit(solution)/shard_map/other_part/pallas_call | solution.py:282
  48.2 9.1 %all-to-all-done.1.parts_ref = bf16[4,256,128]{2,1,0:T(8,128)(2,1)S(1)} async-done(((bf16[4,256,128]{2,1,0:T(8,128)(2,1)}), bf16[4,256,128]{2,1,0:T(8,128)(2,1)S(1)}, u32[]{:S(2)}, u32[]{:S(2)}) %all-to-all-start.1) | async-done | bytes 262176 | tf_op jit(solution)/shard_map/sum_z/all_to_all | solution.py:51
  57.3 0.8 %finish.1 = (bf16[256,128]{1,0:T(8,128)(2,1)S(1)}, bf16[4,256,128]{2,1,0:T(8,128)(2,1)}) custom-call(s32[1]{0:T(128)} %bitcast.member_ref, f32[256,128]{1,0:T(8,128)S(1)} %get-tuple-element.35.keep_ref, bf16[4,256,128]{2,1,0:T(8,128)(2,1)S(1)} %all-to-all-done.1.parts_ref, f32[256,128]{1,0:T(8,128)S(1)} %get-tuple-element.49.cosine_ref, ...), custom_call_target="tpu_custom_call" | custom-call | tf_op jit(solution)/shard_map/finish/pallas_call | solution.py:137
  58.2 5.6 %all-to-all-start.2 = ((bf16[4,256,128]{2,1,0:T(8,128)(2,1)}), bf16[4,256,128]{2,1,0:T(8,128)(2,1)S(1)}, u32[]{:S(2)}, u32[]{:S(2)}) async-start(bf16[4,256,128]{2,1,0:T(8,128)(2,1)} %get-tuple-element.40), calls=%async_computation.2 | async-start | bytes 524288 | tf_op jit(solution)/shard_map/handoff_y/all_to_all | solution.py:389
  63.7 2.4 %collective-permute-start.1 = (bf16[256,128]{1,0:T(8,128)(2,1)S(1)}, bf16[256,128]{1,0:T(8,128)(2,1)S(1)}, u32[]{:S(2)}, u32[]{:S(2)}) collective-permute-start(bf16[256,128]{1,0:T(8,128)(2,1)S(1)} %get-tuple-element.38.refs_3_.own_ref), channel_id=1, source_target_pairs={{0,1},{1,0},{2,3},{3,2},{4,5},{5,4},{6,7},{7,6},{8,9},{9,8},{10,11... | collective-permute-start | bytes 196616 | tf_op jit(solution)/shard_map/pair/ppermute | solution.py:47
  66.1 4.3 %all-to-all-done.2.refs_0_ = bf16[4,256,128]{2,1,0:T(8,128)(2,1)S(1)} async-done(((bf16[4,256,128]{2,1,0:T(8,128)(2,1)}), bf16[4,256,128]{2,1,0:T(8,128)(2,1)S(1)}, u32[]{:S(2)}, u32[]{:S(2)}) %all-to-all-start.2) | async-done | bytes 262176 | tf_op jit(solution)/shard_map/handoff_y/all_to_all | solution.py:389
  70.4 0.6 offer.1
  71.0 1.3 %collective-permute-start.2 = (bf16[256,128]{1,0:T(8,128)(2,1)S(1)}, bf16[256,128]{1,0:T(8,128)(2,1)S(1)}, u32[]{:S(2)}, u32[]{:S(2)}) collective-permute-start(bf16[256,128]{1,0:T(8,128)(2,1)S(1)} %get-tuple-element.41), channel_id=1, source_target_pairs={{0,448},{16,464},{32,480},{48,496},{64,384},{80,400},{96,416},{112... | collective-permute-start | bytes 196616 | tf_op jit(solution)/shard_map/handoff_z/ppermute | solution.py:55
  72.3 1.3 %collective-permute-start.3 = (bf16[256,128]{1,0:T(8,128)(2,1)S(1)}, bf16[256,128]{1,0:T(8,128)(2,1)S(1)}, u32[]{:S(2)}, u32[]{:S(2)}) collective-permute-start(bf16[256,128]{1,0:T(8,128)(2,1)S(1)} %get-tuple-element.42), channel_id=1, source_target_pairs={{0,384},{16,400},{32,416},{48,432},{64,448},{80,464},{96,480},{112... | collective-permute-start | bytes 196616 | tf_op jit(solution)/shard_map/handoff_z/ppermute | solution.py:55
  73.6 1.3 %collective-permute-start.4 = (bf16[256,128]{1,0:T(8,128)(2,1)S(1)}, bf16[256,128]{1,0:T(8,128)(2,1)S(1)}, u32[]{:S(2)}, u32[]{:S(2)}) collective-permute-start(bf16[256,128]{1,0:T(8,128)(2,1)S(1)} %get-tuple-element.43), channel_id=1, source_target_pairs={{0,320},{16,336},{32,352},{48,368},{64,256},{80,272},{96,288},{112... | collective-permute-start | bytes 196616 | tf_op jit(solution)/shard_map/handoff_z/ppermute | solution.py:55
  74.9 1.3 %collective-permute-start.5 = (bf16[256,128]{1,0:T(8,128)(2,1)S(1)}, bf16[256,128]{1,0:T(8,128)(2,1)S(1)}, u32[]{:S(2)}, u32[]{:S(2)}) collective-permute-start(bf16[256,128]{1,0:T(8,128)(2,1)S(1)} %get-tuple-element.44), channel_id=1, source_target_pairs={{0,256},{16,272},{32,288},{48,304},{64,320},{80,336},{96,352},{112... | collective-permute-start | bytes 196616 | tf_op jit(solution)/shard_map/handoff_z/ppermute | solution.py:55
  76.2 0.0 collective-permute-done.1.refs_4_
  76.2 3.7 %last.1 = (bf16[256,1024]{1,0:T(8,128)(2,1)}, f32[8,128]{1,0:T(8,128)S(1)}) custom-call(s32[1]{0:T(128)} %bitcast.member_ref, bf16[256,1024]{1,0:T(8,128)(2,1)} %bitcast.13, f32[256,1024]{1,0:T(8,128)} %get-tuple-element.32.refs_0_, f32[256,1024]{1,0:T(8,128)} %get-tuple-element.33.refs_1_, f32[256,1024]{1,0:T(8,128)} %get-tuple-element.34.refs_2_, ...), custom_call_target="tpu_custom_call" | custom-call | flops 536870912 | bytes 3145728 | tf_op jit(solution)/shard_map/last/pallas_call | solution.py:336
  79.9 0.0 collective-permute-done.2.refs_0_
  79.9 0.0 collective-permute-done.3.refs_1_
  79.9 0.0 collective-permute-done.4.refs_2_
  79.9 0.0 collective-permute-done.5.refs_3_
  79.9 1.2 %take.1 = bf16[256,128]{1,0:T(8,128)(2,1)} custom-call(s32[16]{0:T(128)S(1)} %copy-done.1, s32[1]{0:T(128)} %bitcast.7.inst_ref, s32[1]{0:T(128)} %bitcast.8.role_ref, bf16[256,128]{1,0:T(8,128)(2,1)S(1)} %get-tuple-element.38.refs_3_.own_ref, bf16[256,128]{1,0:T(8,128)(2,1)S(1)} %collective-permute-done.2.refs_0_, ...), custom_call_target="tpu_custom_call" | custom-call | tf_op jit(solution)/shard_map/take/pallas_call | solution.py:188
  (4 shorter events, 0.0 us)
Async XLA Ops:
  0.6 8.4 %copy-start = (bf16[1,1,256,1024]{3,2,1,0:T(8,128)(2,1)S(1)}, bf16[1,1,256,1024]{3,2,1,0:T(8,128)(2,1)}, u32[]{:S(2)}) copy-start(bf16[1,1,256,1024]{3,2,1,0:T(8,128)(2,1)} %param.7) | copy-start | bytes 1572868
  0.6 8.4 %copy-start.2 = (bf16[1,1,1,2,2048,128]{5,4,3,2,1,0:T(8,128)(2,1)S(1)}, bf16[1,1,1,2,2048,128]{5,4,3,2,1,0:T(8,128)(2,1)}, u32[]{:S(2)}) copy-start(bf16[1,1,1,2,2048,128]{5,4,3,2,1,0:T(8,128)(2,1)} %param.8) | copy-start | bytes 3145732
  4.1 20.1 %all-to-all-start = ((bf16[4,4,256,128]{3,2,1,0:T(8,128)(2,1)}), bf16[4,4,256,128]{3,2,1,0:T(8,128)(2,1)S(1)}, u32[]{:S(2)}, u32[]{:S(2)}) async-start(bf16[4,4,256,128]{3,2,1,0:T(8,128)(2,1)} %get-tuple-element.26), calls=%async_computation | async-start | bytes 2097152 | tf_op jit(solution)/shard_map/sum_x/all_to_all | solution.py:51
  17.0 27.5 %collective-permute-start = (bf16[2,2048,128]{2,1,0:T(8,128)(2,1)}, bf16[2,2048,128]{2,1,0:T(8,128)(2,1)S(1)}, u32[]{:S(2)}, u32[]{:S(2)}) collective-permute-start(bf16[2,2048,128]{2,1,0:T(8,128)(2,1)} %get-tuple-element.25), channel_id=1, source_target_pairs={{0,1},{1,0},{2,3},{3,2},{4,5},{5,4},{6,7},{7,6},{8,9},{9,8},{10,11... | collective-permute-start | bytes 3145736 | tf_op jit(solution)/shard_map/prefix_first/ppermute | solution.py:47
  25.0 32.3 %all-to-all-start.1 = ((bf16[4,256,128]{2,1,0:T(8,128)(2,1)}), bf16[4,256,128]{2,1,0:T(8,128)(2,1)S(1)}, u32[]{:S(2)}, u32[]{:S(2)}) async-start(bf16[4,256,128]{2,1,0:T(8,128)(2,1)} %get-tuple-element.36), calls=%async_computation.1 | async-start | bytes 524288 | tf_op jit(solution)/shard_map/sum_z/all_to_all | solution.py:51
  44.5 25.9 %copy-start.1 = (s32[16]{0:T(128)S(1)}, s32[16]{0:T(128)}, u32[]{:S(2)}) copy-start(s32[16]{0:T(128)} %pairing_ref.3) | copy-start | bytes 196
  58.2 12.2 %all-to-all-start.2 = ((bf16[4,256,128]{2,1,0:T(8,128)(2,1)}), bf16[4,256,128]{2,1,0:T(8,128)(2,1)S(1)}, u32[]{:S(2)}, u32[]{:S(2)}) async-start(bf16[4,256,128]{2,1,0:T(8,128)(2,1)} %get-tuple-element.40), calls=%async_computation.2 | async-start | bytes 524288 | tf_op jit(solution)/shard_map/handoff_y/all_to_all | solution.py:389
  63.7 12.5 %collective-permute-start.1 = (bf16[256,128]{1,0:T(8,128)(2,1)S(1)}, bf16[256,128]{1,0:T(8,128)(2,1)S(1)}, u32[]{:S(2)}, u32[]{:S(2)}) collective-permute-start(bf16[256,128]{1,0:T(8,128)(2,1)S(1)} %get-tuple-element.38.refs_3_.own_ref), channel_id=1, source_target_pairs={{0,1},{1,0},{2,3},{3,2},{4,5},{5,4},{6,7},{7,6},{8,9},{9,8},{10,11... | collective-permute-start | bytes 196616 | tf_op jit(solution)/shard_map/pair/ppermute | solution.py:47
  71.0 8.9 %collective-permute-start.2 = (bf16[256,128]{1,0:T(8,128)(2,1)S(1)}, bf16[256,128]{1,0:T(8,128)(2,1)S(1)}, u32[]{:S(2)}, u32[]{:S(2)}) collective-permute-start(bf16[256,128]{1,0:T(8,128)(2,1)S(1)} %get-tuple-element.41), channel_id=1, source_target_pairs={{0,448},{16,464},{32,480},{48,496},{64,384},{80,400},{96,416},{112... | collective-permute-start | bytes 196616 | tf_op jit(solution)/shard_map/handoff_z/ppermute | solution.py:55
  72.3 7.6 %collective-permute-start.3 = (bf16[256,128]{1,0:T(8,128)(2,1)S(1)}, bf16[256,128]{1,0:T(8,128)(2,1)S(1)}, u32[]{:S(2)}, u32[]{:S(2)}) collective-permute-start(bf16[256,128]{1,0:T(8,128)(2,1)S(1)} %get-tuple-element.42), channel_id=1, source_target_pairs={{0,384},{16,400},{32,416},{48,432},{64,448},{80,464},{96,480},{112... | collective-permute-start | bytes 196616 | tf_op jit(solution)/shard_map/handoff_z/ppermute | solution.py:55
  73.6 6.3 %collective-permute-start.4 = (bf16[256,128]{1,0:T(8,128)(2,1)S(1)}, bf16[256,128]{1,0:T(8,128)(2,1)S(1)}, u32[]{:S(2)}, u32[]{:S(2)}) collective-permute-start(bf16[256,128]{1,0:T(8,128)(2,1)S(1)} %get-tuple-element.43), channel_id=1, source_target_pairs={{0,320},{16,336},{32,352},{48,368},{64,256},{80,272},{96,288},{112... | collective-permute-start | bytes 196616 | tf_op jit(solution)/shard_map/handoff_z/ppermute | solution.py:55
  74.9 5.0 %collective-permute-start.5 = (bf16[256,128]{1,0:T(8,128)(2,1)S(1)}, bf16[256,128]{1,0:T(8,128)(2,1)S(1)}, u32[]{:S(2)}, u32[]{:S(2)}) collective-permute-start(bf16[256,128]{1,0:T(8,128)(2,1)S(1)} %get-tuple-element.44), channel_id=1, source_target_pairs={{0,256},{16,272},{32,288},{48,304},{64,320},{80,336},{96,352},{112... | collective-permute-start | bytes 196616 | tf_op jit(solution)/shard_map/handoff_z/ppermute | solution.py:55
